TPU v7x, 32 devices: a whole 2x2x4 slice. The times are simulated.
32 devices in a mesh: gz: 4 (over y, core), gy: 8 (over z, x).
Axes of the slice: x: 2, y: 2, z: 4, core: 2. Of those that a mesh axis runs over, the one named last changes fastest.
Arguments:
- density: float32 [32, 64, 512], P(None, 'gy', 'gz'), may hold values from 0.5 to 2
- diffusion: float32 [3], replicated, may hold values from 800 to 3000
- centers: float32 [16, 3], replicated, may hold values from -1 to 1
- sharpness: float32 [16], replicated, may hold values from 1 to 8
- affine: float32 [16, 3, 3], replicated, may hold values from -6 to 6
- offsets: float32 [16, 3], replicated, may hold values from -6 to 6
Outputs:
- density_next: float32 [32, 64, 512], P(None, 'gy', 'gz')
All inputs are finite; a program needn't handle non-finite values.
Results may differ from a plain program's by a relative error of at most 0.00065.
Values sent between devices are 32-bit elements; how exact they have to be, the bound alone decides.
No kernel may reach another device: no remote copies, remote signals or barrier semaphores. Data moves between devices by JAX's collectives and lax.ppermute only.
A program may use at most 64 MiB of HBM per device.

v0:
```python
import jax
import jax.numpy as jnp
from jax import lax
from jax.sharding import PartitionSpec as P

DRIFT_LIMIT = 1200.0


def padded(array, sides, width):
    for axis, dim in sides:
        devices, length = (lax.axis_size(axis), array.shape[dim])
        up = [(i, (i + 1) % devices) for i in range(devices - 1)]
        down = [(j, i) for i, j in up]
        last = lax.slice_in_dim(array, length - width, length, axis=dim)
        leading = lax.slice_in_dim(array, 0, width, axis=dim)
        before = lax.ppermute(last, axis, up)
        after = lax.ppermute(leading, axis, down)
        array = jnp.concatenate([before, array, after], axis=dim)
    return array


def from_behind(block, axis, distance):
    devices = range(lax.axis_size(axis))
    route = [(i - distance, i) for i in devices if i - distance in devices]
    return lax.ppermute(block, axis, route)


def axis_coord(positions, line_total):
    return (2.0 * positions.astype(jnp.float32) + 1.0) / line_total - 1.0


def bump_factor(coords, centers, sharpness, column):
    return jnp.exp(-sharpness[:, None] * (coords[None, :] - centers[:, column : column + 1]) ** 2)


def field_drift(component, x_index, y_index, z_index, mixture, totals):
    centers, sharpness, affine, offsets = mixture
    x_coord = axis_coord(x_index, totals[0])
    y_coord = axis_coord(y_index, totals[1])
    z_coord = axis_coord(z_index, totals[2])
    x_factor = bump_factor(x_coord, centers, sharpness, 0)
    y_factor = bump_factor(y_coord, centers, sharpness, 1)
    z_factor = bump_factor(z_coord, centers, sharpness, 2)
    matrix = affine[:, component, :]
    shift_term = offsets[:, component]
    left_part = jnp.concatenate(
        [
            x_factor * (matrix[:, 0:1] * x_coord[None, :] + shift_term[:, None]),
            x_factor * matrix[:, 1:2],
            x_factor * matrix[:, 2:3],
        ],
        axis=0,
    )
    yz_plane = y_factor[:, :, None] * z_factor[:, None, :]
    right_part = jnp.concatenate(
        [yz_plane, yz_plane * y_coord[None, :, None], yz_plane * z_coord[None, None, :]], axis=0
    )
    right_part = right_part.reshape(right_part.shape[0], -1)
    raw_drift = jnp.dot(
        left_part.T, right_part, precision=lax.Precision.HIGHEST, preferred_element_type=jnp.float32
    )
    return DRIFT_LIMIT * jnp.tanh(
        raw_drift.reshape(x_coord.shape[0], y_coord.shape[0], z_coord.shape[0])
    )


def transport(framed_part, drift_part, diffuse, line_axis):
    length = framed_part.shape[line_axis] - 2
    centre = lax.slice_in_dim(framed_part, 1, length + 1, axis=line_axis)
    onward = lax.slice_in_dim(framed_part, 2, length + 2, axis=line_axis)
    backward = lax.slice_in_dim(framed_part, 0, length, axis=line_axis)
    drift_on = lax.slice_in_dim(drift_part, 2, length + 2, axis=line_axis)
    drift_back = lax.slice_in_dim(drift_part, 0, length, axis=line_axis)
    return diffuse * (onward - 2.0 * centre + backward) - 0.5 * (
        drift_on * onward - drift_back * backward
    )


def implicit_rows(drift_part, diffuse, line_axis, at_start, at_end):
    length = drift_part.shape[line_axis] - 2
    drift_on = lax.slice_in_dim(drift_part, 2, length + 2, axis=line_axis)
    drift_back = lax.slice_in_dim(drift_part, 0, length, axis=line_axis)
    pivots = 1.0 + 2.0 * diffuse
    sub_diag = jnp.where(at_start, 0.0, (-diffuse - 0.5 * drift_back) / pivots)
    super_diag = jnp.where(at_end, 0.0, (-diffuse + 0.5 * drift_on) / pivots)
    return (sub_diag, super_diag)


def edge_masks(positions, line_total, line_axis):
    layout = [1, 1, 1]
    layout[line_axis] = positions.shape[0]
    return ((positions == 0).reshape(layout), (positions == line_total - 1).reshape(layout))


def shifted(values, stride, line_axis, onward):
    line_dim = line_axis % values.ndim
    length = values.shape[line_dim]
    layout = list(values.shape)
    layout[line_dim] = stride
    padding = jnp.zeros(layout, values.dtype)
    if onward:
        return jnp.concatenate(
            [lax.slice_in_dim(values, stride, length, axis=line_dim), padding], axis=line_dim
        )
    return jnp.concatenate(
        [padding, lax.slice_in_dim(values, 0, length - stride, axis=line_dim)], axis=line_dim
    )


def eliminate(row_set, below_set, above_set):
    sub_diag, super_diag, source = row_set
    pivots = 1.0 - sub_diag * below_set[1] - super_diag * above_set[0]
    return (
        -sub_diag * below_set[0] / pivots,
        -super_diag * above_set[1] / pivots,
        (source - sub_diag * below_set[2] - super_diag * above_set[2]) / pivots,
    )


def reduce_lines(sub_diag, super_diag, source, line_axis):
    length = sub_diag.shape[line_axis]
    row_set = (sub_diag, super_diag, source)
    stride = 1
    while stride < length:
        below_set = tuple((shifted(member, stride, line_axis, False) for member in row_set))
        above_set = tuple((shifted(member, stride, line_axis, True) for member in row_set))
        row_set = eliminate(row_set, below_set, above_set)
        stride = stride * 2
    return row_set[2]


def pair_doubling(packed, from_below, from_above, extent):
    lower_pair = from_below(packed, 1)
    upper_pair = from_above(packed, 1)
    below_set = jnp.stack([lower_pair[:, 1], packed[:, 0]], axis=1)
    above_set = jnp.stack([packed[:, 1], upper_pair[:, 0]], axis=1)
    packed = jnp.stack(eliminate(tuple(packed), tuple(below_set), tuple(above_set)))
    stride = 1
    while stride < extent:
        packed = jnp.stack(
            eliminate(
                tuple(packed), tuple(from_below(packed, stride)), tuple(from_above(packed, stride))
            )
        )
        stride = stride * 2
    return packed[2]


def spike_lines(sub_diag, super_diag, source, line_axis, reducer):
    line_dim = line_axis % sub_diag.ndim
    length = sub_diag.shape[line_dim]
    layout = [1] * sub_diag.ndim
    layout[line_dim] = length
    positions = jnp.arange(length, dtype=jnp.int32).reshape(layout)
    interior = (positions > 0) & (positions < length - 1)
    block_sub = jnp.where(interior, sub_diag, 0.0)
    block_super = jnp.where(interior, super_diag, 0.0)
    sources = jnp.stack(
        [
            jnp.where(interior, source, 0.0),
            jnp.broadcast_to((positions == 0).astype(jnp.float32), source.shape),
            jnp.broadcast_to((positions == length - 1).astype(jnp.float32), source.shape),
        ]
    )
    solutions = reduce_lines(block_sub, block_super, sources, line_axis)
    particular, left_spike, right_spike = (solutions[0], solutions[1], solutions[2])

    def take_row(values, offset):
        return lax.index_in_dim(values, offset, line_dim, keepdims=False)

    start_pivot = 1.0 + take_row(super_diag, 0) * take_row(left_spike, 1)
    start_row = (
        take_row(sub_diag, 0) / start_pivot,
        take_row(super_diag, 0) * take_row(right_spike, 1) / start_pivot,
        (take_row(source, 0) - take_row(super_diag, 0) * take_row(particular, 1)) / start_pivot,
    )
    end_pivot = 1.0 + take_row(sub_diag, length - 1) * take_row(right_spike, length - 2)
    end_row = (
        take_row(sub_diag, length - 1) * take_row(left_spike, length - 2) / end_pivot,
        take_row(super_diag, length - 1) / end_pivot,
        (
            take_row(source, length - 1)
            - take_row(sub_diag, length - 1) * take_row(particular, length - 2)
        )
        / end_pivot,
    )
    packed = jnp.stack([jnp.stack([start_row[member], end_row[member]]) for member in range(3)])
    edge_values = reducer(packed)
    return (
        particular
        + left_spike * jnp.expand_dims(edge_values[0], line_dim)
        + right_spike * jnp.expand_dims(edge_values[1], line_dim)
    )


def body(density, diffusion, centers, sharpness, affine, offsets):
    size_x, size_y, size_z = density.shape
    extent_y = lax.axis_size("gy")
    extent_z = lax.axis_size("gz")
    total_y = size_y * extent_y
    total_z = size_z * extent_z
    totals = (size_x, total_y, total_z)
    place_y = lax.axis_index("gy")
    place_z = lax.axis_index("gz")
    mixture = (centers, sharpness, affine, offsets)
    x_index = jnp.arange(size_x, dtype=jnp.int32)
    y_index = place_y * size_y + jnp.arange(size_y, dtype=jnp.int32)
    z_index = place_z * size_z + jnp.arange(size_z, dtype=jnp.int32)
    framed = padded(density, (("gy", 1), ("gz", 2)), 1)
    drift_x = field_drift(
        0, jnp.arange(-1, size_x + 1, dtype=jnp.int32), y_index, z_index, mixture, totals
    )
    drift_y = field_drift(
        1,
        x_index,
        place_y * size_y + jnp.arange(-1, size_y + 1, dtype=jnp.int32),
        z_index,
        mixture,
        totals,
    )
    drift_z = field_drift(
        2,
        x_index,
        y_index,
        place_z * size_z + jnp.arange(-1, size_z + 1, dtype=jnp.int32),
        mixture,
        totals,
    )
    flux_y = transport(framed[:, :, 1:-1], drift_y, diffusion[1], 1)
    flux_z = transport(framed[:, 1:-1, :], drift_z, diffusion[2], 2)
    start_x, end_x = edge_masks(x_index, size_x, 0)
    sub_x, super_x = implicit_rows(drift_x, diffusion[0], 0, start_x, end_x)
    first_section = reduce_lines(
        sub_x, super_x, (density + flux_y + flux_z) / (1.0 + 2.0 * diffusion[0]), -3
    )
    second_source = (first_section - flux_y) / (1.0 + 2.0 * diffusion[1])

    def below_y(packed, stride):
        return from_behind(packed, "gy", stride)

    def above_y(packed, stride):
        return from_behind(packed, "gy", -stride)

    def reducer_y(packed):
        return pair_doubling(packed, below_y, above_y, extent_y)

    start_y, end_y = edge_masks(y_index, total_y, 1)
    sub_y, super_y = implicit_rows(drift_y, diffusion[1], 1, start_y, end_y)
    second_section = spike_lines(sub_y, super_y, second_source, -2, reducer_y)
    third_source = (second_section - flux_z) / (1.0 + 2.0 * diffusion[2])

    def below_z(packed, stride):
        return from_behind(packed, "gz", stride)

    def above_z(packed, stride):
        return from_behind(packed, "gz", -stride)

    def reducer_z(packed):
        return pair_doubling(packed, below_z, above_z, extent_z)

    start_z, end_z = edge_masks(z_index, total_z, 2)
    sub_z, super_z = implicit_rows(drift_z, diffusion[2], 2, start_z, end_z)
    density_next = spike_lines(sub_z, super_z, third_source, -1, reducer_z)
    return density_next


def solution(mesh):
    placed = (P(None, "gy", "gz"), P(), P(), P(), P(), P())
    return jax.shard_map(
        body, mesh=mesh, in_specs=placed, out_specs=P(None, "gy", "gz"), check_vma=False
    )
```

profile of v0, /device:TPU:29, one launch (start us, length us, event | category | flops | bytes accessed | tf_op | source)
XLA Modules:
  0.0 103.5 jit_solution(14721710957265477174)
XLA Ops:
  0.9 3.1 %collective-permute-start.1 = (f32[32,1,128]{2,0,1:T(8,128)S(1)}, f32[32,1,128]{2,0,1:T(8,128)S(1)}, u32[]{:S(2)}, u32[]{:S(2)}) collective-permute-start(f32[32,1,128]{2,0,1:T(8,128)S(1)} %get-tuple-element.175), channel_id=1, source_target_pairs={{0,1},{1,2},{2,3},{3,4},{4,5},{5,6},{6,7},{8,9},{9,10},{10,11},{11... | collective-permute-start | bytes 49160 | tf_op jit(solution)/shard_map/ppermute | solution.py:16
  4.1 3.1 %collective-permute-start = (f32[32,1,128]{2,0,1:T(8,128)S(1)}, f32[32,1,128]{2,0,1:T(8,128)S(1)}, u32[]{:S(2)}, u32[]{:S(2)}) collective-permute-start(f32[32,1,128]{2,0,1:T(8,128)S(1)} %get-tuple-element.174), channel_id=1, source_target_pairs={{1,0},{2,1},{3,2},{4,3},{5,4},{6,5},{7,6},{9,8},{10,9},{11,10},{12... | collective-permute-start | bytes 49160 | tf_op jit(solution)/shard_map/ppermute | solution.py:17
  18.4 1.3 %collective-permute-start.3 = (f32[32,10,1]{2,0,1:T(8,128)}, f32[32,10,1]{2,0,1:T(8,128)S(1)}, u32[]{:S(2)}, u32[]{:S(2)}) collective-permute-start(f32[32,10,1]{2,0,1:T(8,128)} %get-tuple-element.109), channel_id=1, source_target_pairs={{0,8},{8,16},{16,24},{1,9},{9,17},{17,25},{2,10},{10,18},{18,26},{... | collective-permute-start | bytes 3848 | tf_op jit(solution)/shard_map/ppermute | solution.py:16
  19.7 3.8 %collective-permute-start.2 = (f32[32,10,1]{2,0,1:T(8,128)}, f32[32,10,1]{2,0,1:T(8,128)S(1)}, u32[]{:S(2)}, u32[]{:S(2)}) collective-permute-start(f32[32,10,1]{2,0,1:T(8,128)} %get-tuple-element.108), channel_id=1, source_target_pairs={{8,0},{16,8},{24,16},{9,1},{17,9},{25,17},{10,2},{18,10},{26,18},{... | collective-permute-start | bytes 3848 | tf_op jit(solution)/shard_map/ppermute | solution.py:17
  24.8 1.5 %add_divide_fusion = (f32[32,8,128]{2,0,1:T(8,128)S(1)}, f32[32,8,128]{2,0,1:T(8,128)S(1)}) fusion(f32[]{:T(128)} %bitcast.21, f32[32,8,128]{2,1,0:T(8,128)S(1)} %copy-done, f32[32,10,128]{2,0,1:T(8,128)S(1)} %fusion.1, f32[32,8,128]{2,0,1:T(8,128)S(1)} %copy.289, f32[32,1,128]{2,0,1:T(8,128)S(1)} %collective-permute-done.1, ...), kind=kLoop, calls=%fused_computation.111 | loop fusion | flops 819200 | bytes 1247756 | tf_op jit(solution)/shard_map/div | solution.py:234
  28.9 2.2 %collective-permute-start.4 = (f32[3,2,32,128]{3,2,1,0:T(8,128)S(1)}, f32[3,2,32,128]{3,2,1,0:T(8,128)S(1)}, u32[]{:S(2)}, u32[]{:S(2)}) collective-permute-start(f32[3,2,32,128]{3,2,1,0:T(8,128)S(1)} %pad_maximum_fusion.6), channel_id=1, source_target_pairs={{0,1},{1,2},{2,3},{3,4},{4,5},{5,6},{6,7},{8,9},{9,10},{10,11},{11... | collective-permute-start | bytes 294920 | tf_op jit(solution)/shard_map/ppermute | solution.py:25
  31.2 4.0 %collective-permute-start.5 = (f32[3,2,32,128]{3,2,1,0:T(8,128)S(1)}, f32[3,2,32,128]{3,2,1,0:T(8,128)S(1)}, u32[]{:S(2)}, u32[]{:S(2)}) collective-permute-start(f32[3,2,32,128]{3,2,1,0:T(8,128)S(1)} %pad_maximum_fusion.6), channel_id=1, source_target_pairs={{1,0},{2,1},{3,2},{4,3},{5,4},{6,5},{7,6},{9,8},{10,9},{11,10},{12... | collective-permute-start | bytes 294920 | tf_op jit(solution)/shard_map/ppermute | solution.py:25
  35.2 1.6 %collective-permute-done.5 = f32[3,2,32,128]{3,2,1,0:T(8,128)S(1)} collective-permute-done((f32[3,2,32,128]{3,2,1,0:T(8,128)S(1)}, f32[3,2,32,128]{3,2,1,0:T(8,128)S(1)}, u32[]{:S(2)}, u32[]{:S(2)}) %collective-permute-start.5) | collective-permute-done | bytes 98336 | tf_op jit(solution)/shard_map/ppermute | solution.py:25
  36.8 1.9 %collective-permute-start.6 = (f32[3,2,32,128]{3,2,1,0:T(8,128)S(1)}, f32[3,2,32,128]{3,2,1,0:T(8,128)S(1)}, u32[]{:S(2)}, u32[]{:S(2)}) collective-permute-start(f32[3,2,32,128]{3,2,1,0:T(8,128)S(1)} %pad_maximum_fusion.7), channel_id=1, source_target_pairs={{0,1},{1,2},{2,3},{3,4},{4,5},{5,6},{6,7},{8,9},{9,10},{10,11},{11... | collective-permute-start | bytes 294920 | tf_op jit(solution)/shard_map/ppermute | solution.py:25
  38.8 4.6 %collective-permute-start.7 = (f32[3,2,32,128]{3,2,1,0:T(8,128)S(1)}, f32[3,2,32,128]{3,2,1,0:T(8,128)S(1)}, u32[]{:S(2)}, u32[]{:S(2)}) collective-permute-start(f32[3,2,32,128]{3,2,1,0:T(8,128)S(1)} %pad_maximum_fusion.7), channel_id=1, source_target_pairs={{1,0},{2,1},{3,2},{4,3},{5,4},{6,5},{7,6},{9,8},{10,9},{11,10},{12... | collective-permute-start | bytes 294920 | tf_op jit(solution)/shard_map/ppermute | solution.py:25
  43.5 1.5 %collective-permute-done.7 = f32[3,2,32,128]{3,2,1,0:T(8,128)S(1)} collective-permute-done((f32[3,2,32,128]{3,2,1,0:T(8,128)S(1)}, f32[3,2,32,128]{3,2,1,0:T(8,128)S(1)}, u32[]{:S(2)}, u32[]{:S(2)}) %collective-permute-start.7) | collective-permute-done | bytes 98336 | tf_op jit(solution)/shard_map/ppermute | solution.py:25
  45.1 1.3 %collective-permute-start.8 = (f32[3,2,32,128]{3,2,1,0:T(8,128)S(1)}, f32[3,2,32,128]{3,2,1,0:T(8,128)S(1)}, u32[]{:S(2)}, u32[]{:S(2)}) collective-permute-start(f32[3,2,32,128]{3,2,1,0:T(8,128)S(1)} %pad_maximum_fusion.8), channel_id=1, source_target_pairs={{0,2},{1,3},{2,4},{3,5},{4,6},{5,7},{8,10},{9,11},{10,12},{11,13},... | collective-permute-start | bytes 294920 | tf_op jit(solution)/shard_map/ppermute | solution.py:25
  46.4 4.6 %collective-permute-start.9 = (f32[3,2,32,128]{3,2,1,0:T(8,128)S(1)}, f32[3,2,32,128]{3,2,1,0:T(8,128)S(1)}, u32[]{:S(2)}, u32[]{:S(2)}) collective-permute-start(f32[3,2,32,128]{3,2,1,0:T(8,128)S(1)} %pad_maximum_fusion.8), channel_id=1, source_target_pairs={{2,0},{3,1},{4,2},{5,3},{6,4},{7,5},{10,8},{11,9},{12,10},{13,11},... | collective-permute-start | bytes 294920 | tf_op jit(solution)/shard_map/ppermute | solution.py:25
  51.1 1.6 %collective-permute-done.9 = f32[3,2,32,128]{3,2,1,0:T(8,128)S(1)} collective-permute-done((f32[3,2,32,128]{3,2,1,0:T(8,128)S(1)}, f32[3,2,32,128]{3,2,1,0:T(8,128)S(1)}, u32[]{:S(2)}, u32[]{:S(2)}) %collective-permute-start.9) | collective-permute-done | bytes 98336 | tf_op jit(solution)/shard_map/ppermute | solution.py:25
  52.7 4.9 %collective-permute-start.11 = (f32[3,2,32,128]{3,2,1,0:T(8,128)S(1)}, f32[3,2,32,128]{3,2,1,0:T(8,128)S(1)}, u32[]{:S(2)}, u32[]{:S(2)}) collective-permute-start(f32[3,2,32,128]{3,2,1,0:T(8,128)S(1)} %pad_maximum_fusion.9), channel_id=1, source_target_pairs={{4,0},{5,1},{6,2},{7,3},{12,8},{13,9},{14,10},{15,11},{20,16},{21,... | collective-permute-start | bytes 294920 | tf_op jit(solution)/shard_map/ppermute | solution.py:25
  57.6 1.3 %collective-permute-start.10 = (f32[3,2,32,128]{3,2,1,0:T(8,128)S(1)}, f32[3,2,32,128]{3,2,1,0:T(8,128)S(1)}, u32[]{:S(2)}, u32[]{:S(2)}) collective-permute-start(f32[3,2,32,128]{3,2,1,0:T(8,128)S(1)} %pad_maximum_fusion.9), channel_id=1, source_target_pairs={{0,4},{1,5},{2,6},{3,7},{8,12},{9,13},{10,14},{11,15},{16,20},{17,... | collective-permute-start | bytes 294920 | tf_op jit(solution)/shard_map/ppermute | solution.py:25
  60.0 4.8 %collective-permute-done.10 = f32[3,2,32,128]{3,2,1,0:T(8,128)S(1)} collective-permute-done((f32[3,2,32,128]{3,2,1,0:T(8,128)S(1)}, f32[3,2,32,128]{3,2,1,0:T(8,128)S(1)}, u32[]{:S(2)}, u32[]{:S(2)}) %collective-permute-start.10) | collective-permute-done | bytes 98336 | tf_op jit(solution)/shard_map/ppermute | solution.py:25
  71.0 1.3 %collective-permute-start.12 = (f32[3,2,32,8]{2,3,1,0:T(8,128)S(1)}, f32[3,2,32,8]{2,3,1,0:T(8,128)S(1)}, u32[]{:S(2)}, u32[]{:S(2)}) collective-permute-start(f32[3,2,32,8]{2,3,1,0:T(8,128)S(1)} %pad_maximum_fusion.17), channel_id=1, source_target_pairs={{0,8},{8,16},{16,24},{1,9},{9,17},{17,25},{2,10},{10,18},{18,26},{... | collective-permute-start | bytes 18440 | tf_op jit(solution)/shard_map/ppermute | solution.py:25
  72.3 12.0 %collective-permute-start.13 = (f32[3,2,32,8]{2,3,1,0:T(8,128)S(1)}, f32[3,2,32,8]{2,3,1,0:T(8,128)S(1)}, u32[]{:S(2)}, u32[]{:S(2)}) collective-permute-start(f32[3,2,32,8]{2,3,1,0:T(8,128)S(1)} %pad_maximum_fusion.17), channel_id=1, source_target_pairs={{8,0},{16,8},{24,16},{9,1},{17,9},{25,17},{10,2},{18,10},{26,18},{... | collective-permute-start | bytes 18440 | tf_op jit(solution)/shard_map/ppermute | solution.py:25
  85.2 1.3 %collective-permute-start.14 = (f32[3,2,32,8]{2,3,1,0:T(8,128)S(1)}, f32[3,2,32,8]{2,3,1,0:T(8,128)S(1)}, u32[]{:S(2)}, u32[]{:S(2)}) collective-permute-start(f32[3,2,32,8]{2,3,1,0:T(8,128)S(1)} %pad_maximum_fusion.18), channel_id=1, source_target_pairs={{0,8},{8,16},{16,24},{1,9},{9,17},{17,25},{2,10},{10,18},{18,26},{... | collective-permute-start | bytes 18440 | tf_op jit(solution)/shard_map/ppermute | solution.py:25
  86.5 4.9 %collective-permute-start.15 = (f32[3,2,32,8]{2,3,1,0:T(8,128)S(1)}, f32[3,2,32,8]{2,3,1,0:T(8,128)S(1)}, u32[]{:S(2)}, u32[]{:S(2)}) collective-permute-start(f32[3,2,32,8]{2,3,1,0:T(8,128)S(1)} %pad_maximum_fusion.18), channel_id=1, source_target_pairs={{8,0},{16,8},{24,16},{9,1},{17,9},{25,17},{10,2},{18,10},{26,18},{... | collective-permute-start | bytes 18440 | tf_op jit(solution)/shard_map/ppermute | solution.py:25
  92.3 5.6 %collective-permute-start.17 = (f32[3,2,32,8]{2,3,1,0:T(8,128)S(1)}, f32[3,2,32,8]{2,3,1,0:T(8,128)S(1)}, u32[]{:S(2)}, u32[]{:S(2)}) collective-permute-start(f32[3,2,32,8]{2,3,1,0:T(8,128)S(1)} %pad_maximum_fusion.19), channel_id=1, source_target_pairs={{16,0},{24,8},{17,1},{25,9},{18,2},{26,10},{19,3},{27,11},{20,4},{... | collective-permute-start | bytes 18440 | tf_op jit(solution)/shard_map/ppermute | solution.py:25
  98.0 1.3 %collective-permute-start.16 = (f32[3,2,32,8]{2,3,1,0:T(8,128)S(1)}, f32[3,2,32,8]{2,3,1,0:T(8,128)S(1)}, u32[]{:S(2)}, u32[]{:S(2)}) collective-permute-start(f32[3,2,32,8]{2,3,1,0:T(8,128)S(1)} %pad_maximum_fusion.19), channel_id=1, source_target_pairs={{0,16},{8,24},{1,17},{9,25},{2,18},{10,26},{3,19},{11,27},{4,20},{... | collective-permute-start | bytes 18440 | tf_op jit(solution)/shard_map/ppermute | solution.py:25
  99.3 3.3 %collective-permute-done.16 = f32[3,2,32,8]{2,3,1,0:T(8,128)S(1)} collective-permute-done((f32[3,2,32,8]{2,3,1,0:T(8,128)S(1)}, f32[3,2,32,8]{2,3,1,0:T(8,128)S(1)}, u32[]{:S(2)}, u32[]{:S(2)}) %collective-permute-start.16) | collective-permute-done | bytes 6176 | tf_op jit(solution)/shard_map/ppermute | solution.py:25
  (203 shorter events, 21.5 us)
Async XLA Ops:
  0.9 16.2 %collective-permute-start.1 = (f32[32,1,128]{2,0,1:T(8,128)S(1)}, f32[32,1,128]{2,0,1:T(8,128)S(1)}, u32[]{:S(2)}, u32[]{:S(2)}) collective-permute-start(f32[32,1,128]{2,0,1:T(8,128)S(1)} %get-tuple-element.175), channel_id=1, source_target_pairs={{0,1},{1,2},{2,3},{3,4},{4,5},{5,6},{6,7},{8,9},{9,10},{10,11},{11... | collective-permute-start | bytes 49160 | tf_op jit(solution)/shard_map/ppermute | solution.py:16
  4.1 13.5 %collective-permute-start = (f32[32,1,128]{2,0,1:T(8,128)S(1)}, f32[32,1,128]{2,0,1:T(8,128)S(1)}, u32[]{:S(2)}, u32[]{:S(2)}) collective-permute-start(f32[32,1,128]{2,0,1:T(8,128)S(1)} %get-tuple-element.174), channel_id=1, source_target_pairs={{1,0},{2,1},{3,2},{4,3},{5,4},{6,5},{7,6},{9,8},{10,9},{11,10},{12... | collective-permute-start | bytes 49160 | tf_op jit(solution)/shard_map/ppermute | solution.py:17
  7.3 0.7 copy-start.3
  7.9 0.7 copy-start.5
  8.9 0.7 copy-start.2
  10.9 0.7 copy-start.1
  14.3 0.7 copy-start.4
  16.6 0.9 copy-start
  18.4 6.4 %collective-permute-start.3 = (f32[32,10,1]{2,0,1:T(8,128)}, f32[32,10,1]{2,0,1:T(8,128)S(1)}, u32[]{:S(2)}, u32[]{:S(2)}) collective-permute-start(f32[32,10,1]{2,0,1:T(8,128)} %get-tuple-element.109), channel_id=1, source_target_pairs={{0,8},{8,16},{16,24},{1,9},{9,17},{17,25},{2,10},{10,18},{18,26},{... | collective-permute-start | bytes 3848 | tf_op jit(solution)/shard_map/ppermute | solution.py:16
  19.7 5.2 %collective-permute-start.2 = (f32[32,10,1]{2,0,1:T(8,128)}, f32[32,10,1]{2,0,1:T(8,128)S(1)}, u32[]{:S(2)}, u32[]{:S(2)}) collective-permute-start(f32[32,10,1]{2,0,1:T(8,128)} %get-tuple-element.108), channel_id=1, source_target_pairs={{8,0},{16,8},{24,16},{9,1},{17,9},{25,17},{10,2},{18,10},{26,18},{... | collective-permute-start | bytes 3848 | tf_op jit(solution)/shard_map/ppermute | solution.py:17
  28.9 6.3 %collective-permute-start.4 = (f32[3,2,32,128]{3,2,1,0:T(8,128)S(1)}, f32[3,2,32,128]{3,2,1,0:T(8,128)S(1)}, u32[]{:S(2)}, u32[]{:S(2)}) collective-permute-start(f32[3,2,32,128]{3,2,1,0:T(8,128)S(1)} %pad_maximum_fusion.6), channel_id=1, source_target_pairs={{0,1},{1,2},{2,3},{3,4},{4,5},{5,6},{6,7},{8,9},{9,10},{10,11},{11... | collective-permute-start | bytes 294920 | tf_op jit(solution)/shard_map/ppermute | solution.py:25
  31.2 5.6 %collective-permute-start.5 = (f32[3,2,32,128]{3,2,1,0:T(8,128)S(1)}, f32[3,2,32,128]{3,2,1,0:T(8,128)S(1)}, u32[]{:S(2)}, u32[]{:S(2)}) collective-permute-start(f32[3,2,32,128]{3,2,1,0:T(8,128)S(1)} %pad_maximum_fusion.6), channel_id=1, source_target_pairs={{1,0},{2,1},{3,2},{4,3},{5,4},{6,5},{7,6},{9,8},{10,9},{11,10},{12... | collective-permute-start | bytes 294920 | tf_op jit(solution)/shard_map/ppermute | solution.py:25
  36.8 6.7 %collective-permute-start.6 = (f32[3,2,32,128]{3,2,1,0:T(8,128)S(1)}, f32[3,2,32,128]{3,2,1,0:T(8,128)S(1)}, u32[]{:S(2)}, u32[]{:S(2)}) collective-permute-start(f32[3,2,32,128]{3,2,1,0:T(8,128)S(1)} %pad_maximum_fusion.7), channel_id=1, source_target_pairs={{0,1},{1,2},{2,3},{3,4},{4,5},{5,6},{6,7},{8,9},{9,10},{10,11},{11... | collective-permute-start | bytes 294920 | tf_op jit(solution)/shard_map/ppermute | solution.py:25
  38.8 6.3 %collective-permute-start.7 = (f32[3,2,32,128]{3,2,1,0:T(8,128)S(1)}, f32[3,2,32,128]{3,2,1,0:T(8,128)S(1)}, u32[]{:S(2)}, u32[]{:S(2)}) collective-permute-start(f32[3,2,32,128]{3,2,1,0:T(8,128)S(1)} %pad_maximum_fusion.7), channel_id=1, source_target_pairs={{1,0},{2,1},{3,2},{4,3},{5,4},{6,5},{7,6},{9,8},{10,9},{11,10},{12... | collective-permute-start | bytes 294920 | tf_op jit(solution)/shard_map/ppermute | solution.py:25
  45.1 6.0 %collective-permute-start.8 = (f32[3,2,32,128]{3,2,1,0:T(8,128)S(1)}, f32[3,2,32,128]{3,2,1,0:T(8,128)S(1)}, u32[]{:S(2)}, u32[]{:S(2)}) collective-permute-start(f32[3,2,32,128]{3,2,1,0:T(8,128)S(1)} %pad_maximum_fusion.8), channel_id=1, source_target_pairs={{0,2},{1,3},{2,4},{3,5},{4,6},{5,7},{8,10},{9,11},{10,12},{11,13},... | collective-permute-start | bytes 294920 | tf_op jit(solution)/shard_map/ppermute | solution.py:25
  46.4 6.3 %collective-permute-start.9 = (f32[3,2,32,128]{3,2,1,0:T(8,128)S(1)}, f32[3,2,32,128]{3,2,1,0:T(8,128)S(1)}, u32[]{:S(2)}, u32[]{:S(2)}) collective-permute-start(f32[3,2,32,128]{3,2,1,0:T(8,128)S(1)} %pad_maximum_fusion.8), channel_id=1, source_target_pairs={{2,0},{3,1},{4,2},{5,3},{6,4},{7,5},{10,8},{11,9},{12,10},{13,11},... | collective-permute-start | bytes 294920 | tf_op jit(solution)/shard_map/ppermute | solution.py:25
  52.7 7.3 %collective-permute-start.11 = (f32[3,2,32,128]{3,2,1,0:T(8,128)S(1)}, f32[3,2,32,128]{3,2,1,0:T(8,128)S(1)}, u32[]{:S(2)}, u32[]{:S(2)}) collective-permute-start(f32[3,2,32,128]{3,2,1,0:T(8,128)S(1)} %pad_maximum_fusion.9), channel_id=1, source_target_pairs={{4,0},{5,1},{6,2},{7,3},{12,8},{13,9},{14,10},{15,11},{20,16},{21,... | collective-permute-start | bytes 294920 | tf_op jit(solution)/shard_map/ppermute | solution.py:25
  57.6 7.2 %collective-permute-start.10 = (f32[3,2,32,128]{3,2,1,0:T(8,128)S(1)}, f32[3,2,32,128]{3,2,1,0:T(8,128)S(1)}, u32[]{:S(2)}, u32[]{:S(2)}) collective-permute-start(f32[3,2,32,128]{3,2,1,0:T(8,128)S(1)} %pad_maximum_fusion.9), channel_id=1, source_target_pairs={{0,4},{1,5},{2,6},{3,7},{8,12},{9,13},{10,14},{11,15},{16,20},{17,... | collective-permute-start | bytes 294920 | tf_op jit(solution)/shard_map/ppermute | solution.py:25
  71.0 13.3 %collective-permute-start.12 = (f32[3,2,32,8]{2,3,1,0:T(8,128)S(1)}, f32[3,2,32,8]{2,3,1,0:T(8,128)S(1)}, u32[]{:S(2)}, u32[]{:S(2)}) collective-permute-start(f32[3,2,32,8]{2,3,1,0:T(8,128)S(1)} %pad_maximum_fusion.17), channel_id=1, source_target_pairs={{0,8},{8,16},{16,24},{1,9},{9,17},{17,25},{2,10},{10,18},{18,26},{... | collective-permute-start | bytes 18440 | tf_op jit(solution)/shard_map/ppermute | solution.py:25
  72.3 12.9 %collective-permute-start.13 = (f32[3,2,32,8]{2,3,1,0:T(8,128)S(1)}, f32[3,2,32,8]{2,3,1,0:T(8,128)S(1)}, u32[]{:S(2)}, u32[]{:S(2)}) collective-permute-start(f32[3,2,32,8]{2,3,1,0:T(8,128)S(1)} %pad_maximum_fusion.17), channel_id=1, source_target_pairs={{8,0},{16,8},{24,16},{9,1},{17,9},{25,17},{10,2},{18,10},{26,18},{... | collective-permute-start | bytes 18440 | tf_op jit(solution)/shard_map/ppermute | solution.py:25
  85.2 6.2 %collective-permute-start.14 = (f32[3,2,32,8]{2,3,1,0:T(8,128)S(1)}, f32[3,2,32,8]{2,3,1,0:T(8,128)S(1)}, u32[]{:S(2)}, u32[]{:S(2)}) collective-permute-start(f32[3,2,32,8]{2,3,1,0:T(8,128)S(1)} %pad_maximum_fusion.18), channel_id=1, source_target_pairs={{0,8},{8,16},{16,24},{1,9},{9,17},{17,25},{2,10},{10,18},{18,26},{... | collective-permute-start | bytes 18440 | tf_op jit(solution)/shard_map/ppermute | solution.py:25
  86.5 5.8 %collective-permute-start.15 = (f32[3,2,32,8]{2,3,1,0:T(8,128)S(1)}, f32[3,2,32,8]{2,3,1,0:T(8,128)S(1)}, u32[]{:S(2)}, u32[]{:S(2)}) collective-permute-start(f32[3,2,32,8]{2,3,1,0:T(8,128)S(1)} %pad_maximum_fusion.18), channel_id=1, source_target_pairs={{8,0},{16,8},{24,16},{9,1},{17,9},{25,17},{10,2},{18,10},{26,18},{... | collective-permute-start | bytes 18440 | tf_op jit(solution)/shard_map/ppermute | solution.py:25
  92.3 7.0 %collective-permute-start.17 = (f32[3,2,32,8]{2,3,1,0:T(8,128)S(1)}, f32[3,2,32,8]{2,3,1,0:T(8,128)S(1)}, u32[]{:S(2)}, u32[]{:S(2)}) collective-permute-start(f32[3,2,32,8]{2,3,1,0:T(8,128)S(1)} %pad_maximum_fusion.19), channel_id=1, source_target_pairs={{16,0},{24,8},{17,1},{25,9},{18,2},{26,10},{19,3},{27,11},{20,4},{... | collective-permute-start | bytes 18440 | tf_op jit(solution)/shard_map/ppermute | solution.py:25
  98.0 4.6 %collective-permute-start.16 = (f32[3,2,32,8]{2,3,1,0:T(8,128)S(1)}, f32[3,2,32,8]{2,3,1,0:T(8,128)S(1)}, u32[]{:S(2)}, u32[]{:S(2)}) collective-permute-start(f32[3,2,32,8]{2,3,1,0:T(8,128)S(1)} %pad_maximum_fusion.19), channel_id=1, source_target_pairs={{0,16},{8,24},{1,17},{9,25},{2,18},{10,26},{3,19},{11,27},{4,20},{... | collective-permute-start | bytes 18440 | tf_op jit(solution)/shard_map/ppermute | solution.py:25
where the time goes:
time: 104 us; the launch traced here: 103 us
  starting transfers between devices  62.6 us (60%)
  waiting for transfers between devices  15.6 us (15%)
  local copies, waits for them, and re-layouts  10.5 us (10%)
  other arithmetic  8.39 us (8%)
  between operations  5.17 us (5%)
  matrix products  1.19 us (1%)
    ppermute x14, starting transfers between devices, from_behind(): return lax.ppermute(block, axis, route)  51.3 us
    ppermute x14, waiting for transfers between devices, from_behind(): return lax.ppermute(block, axis, route)  15.6 us
    ppermute x2, starting transfers between devices, padded(): after = lax.ppermute(leading, axis, down)  6.84 us
    ppermute x2, starting transfers between devices, padded(): before = lax.ppermute(last, axis, up)  4.4 us
    unnamed x16, local copies, waits for them, and re-layouts  4.38 us
    div x18, other arithmetic, eliminate(): (source - sub_diag * below_set[2] - super_diag * above_set[2]) / pivots  2.36 us
  transfers between devices with their start and end apart: 18, of which 10 were waited for; matrix products, arithmetic and copies ran while one was open for 4% of the time, Pallas kernels for 0%

commit v1 on v0

v1 whole, which is shorter than its diff:
```python
import functools

import jax
import jax.numpy as jnp
from jax import lax
from jax.experimental import pallas as pl
from jax.experimental.pallas import tpu as pltpu
from jax.sharding import PartitionSpec as P

HALF_LIMIT = 600.0
LANES = 128
ROWS = 8
VMEM_LIMIT = 48 * 1024 * 1024


def iota(shape, axis):
    return lax.broadcasted_iota(jnp.int32, shape, axis)


def coordinate(positions, line_total):
    return (2.0 * positions.astype(jnp.float32) + 1.0) / line_total - 1.0


def roll(values, shift, axis):
    return pltpu.roll(values, shift % values.shape[axis], axis)


def matmul(left, right):
    return jnp.dot(
        left, right, precision=lax.Precision.HIGHEST, preferred_element_type=jnp.float32
    )


def lane_params(par):
    maps = par.shape[0]
    lane = iota((maps, LANES), 1)
    pick = ((lane % maps == iota((maps, LANES), 0)) & (lane < 6 * maps)).astype(jnp.float32)
    rows = lax.dot_general(
        par,
        pick,
        (((0,), (0,)), ((), ())),
        precision=lax.Precision.HIGHEST,
        preferred_element_type=jnp.float32,
    )
    group = iota((1, LANES), 1) // (2 * maps)
    first_term = (iota((1, LANES), 1) // maps) % 2 == 0

    def by_component(column, step):
        return jnp.where(
            group == 0,
            rows[column : column + 1],
            jnp.where(
                group == 1,
                rows[column + step : column + step + 1],
                rows[column + 2 * step : column + 2 * step + 1],
            ),
        )

    return {
        "sharpness": rows[3:4],
        "center_x": rows[0:1],
        "center_y": rows[1:2],
        "slope_x": jnp.where(first_term, by_component(4, 3), 0.0),
        "slope_y": jnp.where(first_term, by_component(5, 3), 0.0),
        "rest": jnp.where(first_term, by_component(13, 1), by_component(6, 3)),
    }


def side_factors(params, coord, center, slope):
    bump = jnp.exp(-params["sharpness"] * (coord - params[center]) ** 2)
    return bump, coord * params[slope]


def z_matrix(par, z_start, size_z, total_z):
    maps = par.shape[0]
    tall = jnp.concatenate([par[:, 2:4]] * (LANES // maps), axis=0)
    lane = iota((LANES, 2 * LANES), 1)
    position = jnp.where(
        lane < LANES, z_start + lane, jnp.where(lane == LANES, z_start + size_z, z_start - 1)
    )
    coord = coordinate(position, total_z)
    row = iota((LANES, 2 * LANES), 0)
    bump = jnp.exp(-tall[:, 1:2] * (coord - tall[:, 0:1]) ** 2)
    return jnp.where((row // maps) % 2 == 0, bump, bump * coord)


def component_part(values, maps, component):
    return jnp.where(iota(values.shape, 0) // (2 * maps) == component, values, 0.0)


def half_drift(left, right):
    return HALF_LIMIT * jnp.tanh(matmul(left, right))


def pack_rows(first, last):
    f2, l2 = first[:, LANES:], last[:, LANES:]
    lane = iota(f2.shape, 1)
    extra = jnp.where(
        lane == 0,
        f2,
        jnp.where(
            lane == 1, roll(f2, 2, 1), jnp.where(lane == 2, roll(l2, 2, 1), roll(l2, 4, 1))
        ),
    )
    return jnp.concatenate([first[:, :LANES], last[:, :LANES], extra], axis=0)


def unpack_rows(message, size_x):
    extra = message[2 * size_x :]
    lane = iota(extra.shape, 1)
    by_two, by_four = roll(extra, -2, 1), roll(extra, -4, 1)
    f2 = jnp.where(lane == LANES - 1, by_two, extra)
    l2 = jnp.where(lane == LANES - 1, by_four, by_two)
    return (
        jnp.concatenate([message[:size_x], f2], axis=1),
        jnp.concatenate([message[size_x : 2 * size_x], l2], axis=1),
    )


def merge_coefs(low, high):
    inverse = 1.0 / (1.0 - low[3] * high[0])
    onward, back = low[1] * inverse, high[2] * inverse
    return (
        low[0] + onward * high[0] * low[2],
        onward * high[1],
        back * low[2],
        high[3] + back * low[3] * high[1],
    )


def merge_values(low, high, low_values, high_values):
    inverse = 1.0 / (1.0 - low[3] * high[0])
    return (
        low_values[0] + low[1] * inverse * (high_values[0] + high[0] * low_values[1]),
        high_values[1] + high[2] * inverse * (low_values[1] + low[3] * high_values[0]),
    )


def chain(coefs, values, below, above):
    count = len(coefs)
    held, slope = below, None
    befores, firsts = [], []
    for j in range(count):
        a_first, c_first, a_last, c_last = coefs[j]
        r_first, r_last = values[j]
        befores.append((held, slope))
        if slope is None:
            first, first_slope = r_first + a_first * held, c_first
            held, slope = r_last + a_last * held, c_last
        else:
            inverse = 1.0 / (1.0 - a_first * slope)
            first = (r_first + a_first * held) * inverse
            first_slope = c_first * inverse
            held, slope = (
                r_last + a_last * (held + slope * first),
                c_last + a_last * slope * first_slope,
            )
        firsts.append((first, first_slope))
    seen_above = [None] * count
    seen_below = [None] * count
    upper = above
    for j in reversed(range(count)):
        seen_above[j] = upper
        upper = firsts[j][0] + firsts[j][1] * upper
        held, slope = befores[j]
        seen_below[j] = held if slope is None else held + slope * upper
    return seen_below, seen_above


def solve_x(up, down, source, pivot):
    size = source.shape[0]
    half = size // 2
    low_g, low_c, high_g, high_c = {}, {}, {}, {}
    g = c = None
    for i in range(half):
        if i == 0:
            weight = 1.0 / pivot
            c = down[1] * weight
            g = source[0] * weight
        else:
            weight = 1.0 / (pivot - up[i - 1] * c)
            g = (source[i] + up[i - 1] * g) * weight
            c = down[i + 1] * weight
        low_g[i], low_c[i] = g, c
    for i in reversed(range(half, size)):
        if i == size - 1:
            weight = 1.0 / pivot
            c = up[i - 1] * weight
            g = source[i] * weight
        else:
            weight = 1.0 / (pivot - down[i + 1] * c)
            g = (source[i] + down[i + 1] * g) * weight
            c = up[i - 1] * weight
        high_g[i], high_c[i] = g, c
    out = [None] * size
    inverse = 1.0 / (1.0 - low_c[half - 1] * high_c[half])
    out[half - 1] = (low_g[half - 1] + low_c[half - 1] * high_g[half]) * inverse
    out[half] = high_g[half] + high_c[half] * out[half - 1]
    for i in reversed(range(half - 1)):
        out[i] = low_g[i] + low_c[i] * out[i + 1]
    for i in range(half + 1, size):
        out[i] = high_g[i] + high_c[i] * out[i - 1]
    return out


def start_kernel(
    extent_y, extent_z, diffusion, par_ref, density, message, base, from_below, from_above, solved
):
    size_x, size_y, size_z = density.shape
    total_y, total_z = size_y * extent_y, size_z * extent_z
    y_start = lax.axis_index("gy") * size_y
    z_start = lax.axis_index("gz") * size_z
    maps = par_ref.shape[0]
    par = par_ref[...]
    params = lane_params(par)
    x_coord = coordinate(iota((size_x, LANES), 0), size_x)
    x_bump, x_part = side_factors(params, x_coord, "center_x", "slope_x")
    y_row = iota((size_y, LANES), 0)

    def y_factors(position):
        bump, part = side_factors(params, coordinate(position, total_y), "center_y", "slope_y")
        return bump, part + params["rest"]

    y_bump, y_part = y_factors(y_start + y_row)
    out_bump, out_part = y_factors(jnp.where(y_row == 0, y_start + size_y, y_start - 1))
    z_values = z_matrix(par, z_start, size_z, total_z)
    parts = [component_part(z_values, maps, c) for c in range(3)]
    d0, d1, d2 = diffusion[0], diffusion[1], diffusion[2]

    def rows_by_x(bump, part):
        return jnp.concatenate(
            [
                (x_bump[i : i + 1] * bump) * (x_part[i : i + 1] + part)
                for i in range(size_x)
            ],
            axis=0,
        )

    right = jnp.concatenate([parts[0], parts[1][:, :LANES], parts[2][:, :LANES]], axis=1)
    drifts = half_drift(rows_by_x(y_bump, y_part), right)
    out_drift = half_drift(rows_by_x(out_bump, out_part), parts[0][:, :LANES])

    def block(columns):
        return drifts[:, columns * LANES : (columns + 1) * LANES].reshape(size_x, size_y, LANES)

    drift_x, plane_drift, drift_y, drift_z = block(0), block(1), block(2), block(3)
    out_drift = out_drift.reshape(size_x, size_y, LANES)
    rho = density[...]
    zero = jnp.zeros((1, size_y, LANES), jnp.float32)
    up, down = (d0 + drift_x) * rho, (d0 - drift_x) * rho
    total = (
        jnp.concatenate([zero, up[:-1]], axis=0)
        + jnp.concatenate([down[1:], zero], axis=0)
        - (2.0 * (d0 + d1 + d2)) * rho
    )
    sublane = iota((size_x, size_y, LANES), 1)
    lane = iota((size_x, size_y, LANES), 2)
    up, down = roll((d1 + drift_y) * rho, 1, 1), roll((d1 - drift_y) * rho, -1, 1)
    at_low, at_high = sublane == 0, sublane == size_y - 1
    row_source = jnp.where(at_low, up, jnp.where(at_high, down, 0.0))
    total = total + jnp.where(at_low, 0.0, up) + jnp.where(at_high, 0.0, down)
    up, down = roll((d2 + drift_z) * rho, 1, 2), roll((d2 - drift_z) * rho, -1, 2)
    at_low, at_high = lane == 0, lane == size_z - 1
    plane_source = jnp.where(at_low, up, jnp.where(at_high, down, 0.0))
    total = total + jnp.where(at_low, 0.0, up) + jnp.where(at_high, 0.0, down)

    source = jnp.concatenate([total, row_source, plane_source], axis=1)
    drift = jnp.concatenate([drift_x, out_drift, plane_drift], axis=1)
    ups, downs = d0 + drift, d0 - drift
    answers = solve_x(ups, downs, source, 1.0 + 2.0 * d0)
    for i in range(size_x):
        solved[i] = answers[i]

    def rows_by_y(position):
        row = iota((1, LANES), 0)
        bump, part = y_factors(row + position)
        return (x_bump * bump) * (x_part + part)

    left = jnp.concatenate([rows_by_y(y_start + j) for j in range(-1, size_y + 1)], axis=0)
    line_drift = half_drift(left, parts[1]).reshape(size_y + 2, size_x, 2 * LANES)
    pivot = 1.0 + 2.0 * d1
    at_start = y_start == 0
    at_end = y_start + size_y == total_y
    g = a = c = None
    gs, as_, cs = [], [], []
    for j in range(size_y):
        value = jnp.concatenate([solved[:, j, :], solved[:, 2 * size_y + j, :]], axis=1)
        lower = d1 + line_drift[j]
        upper = d1 - line_drift[j + 2]
        if j == 0:
            lower = jnp.where(at_start, 0.0, lower)
        if j == size_y - 1:
            upper = jnp.where(at_end, 0.0, upper)
        if j == 0:
            weight = 1.0 / pivot
            g, a = value * weight, lower * weight
        else:
            weight = 1.0 / (pivot - lower * c)
            g, a = (value + lower * g) * weight, lower * a * weight
        c = upper * weight
        gs.append(g)
        as_.append(a)
        cs.append(c)
    base[size_y - 1], from_below[size_y - 1], from_above[size_y - 1] = g, a, c
    r_last = g
    for j in reversed(range(size_y - 1)):
        g, a, c = gs[j] + cs[j] * g, as_[j] + cs[j] * a, cs[j] * c
        base[j], from_below[j], from_above[j] = g, a, c
    pushed_up = solved[:, size_y, :] / (d1 + line_drift[size_y][:, :LANES])
    pushed_down = solved[:, 2 * size_y - 1, :] / (d1 - line_drift[1][:, :LANES])
    blank = jnp.zeros_like(pushed_up)
    message[...] = pack_rows(
        g + jnp.concatenate([pushed_down, blank], axis=1),
        r_last + jnp.concatenate([pushed_up, blank], axis=1),
    )


def line_kernel(extent_y, extent_z, size_x, size_y, size_z, diffusion, par_ref, coefs, drifts):
    total_y, total_z = size_y * extent_y, size_z * extent_z
    z_start = lax.axis_index("gz") * size_z
    maps = par_ref.shape[0]
    par = par_ref[...]
    params = lane_params(par)
    x_coord = coordinate(iota((size_x, LANES), 0), size_x)
    x_bump, x_part = side_factors(params, x_coord, "center_x", "slope_x")
    right = component_part(z_matrix(par, z_start, size_z, total_z), maps, 1)
    d1 = diffusion[1]
    pivot = 1.0 + 2.0 * d1

    @pl.loop(0, extent_y)
    def _(number):
        rows = []
        for j in range(size_y):
            position = iota((1, LANES), 0) + (number * size_y + j)
            bump, part = side_factors(
                params, coordinate(position, total_y), "center_y", "slope_y"
            )
            rows.append((x_bump * bump) * (x_part + (part + params["rest"])))
        drift = half_drift(jnp.concatenate(rows, axis=0), right)
        drifts[pl.ds(number * size_y + 1, size_y)] = drift.reshape(size_y, size_x, 2 * LANES)

    drifts[0] = jnp.full((size_x, 2 * LANES), -d1, jnp.float32)
    drifts[total_y + 1] = jnp.full((size_x, 2 * LANES), d1, jnp.float32)

    @pl.loop(0, extent_y)
    def _(number):
        start = number * size_y
        weight = 1.0 / pivot
        a_first = (d1 + drifts[start]) * weight
        c_first = (d1 - drifts[start + 2]) * weight
        a_last, c_last = a_first, c_first
        for j in range(1, size_y):
            lower = d1 + drifts[start + j]
            upper = d1 - drifts[start + j + 2]
            weight = 1.0 / (pivot - lower * c_last)
            step, c_last = lower * weight, upper * weight
            a_last = step * a_last
            a_first = a_first + c_first * a_last
            c_first = c_first * c_last
        coefs[number, 0] = a_first
        coefs[number, 1] = c_first
        coefs[number, 2] = a_last
        coefs[number, 3] = c_last


def z_coef_kernel(
    extent_y, extent_z, size_x, size_y, size_z, diffusion, par_ref, steps, ends, pushes, packed
):
    total_y, total_z = size_y * extent_y, size_z * extent_z
    y_start = lax.axis_index("gy") * size_y
    z_start = lax.axis_index("gz") * size_z
    maps = par_ref.shape[0]
    par = par_ref[...]
    params = lane_params(par)
    x_coord = coordinate(iota((size_x, LANES), 0), size_x)
    x_bump, x_part = side_factors(params, x_coord, "center_x", "slope_x")
    right = component_part(z_matrix(par, z_start, size_z, total_z), maps, 2)
    d2 = diffusion[2]
    scale = 1.0 / (1.0 + 2.0 * d2)
    rows = []
    for j in range(size_y):
        position = iota((1, LANES), 0) + (y_start + j)
        bump, part = side_factors(params, coordinate(position, total_y), "center_y", "slope_y")
        rows.append((x_bump * bump) * (x_part + (part + params["rest"])))
    drift = half_drift(jnp.concatenate(rows, axis=0), right)
    inner, outer = drift[:, :LANES], drift[:, LANES:]
    lane = iota(inner.shape, 1)
    low, high = lane == 0, lane == size_z - 1
    before, after = roll(inner, 1, 1), roll(inner, -1, 1)
    pushes[...] = (1.0 / jnp.where(low, d2 + before, d2 - after)).reshape(pushes.shape)
    before = jnp.where(low, roll(outer, 1, 1), before)
    after = jnp.where(high, roll(outer, -1, 1), after)
    below = jnp.where(low & (z_start == 0), 0.0, (d2 + before) * scale)
    above = jnp.where(high & (z_start + size_z == total_z), 0.0, (d2 - after) * scale)
    stride, level = 1, 0
    while stride < size_z:
        low, high = lane < stride, lane >= size_z - stride
        low_a = jnp.where(low, 1.0, roll(below, stride, 1))
        low_c = jnp.where(low, 0.0, roll(above, stride, 1))
        high_a = jnp.where(high, 0.0, roll(below, -stride, 1))
        high_c = jnp.where(high, 1.0, roll(above, -stride, 1))
        inverse = 1.0 / (1.0 - below * low_c - above * high_a)
        below, above = below * inverse, above * inverse
        factor = scale if level == 0 else 1.0
        steps[level, 0] = (inverse * factor).reshape(pushes.shape)
        steps[level, 1] = jnp.where(low, 0.0, below * factor).reshape(pushes.shape)
        steps[level, 2] = jnp.where(high, 0.0, above * factor).reshape(pushes.shape)
        below, above = below * low_a, above * high_c
        stride, level = stride * 2, level + 1
    ends[0] = below.reshape(pushes.shape)
    ends[1] = above.reshape(pushes.shape)
    packed[...] = pack_ends(
        [ends[0, j] for j in range(size_y)], 1, size_y
    ) + pack_ends([ends[1, j] for j in range(size_y)], 2, size_y)


def pack_ends(rows, slot, size_y):
    shape = rows[0].shape
    lane = iota(shape, 1)
    out = jnp.zeros(shape, jnp.float32)
    for j in range(size_y):
        first = slot * 2 * size_y + j
        last = first + size_y
        out = jnp.where(lane == first, roll(rows[j], first, 1), out)
        out = jnp.where(lane == last, roll(rows[j], last - (LANES - 1), 1), out)
    return out


def gather_members(refs, own, count):
    held = [ref[...] for ref in refs]
    return [
        functools.reduce(
            lambda acc, s: jnp.where((own ^ s) == j, held[s], acc), range(1, count), held[0]
        )
        for j in range(count)
    ]


def merge_kernel(stride, radix, size_x, coefs, *refs):
    received, message = refs[:radix], refs[radix]
    digit = lax.rem(lax.div(lax.axis_index("gy"), stride), radix)
    first = lax.div(lax.axis_index("gy"), stride) - digit
    values = [unpack_rows(m, size_x) for m in gather_members(received, digit, radix)]
    group = [tuple(coefs[first + j, q] for q in range(4)) for j in range(radix)]
    merged, total = group[0], values[0]
    for j in range(1, radix):
        total = merge_values(merged, group[j], total, values[j])
        merged = merge_coefs(merged, group[j])
    message[...] = pack_rows(*total)


def group_kernel(radix, coefs, merged):
    @pl.loop(0, merged.shape[0])
    def _(number):
        total = tuple(coefs[number * radix, q] for q in range(4))
        for j in range(1, radix):
            total = merge_coefs(total, tuple(coefs[number * radix + j, q] for q in range(4)))
        for q in range(4):
            merged[number, q] = total[q]


def middle_kernel(levels, size_x, *refs):
    refs = list(refs)
    steps, pushes, packed, base, from_below, from_above = refs[:6]
    refs = refs[6:]
    inputs = []
    for stride, radix in levels:
        inputs.append((refs[0], refs[1 : 1 + radix]))
        refs = refs[1 + radix :]
    message, doubled, seen = refs
    size_y = base.shape[0]
    below = above = jnp.zeros((size_x, 2 * LANES), jnp.float32)
    for (stride, radix), (coefs, received) in zip(reversed(levels), reversed(inputs)):
        digit = lax.rem(lax.div(lax.axis_index("gy"), stride), radix)
        first = lax.div(lax.axis_index("gy"), stride) - digit
        values = [unpack_rows(m, size_x) for m in gather_members(received, digit, radix)]
        group = [tuple(coefs[first + j, q] for q in range(4)) for j in range(radix)]
        lows, highs = chain(group, values, below, above)
        for j in range(radix):
            seen[j, 0] = lows[j]
            seen[j, 1] = highs[j]
        below, above = seen[digit, 0], seen[digit, 1]
    inner, outer = [], []
    for j in range(size_y):
        value = base[j] + from_below[j] * below + from_above[j] * above
        inner.append(value[:, :LANES])
        outer.append(value[:, LANES:] * pushes[j])
    values = jnp.stack(inner)
    stride, level = 1, 0
    while stride < LANES:
        values = (
            steps[level, 0] * values
            + steps[level, 1] * roll(values, stride, 2)
            + steps[level, 2] * roll(values, -stride, 2)
        )
        stride, level = stride * 2, level + 1
    doubled[...] = values
    lane = iota(inner[0].shape, 1)
    rows = []
    for j in range(size_y):
        rows.append(
            values[j]
            + jnp.where(
                lane == 0,
                roll(outer[j], 1, 1),
                jnp.where(lane == LANES - 1, roll(outer[j], -1, 1), 0.0),
            )
        )
    message[...] = pack_ends(rows, 0, size_y) + packed[...]


def merge_z(low, high):
    inverse = 1.0 / (1.0 - low[5] * high[2])
    onward, back = low[4] * inverse, high[3] * inverse
    return (
        low[0] + onward * (high[0] + high[2] * low[1]),
        high[1] + back * (low[1] + low[5] * high[0]),
        low[2] + onward * high[2] * low[3],
        back * low[3],
        onward * high[4],
        high[5] + back * low[5] * high[4],
    )


def unpack_ends(message, size_y):
    return tuple(message if s == 0 else roll(message, -s * size_y, 1) for s in range(6))


def merge_z_kernel(stride, radix, size_y, *refs):
    received, message = refs[:radix], refs[radix]
    digit = lax.rem(lax.div(lax.axis_index("gz"), stride), radix)
    members = [unpack_ends(m, size_y) for m in gather_members(received, digit, radix)]
    total = functools.reduce(merge_z, members)
    lane = iota(total[0].shape, 1)
    out = jnp.zeros(total[0].shape, jnp.float32)
    for s in range(6):
        shifted = total[s] if s == 0 else roll(total[s], s * size_y, 1)
        out = jnp.where(lane // size_y == s, shifted, out)
    message[...] = out


def end_kernel(levels, density, doubled, ends, *refs):
    refs = list(refs)
    inputs = []
    for stride, radix in levels:
        inputs.append(refs[:radix])
        refs = refs[radix:]
    out, seen = refs
    size_x, size_y, _ = density.shape
    below = above = jnp.zeros((size_x, LANES), jnp.float32)
    for (stride, radix), received in zip(reversed(levels), reversed(inputs)):
        digit = lax.rem(lax.div(lax.axis_index("gz"), stride), radix)
        members = [unpack_ends(m, size_y) for m in gather_members(received, digit, radix)]
        lows, highs = chain(
            [(m[2], m[4], m[3], m[5]) for m in members],
            [(m[0], m[1]) for m in members],
            below,
            above,
        )
        for j in range(radix):
            seen[j, 0] = lows[j]
            seen[j, 1] = highs[j]
        below, above = seen[digit, 0], seen[digit, 1]
    for j in range(size_y):
        out[:, j, :] = (
            density[:, j, :]
            + doubled[j]
            + ends[0, j] * below[:, j : j + 1]
            + ends[1, j] * above[:, j : j + 1]
        )


def radices(extent):
    rounds, stride = [], 1
    while stride < extent:
        left = extent // stride
        power = left.bit_length() - 1
        radix = 4 if left % 4 == 0 and power % 2 == 0 else 2
        rounds.append((stride, radix))
        stride *= radix
    return rounds


def exchange(message, axis, stride, radix):
    devices = range(lax.axis_size(axis))
    return [message] + [
        lax.ppermute(message, axis, [(i, i ^ (s * stride)) for i in devices])
        for s in range(1, radix)
    ]


def body(density, diffusion, centers, sharpness, affine, offsets):
    size_x, size_y, size_z = density.shape
    extent_y, extent_z = lax.axis_size("gy"), lax.axis_size("gz")
    sizes = (extent_y, extent_z, size_x, size_y, size_z)
    maps = centers.shape[0]
    wide = (size_y, size_x, 2 * LANES)
    narrow = (size_y, size_x, LANES)
    float32 = jnp.float32

    def shape(*dims):
        return jax.ShapeDtypeStruct(dims, float32)

    vmem = pl.BlockSpec(memory_space=pltpu.VMEM)
    smem = pl.BlockSpec(memory_space=pltpu.SMEM)

    def call(kernel, inputs, outputs, in_specs=None, scratch=(), flops=10**6):
        return pl.pallas_call(
            kernel,
            out_shape=outputs,
            in_specs=in_specs or [vmem] * len(inputs),
            out_specs=jax.tree.map(lambda _: vmem, outputs),
            scratch_shapes=list(scratch),
            compiler_params=pltpu.CompilerParams(vmem_limit_bytes=VMEM_LIMIT),
            cost_estimate=pl.CostEstimate(flops=flops, bytes_accessed=10**6, transcendentals=0),
        )(*inputs)

    par = jnp.concatenate(
        [centers, sharpness[:, None], affine.reshape(maps, 9), offsets], axis=1
    )
    message, base, from_below, from_above = call(
        functools.partial(start_kernel, extent_y, extent_z),
        (diffusion, par, density),
        (shape(3 * size_x, LANES), shape(*wide), shape(*wide), shape(*wide)),
        [smem, vmem, vmem],
        [pltpu.VMEM((size_x, 3 * size_y, LANES), float32)],
    )
    total_y = extent_y * size_y
    coefs = call(
        functools.partial(line_kernel, *sizes),
        (diffusion, par),
        shape(extent_y, 4, size_x, 2 * LANES),
        [smem, vmem],
        [pltpu.VMEM((total_y + 2, size_x, 2 * LANES), float32)],
    )
    doublings = size_z.bit_length() - 1
    steps, ends, pushes, packed = call(
        functools.partial(z_coef_kernel, *sizes),
        (diffusion, par),
        (shape(doublings, 3, *narrow), shape(2, *narrow), shape(*narrow), shape(size_x, LANES)),
        [smem, vmem],
    )
    y_levels, z_levels = radices(extent_y), radices(extent_z)
    line_inputs = []
    for number, (stride, radix) in enumerate(y_levels):
        received = exchange(message, "gy", stride, radix)
        line_inputs += [coefs] + received
        if number + 1 < len(y_levels):
            message = call(
                functools.partial(merge_kernel, stride, radix, size_x),
                [coefs] + received,
                shape(3 * size_x, LANES),
            )
            coefs = call(
                functools.partial(group_kernel, radix),
                [coefs],
                shape(extent_y // (stride * radix), 4, size_x, 2 * LANES),
            )
    message, doubled = call(
        functools.partial(middle_kernel, y_levels, size_x),
        [steps, pushes, packed, base, from_below, from_above] + line_inputs,
        (shape(size_x, LANES), shape(*narrow)),
        scratch=[pltpu.VMEM((4, 2, size_x, 2 * LANES), float32)],
    )
    end_inputs = []
    for number, (stride, radix) in enumerate(z_levels):
        received = exchange(message, "gz", stride, radix)
        end_inputs += received
        if number + 1 < len(z_levels):
            message = call(
                functools.partial(merge_z_kernel, stride, radix, size_y),
                received,
                shape(size_x, LANES),
            )
    return call(
        functools.partial(end_kernel, z_levels),
        [density, doubled, ends] + end_inputs,
        shape(size_x, size_y, size_z),
        scratch=[pltpu.VMEM((4, 2, size_x, LANES), float32)],
    )


def solution(mesh):
    placed = (P(None, "gy", "gz"), P(), P(), P(), P(), P())
    return jax.shard_map(
        body, mesh=mesh, in_specs=placed, out_specs=P(None, "gy", "gz"), check_vma=False
    )
```

time: 104 us -> 29.7 us (0.29)
  the two profiles are of different devices: /device:TPU:29 before, /device:TPU:0 now
where the time goes in v1:
time: 29.7 us; the launch traced here: 29.5 us
  Pallas kernels  11.6 us (39%)
  starting transfers between devices  9.38 us (32%)
  local copies, waits for them, and re-layouts  4.59 us (15%)
  waiting for transfers between devices  3.76 us (13%)
    pallas_call x7, Pallas kernels, call(): pl.pallas_call(kernel, out_shape=outputs, in_specs=in_specs or [vmem] * l...  11.6 us
    ppermute x7, starting transfers between devices, exchange(): lax.ppermute(message, axis, [(i, i ^ s * stride) for i in devices])  9.38 us
    ppermute x7, waiting for transfers between devices, exchange(): lax.ppermute(message, axis, [(i, i ^ s * stride) for i in devices])  3.76 us
    unnamed x8, local copies, waits for them, and re-layouts  3.08 us
    reshape x2, local copies, waits for them, and re-layouts, body(): affine.reshape(maps, 9)  0.78 us
    broadcast_in_dim x1, local copies, waits for them, and re-layouts, body(): sharpness[:, None]  0.73 us
  transfers between devices with their start and end apart: 7, of which 3 were waited for; matrix products, arithmetic and copies ran while one was open for 0% of the time, Pallas kernels for 25%

profile of v1, /device:TPU:0, one launch (start us, length us, event | category | flops | bytes accessed | tf_op | source)
XLA Modules:
  0.0 29.5 jit_solution(7469400813936156612)
XLA Ops:
  0.0 0.8 %copy.11 = f32[16,3]{1,0:T(8,128)S(1)} copy(f32[16,3]{0,1:T(4,128)} %param.8) | data formatting | bytes 384 | tf_op args[2]
  0.8 0.7 %copy.12 = f32[16,1]{1,0:T(8,128)S(1)} copy(f32[16,1]{0,1:T(1,128)} %bitcast.3) | data formatting | bytes 128 | tf_op jit(solution)/shard_map/broadcast_in_dim | solution.py:619
  1.5 0.7 %reshape.3 = f32[16,9]{0,1:T(8,128)S(1)} reshape(f32[16,3,3]{0,2,1:T(4,128)} %param.10) | data formatting | bytes 1152 | tf_op jit(solution)/shard_map/reshape | solution.py:619
  2.2 0.1 copy.13
  2.3 0.8 %copy.14 = f32[16,3]{1,0:T(8,128)S(1)} copy(f32[16,3]{0,1:T(4,128)} %param.11) | data formatting | bytes 384 | tf_op args[5]
  3.0 0.1 pad_maximum_fusion.par_ref
  3.1 0.9 %copy-done = f32[32,8,128]{2,1,0:T(8,128)S(1)} copy-done((f32[32,8,128]{2,1,0:T(8,128)S(1)}, f32[32,8,128]{2,1,0:T(8,128)}, u32[]{:S(2)}) %copy-start) | copy-done | bytes 131096
  4.0 0.7 %copy-done.2 = f32[3]{0:T(128)S(1)} copy-done((f32[3]{0:T(128)S(1)}, f32[3]{0:T(128)}, u32[]{:S(2)}) %copy-start.2) | copy-done | bytes 36
  4.7 2.1 %shard_map.65 = (f32[96,128]{1,0:T(8,128)S(1)}, f32[8,32,256]{2,1,0:T(8,128)S(1)}, f32[8,32,256]{2,1,0:T(8,128)S(1)}, f32[8,32,256]{2,1,0:T(8,128)S(1)}) custom-call(f32[3]{0:T(128)S(1)} %copy-done.2, f32[16,16]{1,0:T(8,128)S(1)} %pad_maximum_fusion.par_ref, f32[32,8,128]{2,1,0:T(8,128)S(1)} %copy-done), custom_call_target="tpu_custom_call" | custom-call | flops 1000000 | bytes 1000000 | tf_op jit(solution)/shard_map/pallas_call | solution.py:608
  6.8 3.0 %collective-permute-start = (f32[96,128]{1,0:T(8,128)S(1)}, f32[96,128]{1,0:T(8,128)S(1)}, u32[]{:S(2)}, u32[]{:S(2)}) collective-permute-start(f32[96,128]{1,0:T(8,128)S(1)} %get-tuple-element.21.refs_0_.refs_7_), channel_id=1, source_target_pairs={{0,1},{1,0},{2,3},{3,2},{4,5},{5,4},{6,7},{7,6},{8,9},{9,8},{10,11... | collective-permute-start | bytes 147464 | tf_op jit(solution)/shard_map/ppermute | solution.py:587
  9.8 4.9 %shard_map.66.coefs.refs_6_ = f32[8,4,32,256]{3,2,1,0:T(8,128)S(1)} custom-call(f32[3]{0:T(128)S(1)} %copy-done.2, f32[16,16]{1,0:T(8,128)S(1)} %pad_maximum_fusion.par_ref), custom_call_target="tpu_custom_call" | custom-call | flops 1000000 | bytes 1000000 | tf_op jit(solution)/shard_map/pallas_call | solution.py:608
  14.8 0.2 shard_map.68.refs_10_
  14.9 3.7 %collective-permute-start.3 = (f32[96,128]{1,0:T(8,128)S(1)}, f32[96,128]{1,0:T(8,128)S(1)}, u32[]{:S(2)}, u32[]{:S(2)}) collective-permute-start(f32[96,128]{1,0:T(8,128)S(1)} %shard_map.68.refs_10_), channel_id=1, source_target_pairs={{0,6},{1,7},{2,4},{3,5},{4,2},{5,3},{6,0},{7,1},{8,14},{9,15},{10,... | collective-permute-start | bytes 147464 | tf_op jit(solution)/shard_map/ppermute | solution.py:587
  18.6 0.8 %collective-permute-start.1 = (f32[96,128]{1,0:T(8,128)S(1)}, f32[96,128]{1,0:T(8,128)S(1)}, u32[]{:S(2)}, u32[]{:S(2)}) collective-permute-start(f32[96,128]{1,0:T(8,128)S(1)} %shard_map.68.refs_10_), channel_id=1, source_target_pairs={{0,2},{1,3},{2,0},{3,1},{4,6},{5,7},{6,4},{7,5},{8,10},{9,11},{10,... | collective-permute-start | bytes 147464 | tf_op jit(solution)/shard_map/ppermute | solution.py:587
  19.4 0.1 shard_map.67.refs_9_
  19.5 2.3 %shard_map.64 = (f32[7,3,8,32,128]{4,3,2,1,0:T(8,128)S(1)}, f32[2,8,32,128]{3,2,1,0:T(8,128)S(1)}, f32[8,32,128]{2,1,0:T(8,128)S(1)}, f32[32,128]{1,0:T(8,128)S(1)}) custom-call(f32[3]{0:T(128)S(1)} %copy-done.2, f32[16,16]{1,0:T(8,128)S(1)} %pad_maximum_fusion.par_ref), custom_call_target="tpu_custom_call" | custom-call | flops 1000000 | bytes 1000000 | tf_op jit(solution)/shard_map/pallas_call | solution.py:608
  21.8 1.8 %collective-permute-done.2.refs_12_ = f32[96,128]{1,0:T(8,128)S(1)} collective-permute-done((f32[96,128]{1,0:T(8,128)S(1)}, f32[96,128]{1,0:T(8,128)S(1)}, u32[]{:S(2)}, u32[]{:S(2)}) %collective-permute-start.2) | collective-permute-done | bytes 49184 | tf_op jit(solution)/shard_map/ppermute | solution.py:587
  23.6 1.0 %shard_map.69 = (f32[32,128]{1,0:T(8,128)S(1)}, f32[8,32,128]{2,1,0:T(8,128)S(1)}) custom-call(f32[7,3,8,32,128]{4,3,2,1,0:T(8,128)S(1)} %get-tuple-element.15.refs_0_, f32[8,32,128]{2,1,0:T(8,128)S(1)} %get-tuple-element.16.refs_1_, f32[32,128]{1,0:T(8,128)S(1)} %get-tuple-element.17.refs_2_, f32[8,32,256]{2,1,0:T(8,128)S(1)} %get-tuple-element.18.refs_3_, ...), custom_call_target="tpu_custom_call" | custom-call | flops 1000000 | bytes 1000000 | tf_op jit(solution)/shard_map/pallas_call | solution.py:608
  24.6 0.1 collective-permute-start.6
  24.6 1.6 %collective-permute-start.5 = (f32[32,128]{1,0:T(8,128)S(1)}, f32[32,128]{1,0:T(8,128)S(1)}, u32[]{:S(2)}, u32[]{:S(2)}) collective-permute-start(f32[32,128]{1,0:T(8,128)S(1)} %get-tuple-element.24.refs_0_), channel_id=1, source_target_pairs={{0,16},{8,24},{16,0},{24,8},{1,17},{9,25},{17,1},{25,9},{2,18},{10... | collective-permute-start | bytes 49160 | tf_op jit(solution)/shard_map/ppermute | solution.py:587
  26.2 0.3 collective-permute-start.4
  26.5 1.4 %collective-permute-done.6.refs_3_ = f32[32,128]{1,0:T(8,128)S(1)} collective-permute-done((f32[32,128]{1,0:T(8,128)S(1)}, f32[32,128]{1,0:T(8,128)S(1)}, u32[]{:S(2)}, u32[]{:S(2)}) %collective-permute-start.6) | collective-permute-done | bytes 16416 | tf_op jit(solution)/shard_map/ppermute | solution.py:587
  27.9 0.6 %collective-permute-done.5.refs_2_ = f32[32,128]{1,0:T(8,128)S(1)} collective-permute-done((f32[32,128]{1,0:T(8,128)S(1)}, f32[32,128]{1,0:T(8,128)S(1)}, u32[]{:S(2)}, u32[]{:S(2)}) %collective-permute-start.5) | collective-permute-done | bytes 16416 | tf_op jit(solution)/shard_map/ppermute | solution.py:587
  28.5 1.0 %shard_map.70 = f32[32,8,128]{2,1,0:T(8,128)} custom-call(f32[32,8,128]{2,1,0:T(8,128)S(1)} %copy-done.1, f32[8,32,128]{2,1,0:T(8,128)S(1)} %get-tuple-element.22.doubled, f32[2,8,32,128]{3,2,1,0:T(8,128)S(1)} %get-tuple-element.23.ends, f32[32,128]{1,0:T(8,128)S(1)} %get-tuple-element.24.refs_0_, f32[32,128]{1,0:T(8,128)S(1)} %collective-permute-done.4.refs_1_, ...), custom_call_target="tpu_custom_call" | custom-call | flops 1000000 | bytes 1000000 | tf_op jit(solution)/shard_map/pallas_call | solution.py:608
  (9 shorter events, 0.0 us)
Async XLA Ops:
  3.1 0.9 %copy-start = (f32[32,8,128]{2,1,0:T(8,128)S(1)}, f32[32,8,128]{2,1,0:T(8,128)}, u32[]{:S(2)}) copy-start(f32[32,8,128]{2,1,0:T(8,128)} %density.3) | copy-start | bytes 393220
  4.0 0.7 %copy-start.2 = (f32[3]{0:T(128)S(1)}, f32[3]{0:T(128)}, u32[]{:S(2)}) copy-start(f32[3]{0:T(128)} %diffusion.5) | copy-start | bytes 40
  6.8 7.9 %collective-permute-start = (f32[96,128]{1,0:T(8,128)S(1)}, f32[96,128]{1,0:T(8,128)S(1)}, u32[]{:S(2)}, u32[]{:S(2)}) collective-permute-start(f32[96,128]{1,0:T(8,128)S(1)} %get-tuple-element.21.refs_0_.refs_7_), channel_id=1, source_target_pairs={{0,1},{1,0},{2,3},{3,2},{4,5},{5,4},{6,7},{7,6},{8,9},{9,8},{10,11... | collective-permute-start | bytes 147464 | tf_op jit(solution)/shard_map/ppermute | solution.py:587
  14.9 6.9 %collective-permute-start.3 = (f32[96,128]{1,0:T(8,128)S(1)}, f32[96,128]{1,0:T(8,128)S(1)}, u32[]{:S(2)}, u32[]{:S(2)}) collective-permute-start(f32[96,128]{1,0:T(8,128)S(1)} %shard_map.68.refs_10_), channel_id=1, source_target_pairs={{0,6},{1,7},{2,4},{3,5},{4,2},{5,3},{6,0},{7,1},{8,14},{9,15},{10,... | collective-permute-start | bytes 147464 | tf_op jit(solution)/shard_map/ppermute | solution.py:587
  18.6 5.0 %collective-permute-start.2 = (f32[96,128]{1,0:T(8,128)S(1)}, f32[96,128]{1,0:T(8,128)S(1)}, u32[]{:S(2)}, u32[]{:S(2)}) collective-permute-start(f32[96,128]{1,0:T(8,128)S(1)} %shard_map.68.refs_10_), channel_id=1, source_target_pairs={{0,4},{1,5},{2,6},{3,7},{4,0},{5,1},{6,2},{7,3},{8,12},{9,13},{10,... | collective-permute-start | bytes 147464 | tf_op jit(solution)/shard_map/ppermute | solution.py:587
  18.6 5.0 %collective-permute-start.1 = (f32[96,128]{1,0:T(8,128)S(1)}, f32[96,128]{1,0:T(8,128)S(1)}, u32[]{:S(2)}, u32[]{:S(2)}) collective-permute-start(f32[96,128]{1,0:T(8,128)S(1)} %shard_map.68.refs_10_), channel_id=1, source_target_pairs={{0,2},{1,3},{2,0},{3,1},{4,6},{5,7},{6,4},{7,5},{8,10},{9,11},{10,... | collective-permute-start | bytes 147464 | tf_op jit(solution)/shard_map/ppermute | solution.py:587
  23.6 4.9 %copy-start.1 = (f32[32,8,128]{2,1,0:T(8,128)S(1)}, f32[32,8,128]{2,1,0:T(8,128)}, u32[]{:S(2)}) copy-start(f32[32,8,128]{2,1,0:T(8,128)} %density.3) | copy-start | bytes 393220
  24.6 3.3 %collective-permute-start.6 = (f32[32,128]{1,0:T(8,128)S(1)}, f32[32,128]{1,0:T(8,128)S(1)}, u32[]{:S(2)}, u32[]{:S(2)}) collective-permute-start(f32[32,128]{1,0:T(8,128)S(1)} %get-tuple-element.24.refs_0_), channel_id=1, source_target_pairs={{0,24},{8,16},{16,8},{24,0},{1,25},{9,17},{17,9},{25,1},{2,26},{10... | collective-permute-start | bytes 49160 | tf_op jit(solution)/shard_map/ppermute | solution.py:587
  24.6 3.8 %collective-permute-start.5 = (f32[32,128]{1,0:T(8,128)S(1)}, f32[32,128]{1,0:T(8,128)S(1)}, u32[]{:S(2)}, u32[]{:S(2)}) collective-permute-start(f32[32,128]{1,0:T(8,128)S(1)} %get-tuple-element.24.refs_0_), channel_id=1, source_target_pairs={{0,16},{8,24},{16,0},{24,8},{1,17},{9,25},{17,1},{25,9},{2,18},{10... | collective-permute-start | bytes 49160 | tf_op jit(solution)/shard_map/ppermute | solution.py:587
  26.2 2.2 %collective-permute-start.4 = (f32[32,128]{1,0:T(8,128)S(1)}, f32[32,128]{1,0:T(8,128)S(1)}, u32[]{:S(2)}, u32[]{:S(2)}) collective-permute-start(f32[32,128]{1,0:T(8,128)S(1)} %get-tuple-element.24.refs_0_), channel_id=1, source_target_pairs={{0,8},{8,0},{16,24},{24,16},{1,9},{9,1},{17,25},{25,17},{2,10},{10... | collective-permute-start | bytes 49160 | tf_op jit(solution)/shard_map/ppermute | solution.py:587

commit v2 on v1

v2 whole, which is shorter than its diff:
```python
import functools

import jax
import jax.numpy as jnp
from jax import lax
from jax.experimental import pallas as pl
from jax.experimental.pallas import tpu as pltpu
from jax.sharding import PartitionSpec as P

HALF_LIMIT = 600.0
LANES = 128
ROWS = 8
VMEM_LIMIT = 48 * 1024 * 1024


def iota(shape, axis):
    return lax.broadcasted_iota(jnp.int32, shape, axis)


def coordinate(positions, line_total):
    return (2.0 * positions.astype(jnp.float32) + 1.0) / line_total - 1.0


def roll(values, shift, axis):
    return pltpu.roll(values, shift % values.shape[axis], axis)


def matmul(left, right):
    return lax.dot_general(
        left,
        right,
        (((1,), (1,)), ((), ())),
        precision=lax.Precision.HIGHEST,
        preferred_element_type=jnp.float32,
    )


def half_drift(left, right):
    return HALF_LIMIT * jnp.tanh(matmul(left, right))


SHARPNESS, CENTER, SLOPE, OFFSET, DIFFUSION, PREPARED = 0, 1, 4, 7, 8, 16


def component_of(maps):
    return iota((1, LANES), 1) // (2 * maps)


def first_term(maps):
    return (iota((1, LANES), 1) // maps) % 2 == 0


def bump(params, coord, axis):
    center = params[CENTER + axis : CENTER + axis + 1]
    return jnp.exp(-params[SHARPNESS : SHARPNESS + 1] * (coord - center) ** 2)


def slope(params, coord, axis):
    return coord * params[SLOPE + axis : SLOPE + axis + 1]


def x_factors(params, maps, size_x):
    coord = coordinate(iota((size_x, LANES), 0), size_x)
    return bump(params, coord, 0), jnp.where(first_term(maps), slope(params, coord, 0), 0.0)


def y_factors(params, maps, position, total_y):
    coord = coordinate(position, total_y)
    part = slope(params, coord, 1) + params[OFFSET : OFFSET + 1]
    return bump(params, coord, 1), jnp.where(
        first_term(maps), part, params[SLOPE + 2 : SLOPE + 3]
    )


def z_rows(params, maps, position, total_z):
    coord = coordinate(position, total_z)
    return bump(params, coord, 2) * jnp.where(first_term(maps), 1.0, coord)


def inner_z_rows(params, maps, z_start, size_z, total_z):
    return z_rows(params, maps, z_start + iota((size_z, LANES), 0), total_z)


def outer_z_rows(params, maps, z_start, size_z, total_z):
    row = iota((size_z, LANES), 0)
    return z_rows(
        params, maps, jnp.where(row == 0, z_start + size_z, z_start - 1), total_z
    )


def only(rows, maps, component):
    return jnp.where(component_of(maps) == component, rows, 0.0)


def y_rows(params, maps, position, total_y):
    coord = coordinate(position, total_y)
    part = slope(params, coord, 1) + params[OFFSET : OFFSET + 1]
    return bump(params, coord, 1) * jnp.where(first_term(maps), part, 1.0)


def xz_rows(params, maps, size_x, z_start, size_z, total_z):
    row = iota((2 * size_x, LANES), 0)
    x_coord = coordinate(row // 2, size_x)
    z_coord = coordinate(jnp.where(row % 2 == 0, z_start - 1, z_start + size_z), total_z)
    part = slope(params, x_coord, 0) + slope(params, z_coord, 2)
    both = bump(params, x_coord, 0) * bump(params, z_coord, 2)
    both = both * jnp.where(first_term(maps), 1.0, part)
    return jnp.concatenate(
        [both, jnp.zeros((LANES - 2 * size_x, LANES), jnp.float32)], axis=0
    )


def with_extra(main, row):
    return jnp.concatenate([main, jnp.broadcast_to(row, (ROWS, LANES))], axis=0)


def pack_planes(planes):
    lane = iota(planes[0].shape, 1)
    out = jnp.zeros(planes[0].shape, jnp.float32)
    for i, plane in enumerate(planes):
        out = jnp.where(lane // 2 == i, roll(plane, 2 * i + 1, 1), out)
    return out


def merge_coefs(low, high):
    inverse = 1.0 / (1.0 - low[3] * high[0])
    onward, back = low[1] * inverse, high[2] * inverse
    return (
        low[0] + onward * high[0] * low[2],
        onward * high[1],
        back * low[2],
        high[3] + back * low[3] * high[1],
    )


def merge_values(low, high, low_values, high_values):
    inverse = 1.0 / (1.0 - low[3] * high[0])
    return (
        low_values[0] + low[1] * inverse * (high_values[0] + high[0] * low_values[1]),
        high_values[1] + high[2] * inverse * (low_values[1] + low[3] * high_values[0]),
    )


def chain(coefs, values, below, above):
    count = len(coefs)
    held, slope = below, None
    befores, firsts = [], []
    for j in range(count):
        a_first, c_first, a_last, c_last = coefs[j]
        r_first, r_last = values[j]
        befores.append((held, slope))
        if slope is None:
            first, first_slope = r_first + a_first * held, c_first
            held, slope = r_last + a_last * held, c_last
        else:
            inverse = 1.0 / (1.0 - a_first * slope)
            first = (r_first + a_first * held) * inverse
            first_slope = c_first * inverse
            held, slope = (
                r_last + a_last * (held + slope * first),
                c_last + a_last * slope * first_slope,
            )
        firsts.append((first, first_slope))
    seen_above = [None] * count
    seen_below = [None] * count
    upper = above
    for j in reversed(range(count)):
        seen_above[j] = upper
        upper = firsts[j][0] + firsts[j][1] * upper
        held, slope = befores[j]
        seen_below[j] = held if slope is None else held + slope * upper
    return seen_below, seen_above


def solve_x(up, down, source, pivot):
    size = source.shape[0]
    half = size // 2
    low_g, low_c, high_g, high_c = {}, {}, {}, {}
    g = c = None
    for i in range(half):
        if i == 0:
            weight = 1.0 / pivot
            c = down[1] * weight
            g = source[0] * weight
        else:
            weight = 1.0 / (pivot - up[i - 1] * c)
            g = (source[i] + up[i - 1] * g) * weight
            c = down[i + 1] * weight
        low_g[i], low_c[i] = g, c
    for i in reversed(range(half, size)):
        if i == size - 1:
            weight = 1.0 / pivot
            c = up[i - 1] * weight
            g = source[i] * weight
        else:
            weight = 1.0 / (pivot - down[i + 1] * c)
            g = (source[i] + down[i + 1] * g) * weight
            c = up[i - 1] * weight
        high_g[i], high_c[i] = g, c
    out = [None] * size
    inverse = 1.0 / (1.0 - low_c[half - 1] * high_c[half])
    out[half - 1] = (low_g[half - 1] + low_c[half - 1] * high_g[half]) * inverse
    out[half] = high_g[half] + high_c[half] * out[half - 1]
    for i in reversed(range(half - 1)):
        out[i] = low_g[i] + low_c[i] * out[i + 1]
    for i in range(half + 1, size):
        out[i] = high_g[i] + high_c[i] * out[i - 1]
    return out


def start_kernel(
    extent_y,
    extent_z,
    density_hbm,
    diffusion_hbm,
    centers_hbm,
    sharpness_hbm,
    affine_hbm,
    offsets_hbm,
    message,
    base,
    from_below,
    from_above,
    drift_z_out,
    prepared,
    solved,
    drift_y_held,
    density,
    diffusion,
    centers,
    sharpness,
    affine,
    offsets,
    staged,
    semaphores,
):
    copies = [
        pltpu.make_async_copy(source, target, semaphores.at[number])
        for number, (source, target) in enumerate(
            [
                (diffusion_hbm, diffusion),
                (centers_hbm, centers),
                (sharpness_hbm, sharpness),
                (affine_hbm, affine),
                (offsets_hbm, offsets),
                (density_hbm, density),
            ]
        )
    ]
    for copy in copies:
        copy.start()
    size_x, size_y, size_z = density.shape
    total_y, total_z = size_y * extent_y, size_z * extent_z
    y_start = lax.axis_index("gy") * size_y
    z_start = lax.axis_index("gz") * size_z
    maps = centers.shape[1]
    for copy in copies[:-1]:
        copy.wait()

    staged[...] = jnp.zeros(staged.shape, jnp.float32)
    staged[0:1, :maps] = sharpness[...]
    staged[1:4, :maps] = centers[...]
    for c in range(3):
        staged[4 + 3 * c : 7 + 3 * c, :maps] = affine[c]
    staged[13:16, :maps] = offsets[...]
    rows = staged[...]
    width = maps
    while width < LANES:
        rows = rows + roll(rows, width, 1)
        width = 2 * width
    component = component_of(maps)
    rows = jnp.where(component < 3, rows, 0.0)

    def by_component(first, step):
        return jnp.where(
            component == 0,
            rows[first : first + 1],
            jnp.where(
                component == 1,
                rows[first + step : first + step + 1],
                rows[first + 2 * step : first + 2 * step + 1],
            ),
        )

    weights = [jnp.broadcast_to(diffusion[:, c : c + 1], (1, LANES)) for c in range(3)]
    params = jnp.concatenate(
        [rows[0:4]]
        + [by_component(4 + j, 3) for j in range(3)]
        + [by_component(13, 1)]
        + weights
        + [jnp.zeros((PREPARED - DIFFUSION - 3, LANES), jnp.float32)],
        axis=0,
    )
    prepared[...] = params
    d0, d1, d2 = weights

    x_bump, x_part = x_factors(params, maps, size_x)
    y_row = iota((size_y, LANES), 0)
    y_bump, y_part = y_factors(params, maps, y_start + y_row, total_y)
    out_bump, out_part = y_factors(
        params, maps, jnp.where(y_row == 0, y_start + size_y, y_start - 1), total_y
    )
    inner = inner_z_rows(params, maps, z_start, size_z, total_z)
    outer = outer_z_rows(params, maps, z_start, size_z, total_z)
    inner = [only(inner, maps, c) for c in range(3)]
    outer = only(outer, maps, 0)

    def rows_by_x(bumps, part):
        return jnp.concatenate(
            [(x_bump[i : i + 1] * bumps) * (x_part[i : i + 1] + part) for i in range(size_x)],
            axis=0,
        )

    right = jnp.concatenate([inner[0], outer, inner[1], inner[2]], axis=0)
    drifts = half_drift(rows_by_x(y_bump, y_part), right)
    out_drift = half_drift(rows_by_x(out_bump, out_part), inner[0])

    def block(number):
        columns = drifts[:, number * LANES : (number + 1) * LANES]
        return columns.reshape(size_x, size_y, LANES)

    drift_x, plane_drift, drift_y, drift_z = block(0), block(1), block(2), block(3)
    out_drift = out_drift.reshape(size_x, size_y, LANES)
    drift_y_held[...] = drift_y
    drift_z_out[...] = drift_z
    copies[-1].wait()
    rho = density[...]
    zero = jnp.zeros((1, size_y, LANES), jnp.float32)
    up, down = (d0 + drift_x) * rho, (d0 - drift_x) * rho
    total = (
        jnp.concatenate([zero, up[:-1]], axis=0)
        + jnp.concatenate([down[1:], zero], axis=0)
        - (2.0 * (d0 + d1 + d2)) * rho
    )
    sublane = iota((size_x, size_y, LANES), 1)
    lane = iota((size_x, size_y, LANES), 2)
    up, down = roll((d1 + drift_y) * rho, 1, 1), roll((d1 - drift_y) * rho, -1, 1)
    at_low, at_high = sublane == 0, sublane == size_y - 1
    row_source = jnp.where(at_low, up, jnp.where(at_high, down, 0.0))
    total = total + jnp.where(at_low, 0.0, up) + jnp.where(at_high, 0.0, down)
    up, down = roll((d2 + drift_z) * rho, 1, 2), roll((d2 - drift_z) * rho, -1, 2)
    at_low, at_high = lane == 0, lane == size_z - 1
    plane_source = jnp.where(at_low, up, jnp.where(at_high, down, 0.0))
    total = total + jnp.where(at_low, 0.0, up) + jnp.where(at_high, 0.0, down)

    source = jnp.concatenate([total, row_source, plane_source], axis=1)
    drift = jnp.concatenate([drift_x, out_drift, plane_drift], axis=1)
    answers = solve_x(d0 + drift, d0 - drift, source, 1.0 + 2.0 * d0)
    for i in range(size_x):
        solved[i] = answers[i][: 2 * size_y]
    planes = pack_planes([answer[2 * size_y :] for answer in answers])

    row = iota((1, LANES), 0)
    out_rows = []
    for position in (y_start - 1, y_start + size_y):
        bumps, part = y_factors(params, maps, row + position, total_y)
        out_rows.append((x_bump * bumps) * (x_part + part))
    ends = half_drift(jnp.concatenate(out_rows, axis=0), inner[1])
    position = y_start - 1 + iota((2 * ROWS, LANES), 0)
    extra = half_drift(
        y_rows(params, maps, position, total_y),
        only(xz_rows(params, maps, size_x, z_start, size_z, total_z), maps, 1),
    )
    line_drift = (
        [ends[:size_x]]
        + [drift_y_held[:, j, :] for j in range(size_y)]
        + [ends[size_x:]]
    )
    line_drift = [with_extra(line_drift[j], extra[j : j + 1]) for j in range(size_y + 2)]
    pivot = 1.0 + 2.0 * d1
    at_start = y_start == 0
    at_end = y_start + size_y == total_y
    g = a = c = None
    gs, as_, cs = [], [], []
    for j in range(size_y):
        value = with_extra(solved[:, j, :], planes[j : j + 1])
        lower = d1 + line_drift[j]
        upper = d1 - line_drift[j + 2]
        if j == 0:
            lower = jnp.where(at_start, 0.0, lower)
        if j == size_y - 1:
            upper = jnp.where(at_end, 0.0, upper)
        if j == 0:
            weight = 1.0 / pivot
            g, a = value * weight, lower * weight
        else:
            weight = 1.0 / (pivot - lower * c)
            g, a = (value + lower * g) * weight, lower * a * weight
        c = upper * weight
        gs.append(g)
        as_.append(a)
        cs.append(c)
    base[size_y - 1], from_below[size_y - 1], from_above[size_y - 1] = g, a, c
    r_last = g
    for j in reversed(range(size_y - 1)):
        g, a, c = gs[j] + cs[j] * g, as_[j] + cs[j] * a, cs[j] * c
        base[j], from_below[j], from_above[j] = g, a, c
    pushed_up = solved[:, size_y, :] / (d1 + line_drift[size_y][:size_x])
    pushed_down = solved[:, 2 * size_y - 1, :] / (d1 - line_drift[1][:size_x])
    blank = jnp.zeros((1, LANES), jnp.float32)
    width = size_x + ROWS
    message[:width] = g + with_extra(pushed_down, blank)
    message[width:] = r_last + with_extra(pushed_up, blank)


def line_coefs(params, maps, sizes, start, count, store):
    extent_y, extent_z, size_x, size_y, size_z = sizes
    total_y, total_z = size_y * extent_y, size_z * extent_z
    z_start = lax.axis_index("gz") * size_z
    d1 = params[DIFFUSION + 1 : DIFFUSION + 2]
    x_bump, x_part = x_factors(params, maps, size_x)
    inner = only(inner_z_rows(params, maps, z_start, size_z, total_z), maps, 1)
    planes = only(xz_rows(params, maps, size_x, z_start, size_z, total_z), maps, 1)
    whole = count == extent_y
    offsets = list(range(size_y)) if whole else list(range(-1, size_y + 1))
    left, left_extra = [], []
    for j in offsets:
        for b in range(count):
            position = iota((1, LANES), 0) + ((start + b) * size_y + j)
            bumps, part = y_factors(params, maps, position, total_y)
            left.append((x_bump * bumps) * (x_part + part))
        block = iota((max(count, ROWS), LANES), 0)
        left_extra.append(
            y_rows(params, maps, (start + block) * size_y + j, total_y)
        )
    depth = left_extra[0].shape[0]
    main = half_drift(jnp.concatenate(left, axis=0), inner)
    main = main.reshape(len(offsets), count, size_x, LANES)
    main = [main[j] for j in range(len(offsets))]
    extra = half_drift(jnp.concatenate(left_extra, axis=0), planes)
    extra = [extra[j * depth : (j + 1) * depth] for j in range(len(offsets))]
    if whole:
        main = (
            [jnp.concatenate([main[-1][:1], main[-1][:-1]], axis=0)]
            + main
            + [jnp.concatenate([main[0][1:], main[0][-1:]], axis=0)]
        )
        extra = [roll(extra[-1], 1, 0)] + extra + [roll(extra[0], -1, 0)]
    numbers = start + iota((depth, LANES), 0)
    pivot = 1.0 + 2.0 * d1
    at_start, at_end = numbers == 0, numbers == extent_y - 1

    def scan(drifts, starts, ends):
        a_first = c_first = a_last = c_last = None
        for j in range(size_y):
            lower, upper = d1 + drifts[j], d1 - drifts[j + 2]
            if j == 0:
                lower = starts(lower)
            if j == size_y - 1:
                upper = ends(upper)
            if j == 0:
                weight = 1.0 / pivot
                a_first, c_first = lower * weight, upper * weight
                a_last, c_last = a_first, c_first
            else:
                weight = 1.0 / (pivot - lower * c_last)
                step, c_last = lower * weight, upper * weight
                a_last = step * a_last
                a_first = a_first + c_first * a_last
                c_first = c_first * c_last
        return a_first, c_first, a_last, c_last

    def masked(values, number):
        return jnp.concatenate(
            [
                jnp.where(start + b == number, 0.0, values[b])[None]
                for b in range(count)
            ],
            axis=0,
        )

    main = scan(main, lambda v: masked(v, 0), lambda v: masked(v, extent_y - 1))
    extra = scan(
        extra,
        lambda v: jnp.where(at_start, 0.0, v),
        lambda v: jnp.where(at_end, 0.0, v),
    )
    for b in range(count):
        for q in range(4):
            store(b, q, with_extra(main[q][b], extra[q][b : b + 1]))


def near_kernel(sizes, maps, stride, radix, prepared, coefs):
    digit = lax.rem(lax.div(lax.axis_index("gy"), stride), radix)
    start = lax.div(lax.axis_index("gy"), stride) - digit

    def store(b, q, value):
        coefs[b, q] = value

    line_coefs(prepared[...], maps, sizes, start, radix, store)


def far_kernel(sizes, maps, levels, prepared, *outputs):
    held = {}

    def store(b, q, value):
        held[b, q] = value

    extent_y = sizes[0]
    line_coefs(prepared[...], maps, sizes, 0, extent_y, store)
    groups = [tuple(held[b, q] for q in range(4)) for b in range(extent_y)]
    for (_, radix), coefs in zip(levels, outputs):
        groups = [
            functools.reduce(merge_coefs, groups[g : g + radix])
            for g in range(0, len(groups), radix)
        ]
        for number, group in enumerate(groups):
            for q in range(4):
                coefs[number, q] = group[q]


def z_coef_kernel(sizes, maps, prepared, drift_z, steps, ends, pushes, packed):
    extent_y, extent_z, size_x, size_y, size_z = sizes
    total_y, total_z = size_y * extent_y, size_z * extent_z
    y_start = lax.axis_index("gy") * size_y
    z_start = lax.axis_index("gz") * size_z
    params = prepared[...]
    d2 = params[DIFFUSION + 2 : DIFFUSION + 3]
    scale = 1.0 / (1.0 + 2.0 * d2)
    lane = iota((size_y, LANES), 1)
    divisors = []
    for i in range(size_x):
        plane = drift_z[i]
        divisors.append(
            1.0 / jnp.where(lane == 0, d2 + roll(plane, 1, 1), d2 - roll(plane, -1, 1))
        )
    pushes[...] = pack_planes(divisors)
    x_bump, x_part = x_factors(params, maps, size_x)
    outer = only(outer_z_rows(params, maps, z_start, size_z, total_z), maps, 2)
    rows = []
    for j in range(size_y):
        position = iota((1, LANES), 0) + (y_start + j)
        bumps, part = y_factors(params, maps, position, total_y)
        rows.append((x_bump * bumps) * (x_part + part))
    outer = half_drift(jnp.concatenate(rows, axis=0), outer)
    inner = jnp.concatenate([drift_z[:, j, :] for j in range(size_y)], axis=0)
    lane = iota(inner.shape, 1)
    low, high = lane == 0, lane == size_z - 1
    before = jnp.where(low, roll(outer, 1, 1), roll(inner, 1, 1))
    after = jnp.where(high, roll(outer, -1, 1), roll(inner, -1, 1))
    below = jnp.where(low & (z_start == 0), 0.0, (d2 + before) * scale)
    above = jnp.where(high & (z_start + size_z == total_z), 0.0, (d2 - after) * scale)
    shape = (size_y, size_x, LANES)
    stride, level = 1, 0
    while stride < size_z:
        low, high = lane < stride, lane >= size_z - stride
        low_a = jnp.where(low, 1.0, roll(below, stride, 1))
        low_c = jnp.where(low, 0.0, roll(above, stride, 1))
        high_a = jnp.where(high, 0.0, roll(below, -stride, 1))
        high_c = jnp.where(high, 1.0, roll(above, -stride, 1))
        inverse = 1.0 / (1.0 - below * low_c - above * high_a)
        below, above = below * inverse, above * inverse
        factor = scale if level == 0 else 1.0
        steps[level, 0] = (inverse * factor).reshape(shape)
        steps[level, 1] = jnp.where(low, 0.0, below * factor).reshape(shape)
        steps[level, 2] = jnp.where(high, 0.0, above * factor).reshape(shape)
        below, above = below * low_a, above * high_c
        stride, level = stride * 2, level + 1
    below, above = below.reshape(shape), above.reshape(shape)
    ends[0] = below
    ends[1] = above
    packed[...] = pack_ends([below[j] for j in range(size_y)], 1, size_y) + pack_ends(
        [above[j] for j in range(size_y)], 2, size_y
    )


def pack_ends(rows, slot, size_y):
    shape = rows[0].shape
    lane = iota(shape, 1)
    out = jnp.zeros(shape, jnp.float32)
    for j in range(size_y):
        first = slot * 2 * size_y + j
        last = first + size_y
        out = jnp.where(lane == first, roll(rows[j], first, 1), out)
        out = jnp.where(lane == last, roll(rows[j], last - (LANES - 1), 1), out)
    return out


def gather_members(refs, own, count):
    held = [ref[...] for ref in refs]
    return [
        functools.reduce(
            lambda acc, s: jnp.where((own ^ s) == j, held[s], acc), range(1, count), held[0]
        )
        for j in range(count)
    ]


def split_message(message):
    width = message.shape[0] // 2
    return message[:width], message[width:]


def merge_kernel(stride, radix, local, coefs, *refs):
    received, message = refs[:radix], refs[radix]
    digit = lax.rem(lax.div(lax.axis_index("gy"), stride), radix)
    first = 0 if local else lax.div(lax.axis_index("gy"), stride) - digit
    values = [split_message(m) for m in gather_members(received, digit, radix)]
    group = [tuple(coefs[first + j, q] for q in range(4)) for j in range(radix)]
    merged, total = group[0], values[0]
    for j in range(1, radix):
        total = merge_values(merged, group[j], total, values[j])
        merged = merge_coefs(merged, group[j])
    message[...] = jnp.concatenate(total, axis=0)


def middle_kernel(levels, *refs):
    refs = list(refs)
    steps, pushes, packed, base, from_below, from_above = refs[:6]
    refs = refs[6:]
    inputs = []
    for stride, radix in levels:
        inputs.append((refs[0], refs[1 : 1 + radix]))
        refs = refs[1 + radix :]
    message, doubled, seen, turned = refs
    size_y, width = base.shape[:2]
    size_x = width - ROWS
    below = above = jnp.zeros((width, LANES), jnp.float32)
    for number in reversed(range(len(levels))):
        (stride, radix), (coefs, received) = levels[number], inputs[number]
        digit = lax.rem(lax.div(lax.axis_index("gy"), stride), radix)
        first = 0 if number == 0 else lax.div(lax.axis_index("gy"), stride) - digit
        values = [split_message(m) for m in gather_members(received, digit, radix)]
        group = [tuple(coefs[first + j, q] for q in range(4)) for j in range(radix)]
        lows, highs = chain(group, values, below, above)
        for j in range(radix):
            seen[j, 0] = lows[j]
            seen[j, 1] = highs[j]
        below, above = seen[digit, 0], seen[digit, 1]
    inner, outer = [], []
    for j in range(size_y):
        value = base[j] + from_below[j] * below + from_above[j] * above
        inner.append(value[:size_x])
        outer.append(value[size_x : size_x + 1])
    turned[...] = jnp.transpose(jnp.concatenate(outer, axis=0) * pushes[...])
    values = jnp.stack(inner)
    stride, level = 1, 0
    while stride < LANES:
        values = (
            steps[level, 0] * values
            + steps[level, 1] * roll(values, stride, 2)
            + steps[level, 2] * roll(values, -stride, 2)
        )
        stride, level = stride * 2, level + 1
    doubled[...] = values
    ends = pack_ends([values[j] for j in range(size_y)], 0, size_y) + packed[...]
    message[...] = ends
    message[:, :size_y] = ends[:, :size_y] + turned[pl.ds(0, size_x, stride=2), :]
    message[:, size_y : 2 * size_y] = (
        ends[:, size_y : 2 * size_y] + turned[pl.ds(1, size_x, stride=2), :]
    )


def merge_z(low, high):
    inverse = 1.0 / (1.0 - low[5] * high[2])
    onward, back = low[4] * inverse, high[3] * inverse
    return (
        low[0] + onward * (high[0] + high[2] * low[1]),
        high[1] + back * (low[1] + low[5] * high[0]),
        low[2] + onward * high[2] * low[3],
        back * low[3],
        onward * high[4],
        high[5] + back * low[5] * high[4],
    )


def unpack_ends(message, size_y):
    return tuple(message if s == 0 else roll(message, -s * size_y, 1) for s in range(6))


def merge_z_kernel(stride, radix, size_y, *refs):
    received, message = refs[:radix], refs[radix]
    digit = lax.rem(lax.div(lax.axis_index("gz"), stride), radix)
    members = [unpack_ends(m, size_y) for m in gather_members(received, digit, radix)]
    total = functools.reduce(merge_z, members)
    lane = iota(total[0].shape, 1)
    out = jnp.zeros(total[0].shape, jnp.float32)
    for s in range(6):
        shifted = total[s] if s == 0 else roll(total[s], s * size_y, 1)
        out = jnp.where(lane // size_y == s, shifted, out)
    message[...] = out


def end_kernel(levels, density, doubled, ends, *refs):
    refs = list(refs)
    inputs = []
    for stride, radix in levels:
        inputs.append(refs[:radix])
        refs = refs[radix:]
    out, seen = refs
    size_x, size_y, _ = density.shape
    below = above = jnp.zeros((size_x, LANES), jnp.float32)
    for (stride, radix), received in zip(reversed(levels), reversed(inputs)):
        digit = lax.rem(lax.div(lax.axis_index("gz"), stride), radix)
        members = [unpack_ends(m, size_y) for m in gather_members(received, digit, radix)]
        lows, highs = chain(
            [(m[2], m[4], m[3], m[5]) for m in members],
            [(m[0], m[1]) for m in members],
            below,
            above,
        )
        for j in range(radix):
            seen[j, 0] = lows[j]
            seen[j, 1] = highs[j]
        below, above = seen[digit, 0], seen[digit, 1]
    for j in range(size_y):
        out[:, j, :] = (
            density[:, j, :]
            + doubled[j]
            + ends[0, j] * below[:, j : j + 1]
            + ends[1, j] * above[:, j : j + 1]
        )


def radices(extent):
    rounds, stride = [], 1
    while stride < extent:
        left = extent // stride
        power = left.bit_length() - 1
        radix = 4 if left % 4 == 0 and power % 2 == 0 else 2
        rounds.append((stride, radix))
        stride *= radix
    return rounds


def exchange(message, axis, stride, radix):
    devices = range(lax.axis_size(axis))
    return [message] + [
        lax.ppermute(message, axis, [(i, i ^ (s * stride)) for i in devices])
        for s in range(1, radix)
    ]


def body(density, diffusion, centers, sharpness, affine, offsets):
    size_x, size_y, size_z = density.shape
    extent_y, extent_z = lax.axis_size("gy"), lax.axis_size("gz")
    sizes = (extent_y, extent_z, size_x, size_y, size_z)
    maps = centers.shape[0]
    width = size_x + ROWS
    wide = (size_y, width, LANES)
    narrow = (size_y, size_x, LANES)
    float32 = jnp.float32
    y_levels, z_levels = radices(extent_y), radices(extent_z)

    def shape(*dims):
        return jax.ShapeDtypeStruct(dims, float32)

    vmem = pl.BlockSpec(memory_space=pltpu.VMEM)
    hbm = pl.BlockSpec(memory_space=pltpu.HBM)

    def call(kernel, inputs, outputs, in_specs=None, scratch=(), flops=10**6):
        return pl.pallas_call(
            kernel,
            out_shape=outputs,
            in_specs=in_specs or [vmem] * len(inputs),
            out_specs=jax.tree.map(lambda _: vmem, outputs),
            scratch_shapes=list(scratch),
            compiler_params=pltpu.CompilerParams(vmem_limit_bytes=VMEM_LIMIT),
            cost_estimate=pl.CostEstimate(flops=flops, bytes_accessed=10**6, transcendentals=0),
        )(*inputs)

    raw = (
        density,
        diffusion.reshape(1, 3),
        centers.T,
        sharpness.reshape(1, maps),
        affine.transpose(1, 2, 0),
        offsets.T,
    )
    message, base, from_below, from_above, drift_z, prepared = call(
        functools.partial(start_kernel, extent_y, extent_z),
        raw,
        (
            shape(2 * width, LANES),
            shape(*wide),
            shape(*wide),
            shape(*wide),
            shape(size_x, size_y, LANES),
            shape(PREPARED, LANES),
        ),
        [hbm] * len(raw),
        [
            pltpu.VMEM((size_x, 2 * size_y, LANES), float32),
            pltpu.VMEM((size_x, size_y, LANES), float32),
        ]
        + [pltpu.VMEM(array.shape, float32) for array in raw]
        + [pltpu.VMEM((PREPARED, LANES), float32), pltpu.SemaphoreType.DMA((len(raw),))],
    )
    stride, radix = y_levels[0]
    near = call(
        functools.partial(near_kernel, sizes, maps, stride, radix),
        [prepared],
        shape(radix, 4, width, LANES),
    )
    far, count = [], extent_y
    for _, radix in y_levels[:-1]:
        count = count // radix
        far.append(shape(count, 4, width, LANES))
    if far:
        far = call(functools.partial(far_kernel, sizes, maps, y_levels[:-1]), [prepared], far)
    coefs = [near] + list(far)
    doublings = size_z.bit_length() - 1
    steps, ends, pushes, packed = call(
        functools.partial(z_coef_kernel, sizes, maps),
        (prepared, drift_z),
        (
            shape(doublings, 3, *narrow),
            shape(2, *narrow),
            shape(size_y, LANES),
            shape(size_x, LANES),
        ),
    )
    line_inputs = []
    for number, (stride, radix) in enumerate(y_levels):
        received = exchange(message, "gy", stride, radix)
        line_inputs += [coefs[number]] + received
        if number + 1 < len(y_levels):
            message = call(
                functools.partial(merge_kernel, stride, radix, number == 0),
                [coefs[number]] + received,
                shape(2 * width, LANES),
            )
    message, doubled = call(
        functools.partial(middle_kernel, y_levels),
        [steps, pushes, packed, base, from_below, from_above] + line_inputs,
        (shape(size_x, LANES), shape(*narrow)),
        scratch=[
            pltpu.VMEM((4, 2, width, LANES), float32),
            pltpu.VMEM((LANES, size_y), float32),
        ],
    )
    end_inputs = []
    for number, (stride, radix) in enumerate(z_levels):
        received = exchange(message, "gz", stride, radix)
        end_inputs += received
        if number + 1 < len(z_levels):
            message = call(
                functools.partial(merge_z_kernel, stride, radix, size_y),
                received,
                shape(size_x, LANES),
            )
    return call(
        functools.partial(end_kernel, z_levels),
        [density, doubled, ends] + end_inputs,
        shape(size_x, size_y, size_z),
        scratch=[pltpu.VMEM((4, 2, size_x, LANES), float32)],
    )


def solution(mesh):
    placed = (P(None, "gy", "gz"), P(), P(), P(), P(), P())
    return jax.shard_map(
        body, mesh=mesh, in_specs=placed, out_specs=P(None, "gy", "gz"), check_vma=False
    )
```

time: 29.7 us -> 26.6 us (0.90)
  Pallas kernels: 11.6 us -> 7.83 us
  waiting for transfers between devices: 3.76 us -> 4.4 us
  starting transfers between devices: 9.38 us -> 9.76 us
  local copies, waits for them, and re-layouts: 4.59 us -> 4.27 us
    pallas_call x7, Pallas kernels: 11.6 us -> 7.83 us  [call(): pl.pallas_call(kernel, out_shape=outputs, in_specs=in_specs or [vmem] * l...]
    unnamed x8 -> x14, local copies, waits for them, and re-layouts: 3.08 us -> 4.27 us
    reshape x2 -> x0, local copies, waits for them, and re-layouts: 0.78 us -> none  [body(): affine.reshape(maps, 9)]
    broadcast_in_dim x1 -> x0, local copies, waits for them, and re-layouts: 0.73 us -> none  [body(): sharpness[:, None]]
    ppermute x7, waiting for transfers between devices: 3.76 us -> 4.4 us  [exchange(): lax.ppermute(message, axis, [(i, i ^ s * stride) for i in devices])]
    ppermute x7, starting transfers between devices: 9.38 us -> 9.76 us  [exchange(): lax.ppermute(message, axis, [(i, i ^ s * stride) for i in devices])]
  transfers between devices with their start and end apart: 7 -> 7, of which waited for: 3 -> 4; matrix products, arithmetic and copies ran while one was open for 0% -> 0% of each run, Pallas kernels for 25% -> 14%
where the time goes in v2:
time: 26.6 us; the launch traced here: 26.3 us
  starting transfers between devices  9.76 us (37%)
  Pallas kernels  7.83 us (29%)
  waiting for transfers between devices  4.4 us (17%)
  local copies, waits for them, and re-layouts  4.27 us (16%)
    ppermute x7, starting transfers between devices, exchange(): lax.ppermute(message, axis, [(i, i ^ s * stride) for i in devices])  9.76 us
    pallas_call x7, Pallas kernels, call(): pl.pallas_call(kernel, out_shape=outputs, in_specs=in_specs or [vmem] * l...  7.83 us
    ppermute x7, waiting for transfers between devices, exchange(): lax.ppermute(message, axis, [(i, i ^ s * stride) for i in devices])  4.4 us
    unnamed x14, local copies, waits for them, and re-layouts  4.27 us
  transfers between devices with their start and end apart: 7, of which 4 were waited for; matrix products, arithmetic and copies ran while one was open for 0% of the time, Pallas kernels for 14%

profile of v2, /device:TPU:0, one launch (start us, length us, event | category | flops | bytes accessed | tf_op | source)
XLA Modules:
  0.0 26.3 jit_solution(8238644768622597643)
XLA Ops:
  0.0 0.9 %copy-done = f32[32,8,128]{2,1,0:T(8,128)S(1)} copy-done((f32[32,8,128]{2,1,0:T(8,128)S(1)}, f32[32,8,128]{2,1,0:T(8,128)}, u32[]{:S(2)}) %copy-start) | copy-done | bytes 131096
  0.9 0.7 %copy-done.2 = f32[16,3,3]{0,2,1:T(4,128)S(1)} copy-done((f32[16,3,3]{0,2,1:T(4,128)S(1)}, f32[16,3,3]{0,2,1:T(4,128)}, u32[]{:S(2)}) %copy-start.2) | copy-done | bytes 600
  1.6 0.7 %copy-done.3 = f32[16,3]{0,1:T(4,128)S(1)} copy-done((f32[16,3]{0,1:T(4,128)S(1)}, f32[16,3]{0,1:T(4,128)}, u32[]{:S(2)}) %copy-start.3) | copy-done | bytes 216
  2.3 0.7 %copy-done.4 = f32[16,3]{0,1:T(4,128)S(1)} copy-done((f32[16,3]{0,1:T(4,128)S(1)}, f32[16,3]{0,1:T(4,128)}, u32[]{:S(2)}) %copy-start.4) | copy-done | bytes 216
  3.0 0.7 %copy-done.5 = f32[3]{0:T(128)S(1)} copy-done((f32[3]{0:T(128)S(1)}, f32[3]{0:T(128)}, u32[]{:S(2)}) %copy-start.5) | copy-done | bytes 36
  3.6 0.7 %copy-done.6 = f32[16]{0:T(128)S(1)} copy-done((f32[16]{0:T(128)S(1)}, f32[16]{0:T(128)}, u32[]{:S(2)}) %copy-start.6) | copy-done | bytes 88
  4.3 2.0 %shard_map.64 = (f32[80,128]{1,0:T(8,128)S(1)}, f32[8,40,128]{2,1,0:T(8,128)S(1)}, f32[8,40,128]{2,1,0:T(8,128)S(1)}, f32[8,40,128]{2,1,0:T(8,128)S(1)}, f32[32,...) custom-call(f32[32,8,128]{2,1,0:T(8,128)S(1)} %copy-done, f32[1,3]{1,0:T(1,128)S(1)} %bitcast.8, f32[3,16]{1,0:T(4,128)S(1)} %bitcast.6, ...), custom_call_target="tpu_custom_call" | custom-call | flops 1000000 | bytes 1000000 | tf_op jit(solution)/shard_map/pallas_call | solution.py:752
  6.3 3.0 %collective-permute-start = (f32[80,128]{1,0:T(8,128)S(1)}, f32[80,128]{1,0:T(8,128)S(1)}, u32[]{:S(2)}, u32[]{:S(2)}) collective-permute-start(f32[80,128]{1,0:T(8,128)S(1)} %get-tuple-element.25.refs_0_.refs_7_), channel_id=1, source_target_pairs={{0,1},{1,0},{2,3},{3,2},{4,5},{5,4},{6,7},{7,6},{8,9},{9,8},{10,11... | collective-permute-start | bytes 122888 | tf_op jit(solution)/shard_map/ppermute | solution.py:729
  9.3 0.6 %shard_map.66.coefs.refs_6_ = f32[2,4,40,128]{3,2,1,0:T(8,128)S(1)} custom-call(f32[16,128]{1,0:T(8,128)S(1)} %get-tuple-element.17.prepared), custom_call_target="tpu_custom_call" | custom-call | flops 1000000 | bytes 1000000 | tf_op jit(solution)/shard_map/pallas_call | solution.py:752
  9.9 1.4 %collective-permute-done.refs_1_.refs_8_ = f32[80,128]{1,0:T(8,128)S(1)} collective-permute-done((f32[80,128]{1,0:T(8,128)S(1)}, f32[80,128]{1,0:T(8,128)S(1)}, u32[]{:S(2)}, u32[]{:S(2)}) %collective-permute-start) | collective-permute-done | bytes 40992 | tf_op jit(solution)/shard_map/ppermute | solution.py:729
  11.3 4.2 %collective-permute-start.3 = (f32[80,128]{1,0:T(8,128)S(1)}, f32[80,128]{1,0:T(8,128)S(1)}, u32[]{:S(2)}, u32[]{:S(2)}) collective-permute-start(f32[80,128]{1,0:T(8,128)S(1)} %shard_map.68.refs_10_), channel_id=1, source_target_pairs={{0,6},{1,7},{2,4},{3,5},{4,2},{5,3},{6,0},{7,1},{8,14},{9,15},{10,... | collective-permute-start | bytes 122888 | tf_op jit(solution)/shard_map/ppermute | solution.py:729
  15.5 0.0 collective-permute-start.2
  15.5 0.6 %collective-permute-start.1 = (f32[80,128]{1,0:T(8,128)S(1)}, f32[80,128]{1,0:T(8,128)S(1)}, u32[]{:S(2)}, u32[]{:S(2)}) collective-permute-start(f32[80,128]{1,0:T(8,128)S(1)} %shard_map.68.refs_10_), channel_id=1, source_target_pairs={{0,2},{1,3},{2,0},{3,1},{4,6},{5,7},{6,4},{7,5},{8,10},{9,11},{10,... | collective-permute-start | bytes 122888 | tf_op jit(solution)/shard_map/ppermute | solution.py:729
  16.2 1.6 %shard_map.67.refs_9_ = f32[4,4,40,128]{3,2,1,0:T(8,128)S(1)} custom-call(f32[16,128]{1,0:T(8,128)S(1)} %get-tuple-element.17.prepared), custom_call_target="tpu_custom_call" | custom-call | flops 1000000 | bytes 1000000 | tf_op jit(solution)/shard_map/pallas_call | solution.py:752
  17.8 1.6 %shard_map.65 = (f32[7,3,8,32,128]{4,3,2,1,0:T(8,128)S(1)}, f32[2,8,32,128]{3,2,1,0:T(8,128)S(1)}, f32[8,128]{1,0:T(8,128)S(1)}, f32[32,128]{1,0:T(8,128)S(1)}) custom-call(f32[16,128]{1,0:T(8,128)S(1)} %get-tuple-element.17.prepared, f32[32,8,128]{2,1,0:T(8,128)S(1)} %get-tuple-element.18.drift_z), custom_call_target="tpu_custom_call" | custom-call | flops 1000000 | bytes 1000000 | tf_op jit(solution)/shard_map/pallas_call | solution.py:752
  19.3 0.0 collective-permute-done.3.refs_13_
  19.3 1.1 %collective-permute-done.2.refs_12_ = f32[80,128]{1,0:T(8,128)S(1)} collective-permute-done((f32[80,128]{1,0:T(8,128)S(1)}, f32[80,128]{1,0:T(8,128)S(1)}, u32[]{:S(2)}, u32[]{:S(2)}) %collective-permute-start.2) | collective-permute-done | bytes 40992 | tf_op jit(solution)/shard_map/ppermute | solution.py:729
  20.4 1.0 %shard_map.69 = (f32[32,128]{1,0:T(8,128)S(1)}, f32[8,32,128]{2,1,0:T(8,128)S(1)}) custom-call(f32[7,3,8,32,128]{4,3,2,1,0:T(8,128)S(1)} %get-tuple-element.19.refs_0_, f32[8,128]{1,0:T(8,128)S(1)} %get-tuple-element.20.refs_1_, f32[32,128]{1,0:T(8,128)S(1)} %get-tuple-element.21.refs_2_, f32[8,40,128]{2,1,0:T(8,128)S(1)} %get-tuple-element.22.refs_3_, ...), custom_call_target="tpu_custom_call" | custom-call | flops 1000000 | bytes 1000000 | tf_op jit(solution)/shard_map/pallas_call | solution.py:752
  21.4 0.1 collective-permute-start.6
  21.5 1.6 %collective-permute-start.5 = (f32[32,128]{1,0:T(8,128)S(1)}, f32[32,128]{1,0:T(8,128)S(1)}, u32[]{:S(2)}, u32[]{:S(2)}) collective-permute-start(f32[32,128]{1,0:T(8,128)S(1)} %get-tuple-element.28.refs_0_), channel_id=1, source_target_pairs={{0,16},{8,24},{16,0},{24,8},{1,17},{9,25},{17,1},{25,9},{2,18},{10... | collective-permute-start | bytes 49160 | tf_op jit(solution)/shard_map/ppermute | solution.py:729
  23.1 0.3 collective-permute-start.4
  23.4 1.4 %collective-permute-done.6.refs_3_ = f32[32,128]{1,0:T(8,128)S(1)} collective-permute-done((f32[32,128]{1,0:T(8,128)S(1)}, f32[32,128]{1,0:T(8,128)S(1)}, u32[]{:S(2)}, u32[]{:S(2)}) %collective-permute-start.6) | collective-permute-done | bytes 16416 | tf_op jit(solution)/shard_map/ppermute | solution.py:729
  24.8 0.6 %collective-permute-done.5.refs_2_ = f32[32,128]{1,0:T(8,128)S(1)} collective-permute-done((f32[32,128]{1,0:T(8,128)S(1)}, f32[32,128]{1,0:T(8,128)S(1)}, u32[]{:S(2)}, u32[]{:S(2)}) %collective-permute-start.5) | collective-permute-done | bytes 16416 | tf_op jit(solution)/shard_map/ppermute | solution.py:729
  25.3 1.0 %shard_map.70 = f32[32,8,128]{2,1,0:T(8,128)} custom-call(f32[32,8,128]{2,1,0:T(8,128)S(1)} %copy-done.1, f32[8,32,128]{2,1,0:T(8,128)S(1)} %get-tuple-element.26.doubled, f32[2,8,32,128]{3,2,1,0:T(8,128)S(1)} %get-tuple-element.27.ends, f32[32,128]{1,0:T(8,128)S(1)} %get-tuple-element.28.refs_0_, f32[32,128]{1,0:T(8,128)S(1)} %collective-permute-done.4.refs_1_, ...), custom_call_target="tpu_custom_call" | custom-call | flops 1000000 | bytes 1000000 | tf_op jit(solution)/shard_map/pallas_call | solution.py:752
  (11 shorter events, 0.0 us)
Async XLA Ops:
  0.0 0.9 %copy-start = (f32[32,8,128]{2,1,0:T(8,128)S(1)}, f32[32,8,128]{2,1,0:T(8,128)}, u32[]{:S(2)}) copy-start(f32[32,8,128]{2,1,0:T(8,128)} %density.1) | copy-start | bytes 393220
  0.9 0.7 %copy-start.2 = (f32[16,3,3]{0,2,1:T(4,128)S(1)}, f32[16,3,3]{0,2,1:T(4,128)}, u32[]{:S(2)}) copy-start(f32[16,3,3]{0,2,1:T(4,128)} %param.10) | copy-start | bytes 1732
  1.6 0.7 %copy-start.3 = (f32[16,3]{0,1:T(4,128)S(1)}, f32[16,3]{0,1:T(4,128)}, u32[]{:S(2)}) copy-start(f32[16,3]{0,1:T(4,128)} %param.8) | copy-start | bytes 580
  2.3 0.7 %copy-start.4 = (f32[16,3]{0,1:T(4,128)S(1)}, f32[16,3]{0,1:T(4,128)}, u32[]{:S(2)}) copy-start(f32[16,3]{0,1:T(4,128)} %param.11) | copy-start | bytes 580
  3.0 0.7 %copy-start.5 = (f32[3]{0:T(128)S(1)}, f32[3]{0:T(128)}, u32[]{:S(2)}) copy-start(f32[3]{0:T(128)} %param.7) | copy-start | bytes 40
  3.6 0.7 %copy-start.6 = (f32[16]{0:T(128)S(1)}, f32[16]{0:T(128)}, u32[]{:S(2)}) copy-start(f32[16]{0:T(128)} %param.9) | copy-start | bytes 196
  4.3 21.0 %copy-start.1 = (f32[32,8,128]{2,1,0:T(8,128)S(1)}, f32[32,8,128]{2,1,0:T(8,128)}, u32[]{:S(2)}) copy-start(f32[32,8,128]{2,1,0:T(8,128)} %density.1) | copy-start | bytes 393220
  6.3 5.0 %collective-permute-start = (f32[80,128]{1,0:T(8,128)S(1)}, f32[80,128]{1,0:T(8,128)S(1)}, u32[]{:S(2)}, u32[]{:S(2)}) collective-permute-start(f32[80,128]{1,0:T(8,128)S(1)} %get-tuple-element.25.refs_0_.refs_7_), channel_id=1, source_target_pairs={{0,1},{1,0},{2,3},{3,2},{4,5},{5,4},{6,7},{7,6},{8,9},{9,8},{10,11... | collective-permute-start | bytes 122888 | tf_op jit(solution)/shard_map/ppermute | solution.py:729
  11.3 8.0 %collective-permute-start.3 = (f32[80,128]{1,0:T(8,128)S(1)}, f32[80,128]{1,0:T(8,128)S(1)}, u32[]{:S(2)}, u32[]{:S(2)}) collective-permute-start(f32[80,128]{1,0:T(8,128)S(1)} %shard_map.68.refs_10_), channel_id=1, source_target_pairs={{0,6},{1,7},{2,4},{3,5},{4,2},{5,3},{6,0},{7,1},{8,14},{9,15},{10,... | collective-permute-start | bytes 122888 | tf_op jit(solution)/shard_map/ppermute | solution.py:729
  15.5 4.9 %collective-permute-start.2 = (f32[80,128]{1,0:T(8,128)S(1)}, f32[80,128]{1,0:T(8,128)S(1)}, u32[]{:S(2)}, u32[]{:S(2)}) collective-permute-start(f32[80,128]{1,0:T(8,128)S(1)} %shard_map.68.refs_10_), channel_id=1, source_target_pairs={{0,4},{1,5},{2,6},{3,7},{4,0},{5,1},{6,2},{7,3},{8,12},{9,13},{10,... | collective-permute-start | bytes 122888 | tf_op jit(solution)/shard_map/ppermute | solution.py:729
  15.5 4.9 %collective-permute-start.1 = (f32[80,128]{1,0:T(8,128)S(1)}, f32[80,128]{1,0:T(8,128)S(1)}, u32[]{:S(2)}, u32[]{:S(2)}) collective-permute-start(f32[80,128]{1,0:T(8,128)S(1)} %shard_map.68.refs_10_), channel_id=1, source_target_pairs={{0,2},{1,3},{2,0},{3,1},{4,6},{5,7},{6,4},{7,5},{8,10},{9,11},{10,... | collective-permute-start | bytes 122888 | tf_op jit(solution)/shard_map/ppermute | solution.py:729
  21.4 3.3 %collective-permute-start.6 = (f32[32,128]{1,0:T(8,128)S(1)}, f32[32,128]{1,0:T(8,128)S(1)}, u32[]{:S(2)}, u32[]{:S(2)}) collective-permute-start(f32[32,128]{1,0:T(8,128)S(1)} %get-tuple-element.28.refs_0_), channel_id=1, source_target_pairs={{0,24},{8,16},{16,8},{24,0},{1,25},{9,17},{17,9},{25,1},{2,26},{10... | collective-permute-start | bytes 49160 | tf_op jit(solution)/shard_map/ppermute | solution.py:729
  21.5 3.8 %collective-permute-start.5 = (f32[32,128]{1,0:T(8,128)S(1)}, f32[32,128]{1,0:T(8,128)S(1)}, u32[]{:S(2)}, u32[]{:S(2)}) collective-permute-start(f32[32,128]{1,0:T(8,128)S(1)} %get-tuple-element.28.refs_0_), channel_id=1, source_target_pairs={{0,16},{8,24},{16,0},{24,8},{1,17},{9,25},{17,1},{25,9},{2,18},{10... | collective-permute-start | bytes 49160 | tf_op jit(solution)/shard_map/ppermute | solution.py:729
  23.1 2.2 %collective-permute-start.4 = (f32[32,128]{1,0:T(8,128)S(1)}, f32[32,128]{1,0:T(8,128)S(1)}, u32[]{:S(2)}, u32[]{:S(2)}) collective-permute-start(f32[32,128]{1,0:T(8,128)S(1)} %get-tuple-element.28.refs_0_), channel_id=1, source_target_pairs={{0,8},{8,0},{16,24},{24,16},{1,9},{9,1},{17,25},{25,17},{2,10},{10... | collective-permute-start | bytes 49160 | tf_op jit(solution)/shard_map/ppermute | solution.py:729

commit v3 on v2

--- a/solution.py
+++ b/solution.py
@@ -767,6 +767,7 @@
         affine.transpose(1, 2, 0),
         offsets.T,
     )
+    raw = tuple(pltpu.with_memory_space_constraint(array, pltpu.HBM) for array in raw)
     message, base, from_below, from_above, drift_z, prepared = call(
         functools.partial(start_kernel, extent_y, extent_z),
         raw,

time: 26.6 us -> 22.8 us (0.86)
  local copies, waits for them, and re-layouts: 4.27 us -> 0.01 us
  Pallas kernels: 7.83 us -> 8.43 us
    unnamed x14 -> x2, local copies, waits for them, and re-layouts: 4.27 us -> 0.01 us
    pallas_call x7, Pallas kernels: 7.83 us -> 8.43 us  [call(): pl.pallas_call(kernel, out_shape=outputs, in_specs=in_specs or [vmem] * l...]
  transfers between devices with their start and end apart: 7 -> 7, of which waited for: 4 -> 4; matrix products, arithmetic and copies ran while one was open for 0% -> 0% of each run, Pallas kernels for 14% -> 17%
where the time goes in v3:
time: 22.8 us; the launch traced here: 22.7 us
  starting transfers between devices  9.76 us (43%)
  Pallas kernels  8.43 us (37%)
  waiting for transfers between devices  4.4 us (19%)
    ppermute x7, starting transfers between devices, exchange(): lax.ppermute(message, axis, [(i, i ^ s * stride) for i in devices])  9.76 us
    pallas_call x7, Pallas kernels, call(): pl.pallas_call(kernel, out_shape=outputs, in_specs=in_specs or [vmem] * l...  8.43 us
    ppermute x7, waiting for transfers between devices, exchange(): lax.ppermute(message, axis, [(i, i ^ s * stride) for i in devices])  4.4 us
  transfers between devices with their start and end apart: 7, of which 4 were waited for; matrix products, arithmetic and copies ran while one was open for 0% of the time, Pallas kernels for 17%

profile of v3, /device:TPU:0, one launch (start us, length us, event | category | flops | bytes accessed | tf_op | source)
XLA Modules:
  0.0 22.7 jit_solution(18408362214940028217)
XLA Ops:
  0.0 0.0 copy-start
  0.0 2.6 %shard_map.64 = (f32[80,128]{1,0:T(8,128)S(1)}, f32[8,40,128]{2,1,0:T(8,128)S(1)}, f32[8,40,128]{2,1,0:T(8,128)S(1)}, f32[8,40,128]{2,1,0:T(8,128)S(1)}, f32[32,...) custom-call(f32[32,8,128]{2,1,0:T(8,128)} %density.1, f32[1,3]{1,0:T(1,128)} %bitcast.8, f32[3,16]{1,0:T(4,128)} %bitcast.6, ...), custom_call_target="tpu_custom_call" | custom-call | flops 1000000 | bytes 1000000 | tf_op jit(solution)/shard_map/pallas_call | solution.py:752
  2.6 3.0 %collective-permute-start = (f32[80,128]{1,0:T(8,128)S(1)}, f32[80,128]{1,0:T(8,128)S(1)}, u32[]{:S(2)}, u32[]{:S(2)}) collective-permute-start(f32[80,128]{1,0:T(8,128)S(1)} %get-tuple-element.25.refs_0_.refs_7_), channel_id=1, source_target_pairs={{0,1},{1,0},{2,3},{3,2},{4,5},{5,4},{6,7},{7,6},{8,9},{9,8},{10,11... | collective-permute-start | bytes 122888 | tf_op jit(solution)/shard_map/ppermute | solution.py:729
  5.6 0.6 %shard_map.66.coefs.refs_6_ = f32[2,4,40,128]{3,2,1,0:T(8,128)S(1)} custom-call(f32[16,128]{1,0:T(8,128)S(1)} %get-tuple-element.17.prepared), custom_call_target="tpu_custom_call" | custom-call | flops 1000000 | bytes 1000000 | tf_op jit(solution)/shard_map/pallas_call | solution.py:752
  6.3 1.4 %collective-permute-done.refs_1_.refs_8_ = f32[80,128]{1,0:T(8,128)S(1)} collective-permute-done((f32[80,128]{1,0:T(8,128)S(1)}, f32[80,128]{1,0:T(8,128)S(1)}, u32[]{:S(2)}, u32[]{:S(2)}) %collective-permute-start) | collective-permute-done | bytes 40992 | tf_op jit(solution)/shard_map/ppermute | solution.py:729
  7.7 4.2 %collective-permute-start.3 = (f32[80,128]{1,0:T(8,128)S(1)}, f32[80,128]{1,0:T(8,128)S(1)}, u32[]{:S(2)}, u32[]{:S(2)}) collective-permute-start(f32[80,128]{1,0:T(8,128)S(1)} %shard_map.68.refs_10_), channel_id=1, source_target_pairs={{0,6},{1,7},{2,4},{3,5},{4,2},{5,3},{6,0},{7,1},{8,14},{9,15},{10,... | collective-permute-start | bytes 122888 | tf_op jit(solution)/shard_map/ppermute | solution.py:729
  11.8 0.0 collective-permute-start.2
  11.9 0.6 %collective-permute-start.1 = (f32[80,128]{1,0:T(8,128)S(1)}, f32[80,128]{1,0:T(8,128)S(1)}, u32[]{:S(2)}, u32[]{:S(2)}) collective-permute-start(f32[80,128]{1,0:T(8,128)S(1)} %shard_map.68.refs_10_), channel_id=1, source_target_pairs={{0,2},{1,3},{2,0},{3,1},{4,6},{5,7},{6,4},{7,5},{8,10},{9,11},{10,... | collective-permute-start | bytes 122888 | tf_op jit(solution)/shard_map/ppermute | solution.py:729
  12.5 1.6 %shard_map.67.refs_9_ = f32[4,4,40,128]{3,2,1,0:T(8,128)S(1)} custom-call(f32[16,128]{1,0:T(8,128)S(1)} %get-tuple-element.17.prepared), custom_call_target="tpu_custom_call" | custom-call | flops 1000000 | bytes 1000000 | tf_op jit(solution)/shard_map/pallas_call | solution.py:752
  14.1 1.6 %shard_map.65 = (f32[7,3,8,32,128]{4,3,2,1,0:T(8,128)S(1)}, f32[2,8,32,128]{3,2,1,0:T(8,128)S(1)}, f32[8,128]{1,0:T(8,128)S(1)}, f32[32,128]{1,0:T(8,128)S(1)}) custom-call(f32[16,128]{1,0:T(8,128)S(1)} %get-tuple-element.17.prepared, f32[32,8,128]{2,1,0:T(8,128)S(1)} %get-tuple-element.18.drift_z), custom_call_target="tpu_custom_call" | custom-call | flops 1000000 | bytes 1000000 | tf_op jit(solution)/shard_map/pallas_call | solution.py:752
  15.7 0.0 collective-permute-done.3.refs_13_
  15.7 1.1 %collective-permute-done.2.refs_12_ = f32[80,128]{1,0:T(8,128)S(1)} collective-permute-done((f32[80,128]{1,0:T(8,128)S(1)}, f32[80,128]{1,0:T(8,128)S(1)}, u32[]{:S(2)}, u32[]{:S(2)}) %collective-permute-start.2) | collective-permute-done | bytes 40992 | tf_op jit(solution)/shard_map/ppermute | solution.py:729
  16.8 0.0 collective-permute-done.1.refs_11_
  16.8 1.0 %shard_map.69 = (f32[32,128]{1,0:T(8,128)S(1)}, f32[8,32,128]{2,1,0:T(8,128)S(1)}) custom-call(f32[7,3,8,32,128]{4,3,2,1,0:T(8,128)S(1)} %get-tuple-element.19.refs_0_, f32[8,128]{1,0:T(8,128)S(1)} %get-tuple-element.20.refs_1_, f32[32,128]{1,0:T(8,128)S(1)} %get-tuple-element.21.refs_2_, f32[8,40,128]{2,1,0:T(8,128)S(1)} %get-tuple-element.22.refs_3_, ...), custom_call_target="tpu_custom_call" | custom-call | flops 1000000 | bytes 1000000 | tf_op jit(solution)/shard_map/pallas_call | solution.py:752
  17.7 0.1 collective-permute-start.6
  17.8 1.6 %collective-permute-start.5 = (f32[32,128]{1,0:T(8,128)S(1)}, f32[32,128]{1,0:T(8,128)S(1)}, u32[]{:S(2)}, u32[]{:S(2)}) collective-permute-start(f32[32,128]{1,0:T(8,128)S(1)} %get-tuple-element.28.refs_0_), channel_id=1, source_target_pairs={{0,16},{8,24},{16,0},{24,8},{1,17},{9,25},{17,1},{25,9},{2,18},{10... | collective-permute-start | bytes 49160 | tf_op jit(solution)/shard_map/ppermute | solution.py:729
  19.4 0.3 %collective-permute-start.4 = (f32[32,128]{1,0:T(8,128)S(1)}, f32[32,128]{1,0:T(8,128)S(1)}, u32[]{:S(2)}, u32[]{:S(2)}) collective-permute-start(f32[32,128]{1,0:T(8,128)S(1)} %get-tuple-element.28.refs_0_), channel_id=1, source_target_pairs={{0,8},{8,0},{16,24},{24,16},{1,9},{9,1},{17,25},{25,17},{2,10},{10... | collective-permute-start | bytes 49160 | tf_op jit(solution)/shard_map/ppermute | solution.py:729
  19.7 1.4 %collective-permute-done.6.refs_3_ = f32[32,128]{1,0:T(8,128)S(1)} collective-permute-done((f32[32,128]{1,0:T(8,128)S(1)}, f32[32,128]{1,0:T(8,128)S(1)}, u32[]{:S(2)}, u32[]{:S(2)}) %collective-permute-start.6) | collective-permute-done | bytes 16416 | tf_op jit(solution)/shard_map/ppermute | solution.py:729
  21.1 0.6 %collective-permute-done.5.refs_2_ = f32[32,128]{1,0:T(8,128)S(1)} collective-permute-done((f32[32,128]{1,0:T(8,128)S(1)}, f32[32,128]{1,0:T(8,128)S(1)}, u32[]{:S(2)}, u32[]{:S(2)}) %collective-permute-start.5) | collective-permute-done | bytes 16416 | tf_op jit(solution)/shard_map/ppermute | solution.py:729
  21.6 0.0 collective-permute-done.4.refs_1_
  21.6 0.0 copy-done
  21.6 1.0 %shard_map.70 = f32[32,8,128]{2,1,0:T(8,128)} custom-call(f32[32,8,128]{2,1,0:T(8,128)S(1)} %copy-done, f32[8,32,128]{2,1,0:T(8,128)S(1)} %get-tuple-element.26.doubled, f32[2,8,32,128]{3,2,1,0:T(8,128)S(1)} %get-tuple-element.27.ends, f32[32,128]{1,0:T(8,128)S(1)} %get-tuple-element.28.refs_0_, f32[32,128]{1,0:T(8,128)S(1)} %collective-permute-done.4.refs_1_, ...), custom_call_target="tpu_custom_call" | custom-call | flops 1000000 | bytes 1000000 | tf_op jit(solution)/shard_map/pallas_call | solution.py:752
  (1 shorter events, 0.0 us)
Async XLA Ops:
  0.0 21.6 %copy-start = (f32[32,8,128]{2,1,0:T(8,128)S(1)}, f32[32,8,128]{2,1,0:T(8,128)}, u32[]{:S(2)}) copy-start(f32[32,8,128]{2,1,0:T(8,128)} %density.1) | copy-start | bytes 393220
  2.6 5.0 %collective-permute-start = (f32[80,128]{1,0:T(8,128)S(1)}, f32[80,128]{1,0:T(8,128)S(1)}, u32[]{:S(2)}, u32[]{:S(2)}) collective-permute-start(f32[80,128]{1,0:T(8,128)S(1)} %get-tuple-element.25.refs_0_.refs_7_), channel_id=1, source_target_pairs={{0,1},{1,0},{2,3},{3,2},{4,5},{5,4},{6,7},{7,6},{8,9},{9,8},{10,11... | collective-permute-start | bytes 122888 | tf_op jit(solution)/shard_map/ppermute | solution.py:729
  7.7 8.0 %collective-permute-start.3 = (f32[80,128]{1,0:T(8,128)S(1)}, f32[80,128]{1,0:T(8,128)S(1)}, u32[]{:S(2)}, u32[]{:S(2)}) collective-permute-start(f32[80,128]{1,0:T(8,128)S(1)} %shard_map.68.refs_10_), channel_id=1, source_target_pairs={{0,6},{1,7},{2,4},{3,5},{4,2},{5,3},{6,0},{7,1},{8,14},{9,15},{10,... | collective-permute-start | bytes 122888 | tf_op jit(solution)/shard_map/ppermute | solution.py:729
  11.8 4.9 %collective-permute-start.2 = (f32[80,128]{1,0:T(8,128)S(1)}, f32[80,128]{1,0:T(8,128)S(1)}, u32[]{:S(2)}, u32[]{:S(2)}) collective-permute-start(f32[80,128]{1,0:T(8,128)S(1)} %shard_map.68.refs_10_), channel_id=1, source_target_pairs={{0,4},{1,5},{2,6},{3,7},{4,0},{5,1},{6,2},{7,3},{8,12},{9,13},{10,... | collective-permute-start | bytes 122888 | tf_op jit(solution)/shard_map/ppermute | solution.py:729
  11.9 4.9 %collective-permute-start.1 = (f32[80,128]{1,0:T(8,128)S(1)}, f32[80,128]{1,0:T(8,128)S(1)}, u32[]{:S(2)}, u32[]{:S(2)}) collective-permute-start(f32[80,128]{1,0:T(8,128)S(1)} %shard_map.68.refs_10_), channel_id=1, source_target_pairs={{0,2},{1,3},{2,0},{3,1},{4,6},{5,7},{6,4},{7,5},{8,10},{9,11},{10,... | collective-permute-start | bytes 122888 | tf_op jit(solution)/shard_map/ppermute | solution.py:729
  17.7 3.3 %collective-permute-start.6 = (f32[32,128]{1,0:T(8,128)S(1)}, f32[32,128]{1,0:T(8,128)S(1)}, u32[]{:S(2)}, u32[]{:S(2)}) collective-permute-start(f32[32,128]{1,0:T(8,128)S(1)} %get-tuple-element.28.refs_0_), channel_id=1, source_target_pairs={{0,24},{8,16},{16,8},{24,0},{1,25},{9,17},{17,9},{25,1},{2,26},{10... | collective-permute-start | bytes 49160 | tf_op jit(solution)/shard_map/ppermute | solution.py:729
  17.8 3.8 %collective-permute-start.5 = (f32[32,128]{1,0:T(8,128)S(1)}, f32[32,128]{1,0:T(8,128)S(1)}, u32[]{:S(2)}, u32[]{:S(2)}) collective-permute-start(f32[32,128]{1,0:T(8,128)S(1)} %get-tuple-element.28.refs_0_), channel_id=1, source_target_pairs={{0,16},{8,24},{16,0},{24,8},{1,17},{9,25},{17,1},{25,9},{2,18},{10... | collective-permute-start | bytes 49160 | tf_op jit(solution)/shard_map/ppermute | solution.py:729
  19.4 2.2 %collective-permute-start.4 = (f32[32,128]{1,0:T(8,128)S(1)}, f32[32,128]{1,0:T(8,128)S(1)}, u32[]{:S(2)}, u32[]{:S(2)}) collective-permute-start(f32[32,128]{1,0:T(8,128)S(1)} %get-tuple-element.28.refs_0_), channel_id=1, source_target_pairs={{0,8},{8,0},{16,24},{24,16},{1,9},{9,1},{17,25},{25,17},{2,10},{10... | collective-permute-start | bytes 49160 | tf_op jit(solution)/shard_map/ppermute | solution.py:729

commit v4 on v3

--- a/solution.py
+++ b/solution.py
@@ -26,13 +26,20 @@
 
 
 def matmul(left, right):
-    return lax.dot_general(
-        left,
-        right,
+    low, high = split(left), split(right)
+    columns = right.shape[0]
+    both = lax.dot_general(
+        jnp.concatenate(low, axis=1),
+        jnp.concatenate([jnp.concatenate([part, part], axis=1) for part in high], axis=0),
         (((1,), (1,)), ((), ())),
-        precision=lax.Precision.HIGHEST,
         preferred_element_type=jnp.float32,
     )
+    return both[:, :columns] + both[:, columns:]
+
+
+def split(values):
+    upper = values.astype(jnp.bfloat16)
+    return upper, (values - upper.astype(jnp.float32)).astype(jnp.bfloat16)
 
 
 def half_drift(left, right):

time: 22.8 us -> 22.4 us (0.982)
  Pallas kernels: 8.43 us -> 7.29 us
  waiting for transfers between devices: 4.4 us -> 5.16 us
    pallas_call x7, Pallas kernels: 8.43 us -> 7.29 us  [call(): pl.pallas_call(kernel, out_shape=outputs, in_specs=in_specs or [vmem] * l...]
    ppermute x7, waiting for transfers between devices: 4.4 us -> 5.16 us  [exchange(): lax.ppermute(message, axis, [(i, i ^ s * stride) for i in devices])]
  transfers between devices with their start and end apart: 7 -> 7, of which waited for: 4 -> 4; matrix products, arithmetic and copies ran while one was open for 0% -> 0% of each run, Pallas kernels for 17% -> 14%
where the time goes in v4:
time: 22.4 us; the launch traced here: 22.3 us
  starting transfers between devices  9.76 us (44%)
  Pallas kernels  7.29 us (33%)
  waiting for transfers between devices  5.16 us (23%)
    ppermute x7, starting transfers between devices, exchange(): lax.ppermute(message, axis, [(i, i ^ s * stride) for i in devices])  9.76 us
    pallas_call x7, Pallas kernels, call(): pl.pallas_call(kernel, out_shape=outputs, in_specs=in_specs or [vmem] * l...  7.29 us
    ppermute x7, waiting for transfers between devices, exchange(): lax.ppermute(message, axis, [(i, i ^ s * stride) for i in devices])  5.16 us
  transfers between devices with their start and end apart: 7, of which 4 were waited for; matrix products, arithmetic and copies ran while one was open for 0% of the time, Pallas kernels for 14%

profile of v4, /device:TPU:0, one launch (start us, length us, event | category | flops | bytes accessed | tf_op | source)
XLA Modules:
  0.0 22.3 jit_solution(559260027327673614)
XLA Ops:
  0.0 0.0 copy-start
  0.0 2.3 %shard_map.64 = (f32[80,128]{1,0:T(8,128)S(1)}, f32[8,40,128]{2,1,0:T(8,128)S(1)}, f32[8,40,128]{2,1,0:T(8,128)S(1)}, f32[8,40,128]{2,1,0:T(8,128)S(1)}, f32[32,...) custom-call(f32[32,8,128]{2,1,0:T(8,128)} %density.1, f32[1,3]{1,0:T(1,128)} %bitcast.8, f32[3,16]{1,0:T(4,128)} %bitcast.6, ...), custom_call_target="tpu_custom_call" | custom-call | flops 1000000 | bytes 1000000 | tf_op jit(solution)/shard_map/pallas_call | solution.py:759
  2.3 3.0 %collective-permute-start = (f32[80,128]{1,0:T(8,128)S(1)}, f32[80,128]{1,0:T(8,128)S(1)}, u32[]{:S(2)}, u32[]{:S(2)}) collective-permute-start(f32[80,128]{1,0:T(8,128)S(1)} %get-tuple-element.25.refs_0_.refs_7_), channel_id=1, source_target_pairs={{0,1},{1,0},{2,3},{3,2},{4,5},{5,4},{6,7},{7,6},{8,9},{9,8},{10,11... | collective-permute-start | bytes 122888 | tf_op jit(solution)/shard_map/ppermute | solution.py:736
  5.3 0.4 %shard_map.66.coefs.refs_6_ = f32[2,4,40,128]{3,2,1,0:T(8,128)S(1)} custom-call(f32[16,128]{1,0:T(8,128)S(1)} %get-tuple-element.17.prepared), custom_call_target="tpu_custom_call" | custom-call | flops 1000000 | bytes 1000000 | tf_op jit(solution)/shard_map/pallas_call | solution.py:759
  5.7 1.5 %collective-permute-done.refs_1_.refs_8_ = f32[80,128]{1,0:T(8,128)S(1)} collective-permute-done((f32[80,128]{1,0:T(8,128)S(1)}, f32[80,128]{1,0:T(8,128)S(1)}, u32[]{:S(2)}, u32[]{:S(2)}) %collective-permute-start) | collective-permute-done | bytes 40992 | tf_op jit(solution)/shard_map/ppermute | solution.py:736
  7.3 4.2 %collective-permute-start.3 = (f32[80,128]{1,0:T(8,128)S(1)}, f32[80,128]{1,0:T(8,128)S(1)}, u32[]{:S(2)}, u32[]{:S(2)}) collective-permute-start(f32[80,128]{1,0:T(8,128)S(1)} %shard_map.68.refs_10_), channel_id=1, source_target_pairs={{0,6},{1,7},{2,4},{3,5},{4,2},{5,3},{6,0},{7,1},{8,14},{9,15},{10,... | collective-permute-start | bytes 122888 | tf_op jit(solution)/shard_map/ppermute | solution.py:736
  11.5 0.0 collective-permute-start.2
  11.5 0.6 %collective-permute-start.1 = (f32[80,128]{1,0:T(8,128)S(1)}, f32[80,128]{1,0:T(8,128)S(1)}, u32[]{:S(2)}, u32[]{:S(2)}) collective-permute-start(f32[80,128]{1,0:T(8,128)S(1)} %shard_map.68.refs_10_), channel_id=1, source_target_pairs={{0,2},{1,3},{2,0},{3,1},{4,6},{5,7},{6,4},{7,5},{8,10},{9,11},{10,... | collective-permute-start | bytes 122888 | tf_op jit(solution)/shard_map/ppermute | solution.py:736
  12.1 1.0 %shard_map.67.refs_9_ = f32[4,4,40,128]{3,2,1,0:T(8,128)S(1)} custom-call(f32[16,128]{1,0:T(8,128)S(1)} %get-tuple-element.17.prepared), custom_call_target="tpu_custom_call" | custom-call | flops 1000000 | bytes 1000000 | tf_op jit(solution)/shard_map/pallas_call | solution.py:759
  13.2 1.5 %shard_map.65 = (f32[7,3,8,32,128]{4,3,2,1,0:T(8,128)S(1)}, f32[2,8,32,128]{3,2,1,0:T(8,128)S(1)}, f32[8,128]{1,0:T(8,128)S(1)}, f32[32,128]{1,0:T(8,128)S(1)}) custom-call(f32[16,128]{1,0:T(8,128)S(1)} %get-tuple-element.17.prepared, f32[32,8,128]{2,1,0:T(8,128)S(1)} %get-tuple-element.18.drift_z), custom_call_target="tpu_custom_call" | custom-call | flops 1000000 | bytes 1000000 | tf_op jit(solution)/shard_map/pallas_call | solution.py:759
  14.7 0.0 collective-permute-done.3.refs_13_
  14.7 1.6 %collective-permute-done.2.refs_12_ = f32[80,128]{1,0:T(8,128)S(1)} collective-permute-done((f32[80,128]{1,0:T(8,128)S(1)}, f32[80,128]{1,0:T(8,128)S(1)}, u32[]{:S(2)}, u32[]{:S(2)}) %collective-permute-start.2) | collective-permute-done | bytes 40992 | tf_op jit(solution)/shard_map/ppermute | solution.py:736
  16.4 0.0 collective-permute-done.1.refs_11_
  16.4 1.0 %shard_map.69 = (f32[32,128]{1,0:T(8,128)S(1)}, f32[8,32,128]{2,1,0:T(8,128)S(1)}) custom-call(f32[7,3,8,32,128]{4,3,2,1,0:T(8,128)S(1)} %get-tuple-element.19.refs_0_, f32[8,128]{1,0:T(8,128)S(1)} %get-tuple-element.20.refs_1_, f32[32,128]{1,0:T(8,128)S(1)} %get-tuple-element.21.refs_2_, f32[8,40,128]{2,1,0:T(8,128)S(1)} %get-tuple-element.22.refs_3_, ...), custom_call_target="tpu_custom_call" | custom-call | flops 1000000 | bytes 1000000 | tf_op jit(solution)/shard_map/pallas_call | solution.py:759
  17.4 0.1 collective-permute-start.6
  17.5 1.6 %collective-permute-start.5 = (f32[32,128]{1,0:T(8,128)S(1)}, f32[32,128]{1,0:T(8,128)S(1)}, u32[]{:S(2)}, u32[]{:S(2)}) collective-permute-start(f32[32,128]{1,0:T(8,128)S(1)} %get-tuple-element.28.refs_0_), channel_id=1, source_target_pairs={{0,16},{8,24},{16,0},{24,8},{1,17},{9,25},{17,1},{25,9},{2,18},{10... | collective-permute-start | bytes 49160 | tf_op jit(solution)/shard_map/ppermute | solution.py:736
  19.0 0.3 %collective-permute-start.4 = (f32[32,128]{1,0:T(8,128)S(1)}, f32[32,128]{1,0:T(8,128)S(1)}, u32[]{:S(2)}, u32[]{:S(2)}) collective-permute-start(f32[32,128]{1,0:T(8,128)S(1)} %get-tuple-element.28.refs_0_), channel_id=1, source_target_pairs={{0,8},{8,0},{16,24},{24,16},{1,9},{9,1},{17,25},{25,17},{2,10},{10... | collective-permute-start | bytes 49160 | tf_op jit(solution)/shard_map/ppermute | solution.py:736
  19.3 1.4 %collective-permute-done.6.refs_3_ = f32[32,128]{1,0:T(8,128)S(1)} collective-permute-done((f32[32,128]{1,0:T(8,128)S(1)}, f32[32,128]{1,0:T(8,128)S(1)}, u32[]{:S(2)}, u32[]{:S(2)}) %collective-permute-start.6) | collective-permute-done | bytes 16416 | tf_op jit(solution)/shard_map/ppermute | solution.py:736
  20.7 0.6 %collective-permute-done.5.refs_2_ = f32[32,128]{1,0:T(8,128)S(1)} collective-permute-done((f32[32,128]{1,0:T(8,128)S(1)}, f32[32,128]{1,0:T(8,128)S(1)}, u32[]{:S(2)}, u32[]{:S(2)}) %collective-permute-start.5) | collective-permute-done | bytes 16416 | tf_op jit(solution)/shard_map/ppermute | solution.py:736
  21.3 0.0 collective-permute-done.4.refs_1_
  21.3 0.0 copy-done
  21.3 1.0 %shard_map.70 = f32[32,8,128]{2,1,0:T(8,128)} custom-call(f32[32,8,128]{2,1,0:T(8,128)S(1)} %copy-done, f32[8,32,128]{2,1,0:T(8,128)S(1)} %get-tuple-element.26.doubled, f32[2,8,32,128]{3,2,1,0:T(8,128)S(1)} %get-tuple-element.27.ends, f32[32,128]{1,0:T(8,128)S(1)} %get-tuple-element.28.refs_0_, f32[32,128]{1,0:T(8,128)S(1)} %collective-permute-done.4.refs_1_, ...), custom_call_target="tpu_custom_call" | custom-call | flops 1000000 | bytes 1000000 | tf_op jit(solution)/shard_map/pallas_call | solution.py:759
  (1 shorter events, 0.0 us)
Async XLA Ops:
  0.0 21.3 %copy-start = (f32[32,8,128]{2,1,0:T(8,128)S(1)}, f32[32,8,128]{2,1,0:T(8,128)}, u32[]{:S(2)}) copy-start(f32[32,8,128]{2,1,0:T(8,128)} %density.1) | copy-start | bytes 393220
  2.3 5.0 %collective-permute-start = (f32[80,128]{1,0:T(8,128)S(1)}, f32[80,128]{1,0:T(8,128)S(1)}, u32[]{:S(2)}, u32[]{:S(2)}) collective-permute-start(f32[80,128]{1,0:T(8,128)S(1)} %get-tuple-element.25.refs_0_.refs_7_), channel_id=1, source_target_pairs={{0,1},{1,0},{2,3},{3,2},{4,5},{5,4},{6,7},{7,6},{8,9},{9,8},{10,11... | collective-permute-start | bytes 122888 | tf_op jit(solution)/shard_map/ppermute | solution.py:736
  7.3 7.4 %collective-permute-start.3 = (f32[80,128]{1,0:T(8,128)S(1)}, f32[80,128]{1,0:T(8,128)S(1)}, u32[]{:S(2)}, u32[]{:S(2)}) collective-permute-start(f32[80,128]{1,0:T(8,128)S(1)} %shard_map.68.refs_10_), channel_id=1, source_target_pairs={{0,6},{1,7},{2,4},{3,5},{4,2},{5,3},{6,0},{7,1},{8,14},{9,15},{10,... | collective-permute-start | bytes 122888 | tf_op jit(solution)/shard_map/ppermute | solution.py:736
  11.5 4.9 %collective-permute-start.2 = (f32[80,128]{1,0:T(8,128)S(1)}, f32[80,128]{1,0:T(8,128)S(1)}, u32[]{:S(2)}, u32[]{:S(2)}) collective-permute-start(f32[80,128]{1,0:T(8,128)S(1)} %shard_map.68.refs_10_), channel_id=1, source_target_pairs={{0,4},{1,5},{2,6},{3,7},{4,0},{5,1},{6,2},{7,3},{8,12},{9,13},{10,... | collective-permute-start | bytes 122888 | tf_op jit(solution)/shard_map/ppermute | solution.py:736
  11.5 4.9 %collective-permute-start.1 = (f32[80,128]{1,0:T(8,128)S(1)}, f32[80,128]{1,0:T(8,128)S(1)}, u32[]{:S(2)}, u32[]{:S(2)}) collective-permute-start(f32[80,128]{1,0:T(8,128)S(1)} %shard_map.68.refs_10_), channel_id=1, source_target_pairs={{0,2},{1,3},{2,0},{3,1},{4,6},{5,7},{6,4},{7,5},{8,10},{9,11},{10,... | collective-permute-start | bytes 122888 | tf_op jit(solution)/shard_map/ppermute | solution.py:736
  17.4 3.3 %collective-permute-start.6 = (f32[32,128]{1,0:T(8,128)S(1)}, f32[32,128]{1,0:T(8,128)S(1)}, u32[]{:S(2)}, u32[]{:S(2)}) collective-permute-start(f32[32,128]{1,0:T(8,128)S(1)} %get-tuple-element.28.refs_0_), channel_id=1, source_target_pairs={{0,24},{8,16},{16,8},{24,0},{1,25},{9,17},{17,9},{25,1},{2,26},{10... | collective-permute-start | bytes 49160 | tf_op jit(solution)/shard_map/ppermute | solution.py:736
  17.5 3.8 %collective-permute-start.5 = (f32[32,128]{1,0:T(8,128)S(1)}, f32[32,128]{1,0:T(8,128)S(1)}, u32[]{:S(2)}, u32[]{:S(2)}) collective-permute-start(f32[32,128]{1,0:T(8,128)S(1)} %get-tuple-element.28.refs_0_), channel_id=1, source_target_pairs={{0,16},{8,24},{16,0},{24,8},{1,17},{9,25},{17,1},{25,9},{2,18},{10... | collective-permute-start | bytes 49160 | tf_op jit(solution)/shard_map/ppermute | solution.py:736
  19.0 2.2 %collective-permute-start.4 = (f32[32,128]{1,0:T(8,128)S(1)}, f32[32,128]{1,0:T(8,128)S(1)}, u32[]{:S(2)}, u32[]{:S(2)}) collective-permute-start(f32[32,128]{1,0:T(8,128)S(1)} %get-tuple-element.28.refs_0_), channel_id=1, source_target_pairs={{0,8},{8,0},{16,24},{24,16},{1,9},{9,1},{17,25},{25,17},{2,10},{10... | collective-permute-start | bytes 49160 | tf_op jit(solution)/shard_map/ppermute | solution.py:736

commit v5 on v4

--- a/solution.py
+++ b/solution.py
@@ -107,8 +107,8 @@
 
 def xz_rows(params, maps, size_x, z_start, size_z, total_z):
     row = iota((2 * size_x, LANES), 0)
-    x_coord = coordinate(row // 2, size_x)
-    z_coord = coordinate(jnp.where(row % 2 == 0, z_start - 1, z_start + size_z), total_z)
+    x_coord = coordinate(row % size_x, size_x)
+    z_coord = coordinate(jnp.where(row < size_x, z_start - 1, z_start + size_z), total_z)
     part = slope(params, x_coord, 0) + slope(params, z_coord, 2)
     both = bump(params, x_coord, 0) * bump(params, z_coord, 2)
     both = both * jnp.where(first_term(maps), 1.0, part)
@@ -123,10 +123,43 @@
 
 def pack_planes(planes):
     lane = iota(planes[0].shape, 1)
-    out = jnp.zeros(planes[0].shape, jnp.float32)
+    first = last = jnp.zeros(planes[0].shape, jnp.float32)
     for i, plane in enumerate(planes):
-        out = jnp.where(lane // 2 == i, roll(plane, 2 * i + 1, 1), out)
-    return out
+        turned = roll(plane, i + 1, 1)
+        first = jnp.where(lane == i, turned, first)
+        last = jnp.where(lane == i + 1, turned, last)
+    return first + roll(last, len(planes) - 1, 1)
+
+
+def lines_of(planes, size_x, side):
+    group = LANES // size_x
+    place = iota((1, LANES), 1) // size_x
+    turned = [roll(planes, (q - side) * size_x, 1) for q in range(group)]
+    rows = []
+    for first in range(0, planes.shape[0], group):
+        row = turned[0][first : first + 1]
+        for q in range(1, group):
+            row = jnp.where(place == q, turned[q][first + q : first + q + 1], row)
+        rows.append(row)
+    return jnp.concatenate(rows, axis=1)
+
+
+def to_lines(rows, size_x):
+    group = LANES // size_x
+    return jnp.concatenate(
+        [
+            jnp.transpose(jnp.concatenate(rows[first : first + group], axis=0))
+            for first in range(0, len(rows), group)
+        ],
+        axis=1,
+    )
+
+
+def turn(values, stride):
+    stride = stride % values.shape[0]
+    if stride % ROWS == 0:
+        return jnp.concatenate([values[-stride:], values[:-stride]], axis=0)
+    return roll(values, stride, 0)
 
 
 def merge_coefs(low, high):
@@ -225,9 +258,8 @@
     affine_hbm,
     offsets_hbm,
     message,
-    base,
-    from_below,
-    from_above,
+    line_values,
+    line_drifts,
     drift_z_out,
     prepared,
     solved,
@@ -374,40 +406,39 @@
         + [ends[size_x:]]
     )
     line_drift = [with_extra(line_drift[j], extra[j : j + 1]) for j in range(size_y + 2)]
+    values = [with_extra(solved[:, j, :], planes[j : j + 1]) for j in range(size_y)]
+    for j in range(size_y):
+        line_values[j] = values[j]
+    for j in range(size_y + 2):
+        line_drifts[j] = line_drift[j]
     pivot = 1.0 + 2.0 * d1
-    at_start = y_start == 0
-    at_end = y_start + size_y == total_y
-    g = a = c = None
-    gs, as_, cs = [], [], []
+    g = c = None
+    gs, cs = [], []
     for j in range(size_y):
-        value = with_extra(solved[:, j, :], planes[j : j + 1])
-        lower = d1 + line_drift[j]
-        upper = d1 - line_drift[j + 2]
-        if j == 0:
-            lower = jnp.where(at_start, 0.0, lower)
-        if j == size_y - 1:
-            upper = jnp.where(at_end, 0.0, upper)
-        if j == 0:
-            weight = 1.0 / pivot
-            g, a = value * weight, lower * weight
-        else:
-            weight = 1.0 / (pivot - lower * c)
-            g, a = (value + lower * g) * weight, lower * a * weight
+        lower, upper = line_factors(line_drift, j, size_y, d1, y_start, total_y)
+        weight = 1.0 / (pivot if j == 0 else pivot - lower * c)
+        g = (values[j] if j == 0 else values[j] + lower * g) * weight
         c = upper * weight
         gs.append(g)
-        as_.append(a)
         cs.append(c)
-    base[size_y - 1], from_below[size_y - 1], from_above[size_y - 1] = g, a, c
-    r_last = g
+    r_first = r_last = g
     for j in reversed(range(size_y - 1)):
-        g, a, c = gs[j] + cs[j] * g, as_[j] + cs[j] * a, cs[j] * c
-        base[j], from_below[j], from_above[j] = g, a, c
+        r_first = gs[j] + cs[j] * r_first
     pushed_up = solved[:, size_y, :] / (d1 + line_drift[size_y][:size_x])
     pushed_down = solved[:, 2 * size_y - 1, :] / (d1 - line_drift[1][:size_x])
     blank = jnp.zeros((1, LANES), jnp.float32)
     width = size_x + ROWS
-    message[:width] = g + with_extra(pushed_down, blank)
+    message[:width] = r_first + with_extra(pushed_down, blank)
     message[width:] = r_last + with_extra(pushed_up, blank)
+
+
+def line_factors(line_drift, j, size_y, d1, y_start, total_y):
+    lower, upper = d1 + line_drift[j], d1 - line_drift[j + 2]
+    if j == 0:
+        lower = jnp.where(y_start == 0, 0.0, lower)
+    if j == size_y - 1:
+        upper = jnp.where(y_start + size_y == total_y, 0.0, upper)
+    return lower, upper
 
 
 def line_coefs(params, maps, sizes, start, count, store):
@@ -487,14 +518,49 @@
             store(b, q, with_extra(main[q][b], extra[q][b : b + 1]))
 
 
-def near_kernel(sizes, maps, stride, radix, prepared, coefs):
+def near_kernel(
+    sizes,
+    maps,
+    stride,
+    radix,
+    prepared,
+    line_values,
+    line_drifts,
+    coefs,
+    base,
+    from_below,
+    from_above,
+):
     digit = lax.rem(lax.div(lax.axis_index("gy"), stride), radix)
     start = lax.div(lax.axis_index("gy"), stride) - digit
+    params = prepared[...]
 
     def store(b, q, value):
         coefs[b, q] = value
 
-    line_coefs(prepared[...], maps, sizes, start, radix, store)
+    line_coefs(params, maps, sizes, start, radix, store)
+    extent_y, _, _, size_y, _ = sizes
+    d1 = params[DIFFUSION + 1 : DIFFUSION + 2]
+    pivot = 1.0 + 2.0 * d1
+    y_start = lax.axis_index("gy") * size_y
+    g = a = c = None
+    gs, as_, cs = [], [], []
+    for j in range(size_y):
+        lower, upper = line_factors(line_drifts, j, size_y, d1, y_start, size_y * extent_y)
+        if j == 0:
+            weight = 1.0 / pivot
+            g, a = line_values[j] * weight, lower * weight
+        else:
+            weight = 1.0 / (pivot - lower * c)
+            g, a = (line_values[j] + lower * g) * weight, lower * a * weight
+        c = upper * weight
+        gs.append(g)
+        as_.append(a)
+        cs.append(c)
+    base[size_y - 1], from_below[size_y - 1], from_above[size_y - 1] = g, a, c
+    for j in reversed(range(size_y - 1)):
+        g, a, c = gs[j] + cs[j] * g, as_[j] + cs[j] * a, cs[j] * c
+        base[j], from_below[j], from_above[j] = g, a, c
 
 
 def far_kernel(sizes, maps, levels, prepared, *outputs):
@@ -523,7 +589,6 @@
     z_start = lax.axis_index("gz") * size_z
     params = prepared[...]
     d2 = params[DIFFUSION + 2 : DIFFUSION + 3]
-    scale = 1.0 / (1.0 + 2.0 * d2)
     lane = iota((size_y, LANES), 1)
     divisors = []
     for i in range(size_x):
@@ -540,47 +605,44 @@
         bumps, part = y_factors(params, maps, position, total_y)
         rows.append((x_bump * bumps) * (x_part + part))
     outer = half_drift(jnp.concatenate(rows, axis=0), outer)
-    inner = jnp.concatenate([drift_z[:, j, :] for j in range(size_y)], axis=0)
-    lane = iota(inner.shape, 1)
-    low, high = lane == 0, lane == size_z - 1
-    before = jnp.where(low, roll(outer, 1, 1), roll(inner, 1, 1))
-    after = jnp.where(high, roll(outer, -1, 1), roll(inner, -1, 1))
+    outer = to_lines([outer[j * size_x : (j + 1) * size_x] for j in range(size_y)], size_x)
+    inner = to_lines([drift_z[:, j, :] for j in range(size_y)], size_x)
+    d2 = jnp.concatenate([d2] * (inner.shape[1] // LANES), axis=1)
+    scale = 1.0 / (1.0 + 2.0 * d2)
+    row = iota(inner.shape, 0)
+    low, high = row == 0, row == size_z - 1
+    before = jnp.where(low, outer[size_z - 1 :], turn(inner, 1))
+    after = jnp.where(high, outer[:1], turn(inner, -1))
     below = jnp.where(low & (z_start == 0), 0.0, (d2 + before) * scale)
     above = jnp.where(high & (z_start + size_z == total_z), 0.0, (d2 - after) * scale)
-    shape = (size_y, size_x, LANES)
     stride, level = 1, 0
     while stride < size_z:
-        low, high = lane < stride, lane >= size_z - stride
-        low_a = jnp.where(low, 1.0, roll(below, stride, 1))
-        low_c = jnp.where(low, 0.0, roll(above, stride, 1))
-        high_a = jnp.where(high, 0.0, roll(below, -stride, 1))
-        high_c = jnp.where(high, 1.0, roll(above, -stride, 1))
+        low, high = row < stride, row >= size_z - stride
+        low_a = jnp.where(low, 1.0, turn(below, stride))
+        low_c = jnp.where(low, 0.0, turn(above, stride))
+        high_a = jnp.where(high, 0.0, turn(below, -stride))
+        high_c = jnp.where(high, 1.0, turn(above, -stride))
         inverse = 1.0 / (1.0 - below * low_c - above * high_a)
         below, above = below * inverse, above * inverse
         factor = scale if level == 0 else 1.0
-        steps[level, 0] = (inverse * factor).reshape(shape)
-        steps[level, 1] = jnp.where(low, 0.0, below * factor).reshape(shape)
-        steps[level, 2] = jnp.where(high, 0.0, above * factor).reshape(shape)
+        steps[level, 0] = inverse * factor
+        steps[level, 1] = jnp.where(low, 0.0, below * factor)
+        steps[level, 2] = jnp.where(high, 0.0, above * factor)
         below, above = below * low_a, above * high_c
         stride, level = stride * 2, level + 1
-    below, above = below.reshape(shape), above.reshape(shape)
     ends[0] = below
     ends[1] = above
-    packed[...] = pack_ends([below[j] for j in range(size_y)], 1, size_y) + pack_ends(
-        [above[j] for j in range(size_y)], 2, size_y
-    )
-
-
-def pack_ends(rows, slot, size_y):
-    shape = rows[0].shape
-    lane = iota(shape, 1)
-    out = jnp.zeros(shape, jnp.float32)
-    for j in range(size_y):
-        first = slot * 2 * size_y + j
-        last = first + size_y
-        out = jnp.where(lane == first, roll(rows[j], first, 1), out)
-        out = jnp.where(lane == last, roll(rows[j], last - (LANES - 1), 1), out)
-    return out
+    packed[...] = jnp.concatenate(
+        [
+            jnp.zeros((2, inner.shape[1]), jnp.float32),
+            below[:1],
+            below[size_z - 1 :],
+            above[:1],
+            above[size_z - 1 :],
+            jnp.zeros((2, inner.shape[1]), jnp.float32),
+        ],
+        axis=0,
+    )
 
 
 def gather_members(refs, own, count):
@@ -599,7 +661,7 @@
 
 
 def merge_kernel(stride, radix, local, coefs, *refs):
-    received, message = refs[:radix], refs[radix]
+    received, message = refs[:radix], refs[-1]
     digit = lax.rem(lax.div(lax.axis_index("gy"), stride), radix)
     first = 0 if local else lax.div(lax.axis_index("gy"), stride) - digit
     values = [split_message(m) for m in gather_members(received, digit, radix)]
@@ -619,7 +681,7 @@
     for stride, radix in levels:
         inputs.append((refs[0], refs[1 : 1 + radix]))
         refs = refs[1 + radix :]
-    message, doubled, seen, turned = refs
+    message, doubled, seen = refs
     size_y, width = base.shape[:2]
     size_x = width - ROWS
     below = above = jnp.zeros((width, LANES), jnp.float32)
@@ -639,23 +701,20 @@
         value = base[j] + from_below[j] * below + from_above[j] * above
         inner.append(value[:size_x])
         outer.append(value[size_x : size_x + 1])
-    turned[...] = jnp.transpose(jnp.concatenate(outer, axis=0) * pushes[...])
-    values = jnp.stack(inner)
+    pushed = jnp.concatenate(outer, axis=0) * pushes[...]
+    values = to_lines(inner, size_x)
     stride, level = 1, 0
-    while stride < LANES:
+    while stride < values.shape[0]:
         values = (
             steps[level, 0] * values
-            + steps[level, 1] * roll(values, stride, 2)
-            + steps[level, 2] * roll(values, -stride, 2)
+            + steps[level, 1] * turn(values, stride)
+            + steps[level, 2] * turn(values, -stride)
         )
         stride, level = stride * 2, level + 1
     doubled[...] = values
-    ends = pack_ends([values[j] for j in range(size_y)], 0, size_y) + packed[...]
-    message[...] = ends
-    message[:, :size_y] = ends[:, :size_y] + turned[pl.ds(0, size_x, stride=2), :]
-    message[:, size_y : 2 * size_y] = (
-        ends[:, size_y : 2 * size_y] + turned[pl.ds(1, size_x, stride=2), :]
-    )
+    message[...] = packed[...]
+    message[0:1] = values[:1] + lines_of(pushed, size_x, 0)
+    message[1:2] = values[-1:] + lines_of(pushed, size_x, 1)
 
 
 def merge_z(low, high):
@@ -671,21 +730,16 @@
     )
 
 
-def unpack_ends(message, size_y):
-    return tuple(message if s == 0 else roll(message, -s * size_y, 1) for s in range(6))
-
-
-def merge_z_kernel(stride, radix, size_y, *refs):
+def unpack_ends(message):
+    return tuple(message[s : s + 1] for s in range(6))
+
+
+def merge_z_kernel(stride, radix, *refs):
     received, message = refs[:radix], refs[radix]
     digit = lax.rem(lax.div(lax.axis_index("gz"), stride), radix)
-    members = [unpack_ends(m, size_y) for m in gather_members(received, digit, radix)]
+    members = [unpack_ends(m) for m in gather_members(received, digit, radix)]
     total = functools.reduce(merge_z, members)
-    lane = iota(total[0].shape, 1)
-    out = jnp.zeros(total[0].shape, jnp.float32)
-    for s in range(6):
-        shifted = total[s] if s == 0 else roll(total[s], s * size_y, 1)
-        out = jnp.where(lane // size_y == s, shifted, out)
-    message[...] = out
+    message[...] = jnp.concatenate(total + total[:2], axis=0)
 
 
 def end_kernel(levels, density, doubled, ends, *refs):
@@ -696,10 +750,10 @@
         refs = refs[radix:]
     out, seen = refs
     size_x, size_y, _ = density.shape
-    below = above = jnp.zeros((size_x, LANES), jnp.float32)
+    below = above = jnp.zeros((1, doubled.shape[1]), jnp.float32)
     for (stride, radix), received in zip(reversed(levels), reversed(inputs)):
         digit = lax.rem(lax.div(lax.axis_index("gz"), stride), radix)
-        members = [unpack_ends(m, size_y) for m in gather_members(received, digit, radix)]
+        members = [unpack_ends(m) for m in gather_members(received, digit, radix)]
         lows, highs = chain(
             [(m[2], m[4], m[3], m[5]) for m in members],
             [(m[0], m[1]) for m in members],
@@ -707,24 +761,24 @@
             above,
         )
         for j in range(radix):
-            seen[j, 0] = lows[j]
-            seen[j, 1] = highs[j]
-        below, above = seen[digit, 0], seen[digit, 1]
-    for j in range(size_y):
-        out[:, j, :] = (
-            density[:, j, :]
-            + doubled[j]
-            + ends[0, j] * below[:, j : j + 1]
-            + ends[1, j] * above[:, j : j + 1]
-        )
+            seen[j, 0:1] = lows[j]
+            seen[j, 1:2] = highs[j]
+        below, above = seen[digit, 0:1], seen[digit, 1:2]
+    values = doubled[...] + ends[0] * below + ends[1] * above
+    group = LANES // size_x
+    for first in range(0, size_y, group):
+        tile = first // group
+        lines = jnp.transpose(values[:, tile * LANES : (tile + 1) * LANES])
+        for q in range(group):
+            out[:, first + q, :] = (
+                density[:, first + q, :] + lines[q * size_x : (q + 1) * size_x]
+            )
 
 
 def radices(extent):
     rounds, stride = [], 1
     while stride < extent:
-        left = extent // stride
-        power = left.bit_length() - 1
-        radix = 4 if left % 4 == 0 and power % 2 == 0 else 2
+        radix = 4 if (extent // stride) % 4 == 0 else 2
         rounds.append((stride, radix))
         stride *= radix
     return rounds
@@ -745,7 +799,7 @@
     maps = centers.shape[0]
     width = size_x + ROWS
     wide = (size_y, width, LANES)
-    narrow = (size_y, size_x, LANES)
+    narrow = (size_z, size_y * size_x)
     float32 = jnp.float32
     y_levels, z_levels = radices(extent_y), radices(extent_z)
 
@@ -775,14 +829,13 @@
         offsets.T,
     )
     raw = tuple(pltpu.with_memory_space_constraint(array, pltpu.HBM) for array in raw)
-    message, base, from_below, from_above, drift_z, prepared = call(
+    message, line_values, line_drifts, drift_z, prepared = call(
         functools.partial(start_kernel, extent_y, extent_z),
         raw,
         (
             shape(2 * width, LANES),
             shape(*wide),
-            shape(*wide),
-            shape(*wide),
+            shape(size_y + 2, width, LANES),
             shape(size_x, size_y, LANES),
             shape(PREPARED, LANES),
         ),
@@ -795,10 +848,10 @@
         + [pltpu.VMEM((PREPARED, LANES), float32), pltpu.SemaphoreType.DMA((len(raw),))],
     )
     stride, radix = y_levels[0]
-    near = call(
+    near, base, from_below, from_above = call(
         functools.partial(near_kernel, sizes, maps, stride, radix),
-        [prepared],
-        shape(radix, 4, width, LANES),
+        [prepared, line_values, line_drifts],
+        (shape(radix, 4, width, LANES), shape(*wide), shape(*wide), shape(*wide)),
     )
     far, count = [], extent_y
     for _, radix in y_levels[:-1]:
@@ -815,7 +868,7 @@
             shape(doublings, 3, *narrow),
             shape(2, *narrow),
             shape(size_y, LANES),
-            shape(size_x, LANES),
+            shape(ROWS, size_y * size_x),
         ),
     )
     line_inputs = []
@@ -825,17 +878,14 @@
         if number + 1 < len(y_levels):
             message = call(
                 functools.partial(merge_kernel, stride, radix, number == 0),
-                [coefs[number]] + received,
+                [coefs[number]] + received + ([packed] if number == 0 else []),
                 shape(2 * width, LANES),
             )
     message, doubled = call(
         functools.partial(middle_kernel, y_levels),
         [steps, pushes, packed, base, from_below, from_above] + line_inputs,
-        (shape(size_x, LANES), shape(*narrow)),
-        scratch=[
-            pltpu.VMEM((4, 2, width, LANES), float32),
-            pltpu.VMEM((LANES, size_y), float32),
-        ],
+        (shape(ROWS, size_y * size_x), shape(*narrow)),
+        scratch=[pltpu.VMEM((4, 2, width, LANES), float32)],
     )
     end_inputs = []
     for number, (stride, radix) in enumerate(z_levels):
@@ -843,15 +893,15 @@
         end_inputs += received
         if number + 1 < len(z_levels):
             message = call(
-                functools.partial(merge_z_kernel, stride, radix, size_y),
+                functools.partial(merge_z_kernel, stride, radix),
                 received,
-                shape(size_x, LANES),
+                shape(ROWS, size_y * size_x),
             )
     return call(
         functools.partial(end_kernel, z_levels),
         [density, doubled, ends] + end_inputs,
         shape(size_x, size_y, size_z),
-        scratch=[pltpu.VMEM((4, 2, size_x, LANES), float32)],
+        scratch=[pltpu.VMEM((4, ROWS, size_y * size_x), float32)],
     )
 
 

time: 22.4 us -> 21.1 us (0.942)
  Pallas kernels: 7.29 us -> 6.31 us
  starting transfers between devices: 9.76 us -> 9.23 us
  waiting for transfers between devices: 5.16 us -> 5.41 us
    pallas_call x7, Pallas kernels: 7.29 us -> 6.31 us  [call(): pl.pallas_call(kernel, out_shape=outputs, in_specs=in_specs or [vmem] * l...]
    ppermute x7, starting transfers between devices: 9.76 us -> 9.23 us  [exchange(): lax.ppermute(message, axis, [(i, i ^ s * stride) for i in devices])]
    ppermute x7, waiting for transfers between devices: 5.16 us -> 5.41 us  [exchange(): lax.ppermute(message, axis, [(i, i ^ s * stride) for i in devices])]
  transfers between devices with their start and end apart: 7 -> 7, of which waited for: 4 -> 5; matrix products, arithmetic and copies ran while one was open for 0% -> 0% of each run, Pallas kernels for 14% -> 12%
where the time goes in v5:
time: 21.1 us; the launch traced here: 21 us
  starting transfers between devices  9.23 us (44%)
  Pallas kernels  6.31 us (30%)
  waiting for transfers between devices  5.41 us (26%)
    ppermute x7, starting transfers between devices, exchange(): lax.ppermute(message, axis, [(i, i ^ s * stride) for i in devices])  9.23 us
    pallas_call x7, Pallas kernels, call(): pl.pallas_call(kernel, out_shape=outputs, in_specs=in_specs or [vmem] * l...  6.31 us
    ppermute x7, waiting for transfers between devices, exchange(): lax.ppermute(message, axis, [(i, i ^ s * stride) for i in devices])  5.41 us
  transfers between devices with their start and end apart: 7, of which 5 were waited for; matrix products, arithmetic and copies ran while one was open for 0% of the time, Pallas kernels for 12%

profile of v5, /device:TPU:0, one launch (start us, length us, event | category | flops | bytes accessed | tf_op | source)
XLA Modules:
  0.0 21.0 jit_solution(3999309910469243216)
XLA Ops:
  0.0 0.0 copy-start
  0.0 2.3 %shard_map.64 = (f32[80,128]{1,0:T(8,128)S(1)}, f32[8,40,128]{2,1,0:T(8,128)S(1)}, f32[10,40,128]{2,1,0:T(8,128)S(1)}, f32[32,8,128]{2,1,0:T(8,128)S(1)}, f32[16,128]{1,0:T(8,128)S(1)}) custom-call(f32[32,8,128]{2,1,0:T(8,128)} %density.1, f32[1,3]{1,0:T(1,128)} %bitcast.8, f32[3,16]{1,0:T(4,128)} %bitcast.6, f32[1,16]{1,0:T(1,128)} %bitcast.9, ...), custom_call_target="tpu_custom_call" | custom-call | flops 1000000 | bytes 1000000 | tf_op jit(solution)/shard_map/pallas_call | solution.py:813
  2.3 4.0 %collective-permute-start.2 = (f32[80,128]{1,0:T(8,128)S(1)}, f32[80,128]{1,0:T(8,128)S(1)}, u32[]{:S(2)}, u32[]{:S(2)}) collective-permute-start(f32[80,128]{1,0:T(8,128)S(1)} %get-tuple-element.31.refs_0_.refs_7_), channel_id=1, source_target_pairs={{0,3},{1,2},{2,1},{3,0},{4,7},{5,6},{6,5},{7,4},{8,11},{9,10},{10,... | collective-permute-start | bytes 122888 | tf_op jit(solution)/shard_map/ppermute | solution.py:790
  6.3 0.5 %collective-permute-start.1 = (f32[80,128]{1,0:T(8,128)S(1)}, f32[80,128]{1,0:T(8,128)S(1)}, u32[]{:S(2)}, u32[]{:S(2)}) collective-permute-start(f32[80,128]{1,0:T(8,128)S(1)} %get-tuple-element.31.refs_0_.refs_7_), channel_id=1, source_target_pairs={{0,2},{1,3},{2,0},{3,1},{4,6},{5,7},{6,4},{7,5},{8,10},{9,11},{10,... | collective-permute-start | bytes 122888 | tf_op jit(solution)/shard_map/ppermute | solution.py:790
  6.8 0.2 collective-permute-start
  7.0 0.8 %shard_map.65 = (f32[7,3,128,256]{3,2,1,0:T(8,128)S(1)}, f32[2,128,256]{2,1,0:T(8,128)S(1)}, f32[8,128]{1,0:T(8,128)S(1)}, f32[8,256]{1,0:T(8,128)S(1)}) custom-call(f32[16,128]{1,0:T(8,128)S(1)} %get-tuple-element.20.prepared, f32[32,8,128]{2,1,0:T(8,128)S(1)} %get-tuple-element.21.drift_z), custom_call_target="tpu_custom_call" | custom-call | flops 1000000 | bytes 1000000 | tf_op jit(solution)/shard_map/pallas_call | solution.py:813
  7.8 0.7 %shard_map.66 = (f32[4,4,40,128]{3,2,1,0:T(8,128)S(1)}, f32[8,40,128]{2,1,0:T(8,128)S(1)}, f32[8,40,128]{2,1,0:T(8,128)S(1)}, f32[8,40,128]{2,1,0:T(8,128)S(1)}) custom-call(f32[16,128]{1,0:T(8,128)S(1)} %get-tuple-element.20.prepared, f32[8,40,128]{2,1,0:T(8,128)S(1)} %get-tuple-element.25.line_values, f32[10,40,128]{2,1,0:T(8,128)S(1)} %get-tuple-element.26.line_drifts), custom_call_target="tpu_custom_call" | custom-call | flops 1000000 | bytes 1000000 | tf_op jit(solution)/shard_map/pallas_call | solution.py:813
  8.5 0.0 collective-permute-done.2.refs_3_.refs_10_
  8.5 1.8 %collective-permute-done.1.refs_2_.refs_9_ = f32[80,128]{1,0:T(8,128)S(1)} collective-permute-done((f32[80,128]{1,0:T(8,128)S(1)}, f32[80,128]{1,0:T(8,128)S(1)}, u32[]{:S(2)}, u32[]{:S(2)}) %collective-permute-start.1) | collective-permute-done | bytes 40992 | tf_op jit(solution)/shard_map/ppermute | solution.py:790
  10.3 0.5 %collective-permute-done.refs_1_.refs_8_ = f32[80,128]{1,0:T(8,128)S(1)} collective-permute-done((f32[80,128]{1,0:T(8,128)S(1)}, f32[80,128]{1,0:T(8,128)S(1)}, u32[]{:S(2)}, u32[]{:S(2)}) %collective-permute-start) | collective-permute-done | bytes 40992 | tf_op jit(solution)/shard_map/ppermute | solution.py:790
  10.8 0.1 shard_map.68.refs_12_
  10.9 2.7 %collective-permute-start.3 = (f32[80,128]{1,0:T(8,128)S(1)}, f32[80,128]{1,0:T(8,128)S(1)}, u32[]{:S(2)}, u32[]{:S(2)}) collective-permute-start(f32[80,128]{1,0:T(8,128)S(1)} %shard_map.68.refs_12_), channel_id=1, source_target_pairs={{0,4},{1,5},{2,6},{3,7},{4,0},{5,1},{6,2},{7,3},{8,12},{9,13},{10,... | collective-permute-start | bytes 122888 | tf_op jit(solution)/shard_map/ppermute | solution.py:790
  13.5 1.0 %shard_map.67.refs_11_ = f32[2,4,40,128]{3,2,1,0:T(8,128)S(1)} custom-call(f32[16,128]{1,0:T(8,128)S(1)} %get-tuple-element.20.prepared), custom_call_target="tpu_custom_call" | custom-call | flops 1000000 | bytes 1000000 | tf_op jit(solution)/shard_map/pallas_call | solution.py:813
  14.6 1.3 %collective-permute-done.3.refs_13_ = f32[80,128]{1,0:T(8,128)S(1)} collective-permute-done((f32[80,128]{1,0:T(8,128)S(1)}, f32[80,128]{1,0:T(8,128)S(1)}, u32[]{:S(2)}, u32[]{:S(2)}) %collective-permute-start.3) | collective-permute-done | bytes 40992 | tf_op jit(solution)/shard_map/ppermute | solution.py:790
  15.8 0.5 %shard_map.69 = (f32[8,256]{1,0:T(8,128)S(1)}, f32[128,256]{1,0:T(8,128)S(1)}) custom-call(f32[7,3,128,256]{3,2,1,0:T(8,128)S(1)} %get-tuple-element.22.refs_0_, f32[8,128]{1,0:T(8,128)S(1)} %get-tuple-element.23.refs_1_, f32[8,256]{1,0:T(8,128)S(1)} %get-tuple-element.24.refs_4_.refs_2_, f32[8,40,128]{2,1,0:T(8,128)S(1)} %get-tuple-element.27.refs_3_, ...), custom_call_target="tpu_custom_call" | custom-call | flops 1000000 | bytes 1000000 | tf_op jit(solution)/shard_map/pallas_call | solution.py:813
  16.3 0.1 collective-permute-start.6
  16.4 1.6 %collective-permute-start.5 = (f32[8,256]{1,0:T(8,128)S(1)}, f32[8,256]{1,0:T(8,128)S(1)}, u32[]{:S(2)}, u32[]{:S(2)}) collective-permute-start(f32[8,256]{1,0:T(8,128)S(1)} %get-tuple-element.34.refs_0_), channel_id=1, source_target_pairs={{0,16},{8,24},{16,0},{24,8},{1,17},{9,25},{17,1},{25,9},{2,18},{10... | collective-permute-start | bytes 24584 | tf_op jit(solution)/shard_map/ppermute | solution.py:790
  18.0 0.3 %collective-permute-start.4 = (f32[8,256]{1,0:T(8,128)S(1)}, f32[8,256]{1,0:T(8,128)S(1)}, u32[]{:S(2)}, u32[]{:S(2)}) collective-permute-start(f32[8,256]{1,0:T(8,128)S(1)} %get-tuple-element.34.refs_0_), channel_id=1, source_target_pairs={{0,8},{8,0},{16,24},{24,16},{1,9},{9,1},{17,25},{25,17},{2,10},{10... | collective-permute-start | bytes 24584 | tf_op jit(solution)/shard_map/ppermute | solution.py:790
  18.2 1.2 %collective-permute-done.6.refs_3_ = f32[8,256]{1,0:T(8,128)S(1)} collective-permute-done((f32[8,256]{1,0:T(8,128)S(1)}, f32[8,256]{1,0:T(8,128)S(1)}, u32[]{:S(2)}, u32[]{:S(2)}) %collective-permute-start.6) | collective-permute-done | bytes 8224 | tf_op jit(solution)/shard_map/ppermute | solution.py:790
  19.5 0.6 %collective-permute-done.5.refs_2_ = f32[8,256]{1,0:T(8,128)S(1)} collective-permute-done((f32[8,256]{1,0:T(8,128)S(1)}, f32[8,256]{1,0:T(8,128)S(1)}, u32[]{:S(2)}, u32[]{:S(2)}) %collective-permute-start.5) | collective-permute-done | bytes 8224 | tf_op jit(solution)/shard_map/ppermute | solution.py:790
  20.1 0.0 collective-permute-done.4.refs_1_
  20.1 0.0 copy-done
  20.1 0.9 %shard_map.70 = f32[32,8,128]{2,1,0:T(8,128)} custom-call(f32[32,8,128]{2,1,0:T(8,128)S(1)} %copy-done, f32[128,256]{1,0:T(8,128)S(1)} %get-tuple-element.32.doubled, f32[2,128,256]{2,1,0:T(8,128)S(1)} %get-tuple-element.33.ends, f32[8,256]{1,0:T(8,128)S(1)} %get-tuple-element.34.refs_0_, f32[8,256]{1,0:T(8,128)S(1)} %collective-permute-done.4.refs_1_, ...), custom_call_target="tpu_custom_call" | custom-call | flops 1000000 | bytes 1000000 | tf_op jit(solution)/shard_map/pallas_call | solution.py:813
Async XLA Ops:
  0.0 20.1 %copy-start = (f32[32,8,128]{2,1,0:T(8,128)S(1)}, f32[32,8,128]{2,1,0:T(8,128)}, u32[]{:S(2)}) copy-start(f32[32,8,128]{2,1,0:T(8,128)} %density.1) | copy-start | bytes 393220
  2.3 6.2 %collective-permute-start.2 = (f32[80,128]{1,0:T(8,128)S(1)}, f32[80,128]{1,0:T(8,128)S(1)}, u32[]{:S(2)}, u32[]{:S(2)}) collective-permute-start(f32[80,128]{1,0:T(8,128)S(1)} %get-tuple-element.31.refs_0_.refs_7_), channel_id=1, source_target_pairs={{0,3},{1,2},{2,1},{3,0},{4,7},{5,6},{6,5},{7,4},{8,11},{9,10},{10,... | collective-permute-start | bytes 122888 | tf_op jit(solution)/shard_map/ppermute | solution.py:790
  6.3 4.0 %collective-permute-start.1 = (f32[80,128]{1,0:T(8,128)S(1)}, f32[80,128]{1,0:T(8,128)S(1)}, u32[]{:S(2)}, u32[]{:S(2)}) collective-permute-start(f32[80,128]{1,0:T(8,128)S(1)} %get-tuple-element.31.refs_0_.refs_7_), channel_id=1, source_target_pairs={{0,2},{1,3},{2,0},{3,1},{4,6},{5,7},{6,4},{7,5},{8,10},{9,11},{10,... | collective-permute-start | bytes 122888 | tf_op jit(solution)/shard_map/ppermute | solution.py:790
  6.8 4.0 %collective-permute-start = (f32[80,128]{1,0:T(8,128)S(1)}, f32[80,128]{1,0:T(8,128)S(1)}, u32[]{:S(2)}, u32[]{:S(2)}) collective-permute-start(f32[80,128]{1,0:T(8,128)S(1)} %get-tuple-element.31.refs_0_.refs_7_), channel_id=1, source_target_pairs={{0,1},{1,0},{2,3},{3,2},{4,5},{5,4},{6,7},{7,6},{8,9},{9,8},{10,11... | collective-permute-start | bytes 122888 | tf_op jit(solution)/shard_map/ppermute | solution.py:790
  10.9 5.0 %collective-permute-start.3 = (f32[80,128]{1,0:T(8,128)S(1)}, f32[80,128]{1,0:T(8,128)S(1)}, u32[]{:S(2)}, u32[]{:S(2)}) collective-permute-start(f32[80,128]{1,0:T(8,128)S(1)} %shard_map.68.refs_12_), channel_id=1, source_target_pairs={{0,4},{1,5},{2,6},{3,7},{4,0},{5,1},{6,2},{7,3},{8,12},{9,13},{10,... | collective-permute-start | bytes 122888 | tf_op jit(solution)/shard_map/ppermute | solution.py:790
  16.3 3.2 %collective-permute-start.6 = (f32[8,256]{1,0:T(8,128)S(1)}, f32[8,256]{1,0:T(8,128)S(1)}, u32[]{:S(2)}, u32[]{:S(2)}) collective-permute-start(f32[8,256]{1,0:T(8,128)S(1)} %get-tuple-element.34.refs_0_), channel_id=1, source_target_pairs={{0,24},{8,16},{16,8},{24,0},{1,25},{9,17},{17,9},{25,1},{2,26},{10... | collective-permute-start | bytes 24584 | tf_op jit(solution)/shard_map/ppermute | solution.py:790
  16.4 3.7 %collective-permute-start.5 = (f32[8,256]{1,0:T(8,128)S(1)}, f32[8,256]{1,0:T(8,128)S(1)}, u32[]{:S(2)}, u32[]{:S(2)}) collective-permute-start(f32[8,256]{1,0:T(8,128)S(1)} %get-tuple-element.34.refs_0_), channel_id=1, source_target_pairs={{0,16},{8,24},{16,0},{24,8},{1,17},{9,25},{17,1},{25,9},{2,18},{10... | collective-permute-start | bytes 24584 | tf_op jit(solution)/shard_map/ppermute | solution.py:790
  18.0 2.1 %collective-permute-start.4 = (f32[8,256]{1,0:T(8,128)S(1)}, f32[8,256]{1,0:T(8,128)S(1)}, u32[]{:S(2)}, u32[]{:S(2)}) collective-permute-start(f32[8,256]{1,0:T(8,128)S(1)} %get-tuple-element.34.refs_0_), channel_id=1, source_target_pairs={{0,8},{8,0},{16,24},{24,16},{1,9},{9,1},{17,25},{25,17},{2,10},{10... | collective-permute-start | bytes 24584 | tf_op jit(solution)/shard_map/ppermute | solution.py:790

commit v6 on v5

--- a/solution.py
+++ b/solution.py
@@ -660,7 +660,7 @@
     return message[:width], message[width:]
 
 
-def merge_kernel(stride, radix, local, coefs, *refs):
+def merge_kernel(stride, radix, local, facing, coefs, *refs):
     received, message = refs[:radix], refs[-1]
     digit = lax.rem(lax.div(lax.axis_index("gy"), stride), radix)
     first = 0 if local else lax.div(lax.axis_index("gy"), stride) - digit
@@ -670,7 +670,11 @@
     for j in range(1, radix):
         total = merge_values(merged, group[j], total, values[j])
         merged = merge_coefs(merged, group[j])
-    message[...] = jnp.concatenate(total, axis=0)
+    if facing:
+        is_low = lax.axis_index("gy") < stride * radix
+        message[...] = jnp.where(is_low, total[1], total[0])
+    else:
+        message[...] = jnp.concatenate(total, axis=0)
 
 
 def middle_kernel(levels, *refs):
@@ -689,8 +693,15 @@
         (stride, radix), (coefs, received) = levels[number], inputs[number]
         digit = lax.rem(lax.div(lax.axis_index("gy"), stride), radix)
         first = 0 if number == 0 else lax.div(lax.axis_index("gy"), stride) - digit
-        values = [split_message(m) for m in gather_members(received, digit, radix)]
+        members = gather_members(received, digit, radix)
         group = [tuple(coefs[first + j, q] for q in range(4)) for j in range(radix)]
+        if members[0].shape[0] == width:
+            c_last, a_first = group[0][3], group[1][0]
+            inverse = 1.0 / (1.0 - c_last * a_first)
+            below = jnp.where(digit == 0, 0.0, (members[0] + c_last * members[1]) * inverse)
+            above = jnp.where(digit == 0, (members[1] + a_first * members[0]) * inverse, 0.0)
+            continue
+        values = [split_message(m) for m in members]
         lows, highs = chain(group, values, below, above)
         for j in range(radix):
             seen[j, 0] = lows[j]
@@ -876,10 +887,11 @@
         received = exchange(message, "gy", stride, radix)
         line_inputs += [coefs[number]] + received
         if number + 1 < len(y_levels):
+            facing = number + 2 == len(y_levels) and y_levels[-1][1] == 2
             message = call(
-                functools.partial(merge_kernel, stride, radix, number == 0),
+                functools.partial(merge_kernel, stride, radix, number == 0, facing),
                 [coefs[number]] + received + ([packed] if number == 0 else []),
-                shape(2 * width, LANES),
+                shape(width if facing else 2 * width, LANES),
             )
     message, doubled = call(
         functools.partial(middle_kernel, y_levels),

time: 21.1 us -> 20.9 us (level)
    ppermute x7, waiting for transfers between devices: 5.41 us -> 5.2 us  [exchange(): lax.ppermute(message, axis, [(i, i ^ s * stride) for i in devices])]
where the time goes in v6:
time: 20.9 us; the launch traced here: 20.8 us
  starting transfers between devices  9.23 us (44%)
  Pallas kernels  6.3 us (30%)
  waiting for transfers between devices  5.2 us (25%)
    ppermute x7, starting transfers between devices, exchange(): lax.ppermute(message, axis, [(i, i ^ s * stride) for i in devices])  9.23 us
    pallas_call x7, Pallas kernels, call(): pl.pallas_call(kernel, out_shape=outputs, in_specs=in_specs or [vmem] * l...  6.3 us
    ppermute x7, waiting for transfers between devices, exchange(): lax.ppermute(message, axis, [(i, i ^ s * stride) for i in devices])  5.2 us
  transfers between devices with their start and end apart: 7, of which 5 were waited for; matrix products, arithmetic and copies ran while one was open for 0% of the time, Pallas kernels for 12%

profile of v6, /device:TPU:0, one launch (start us, length us, event | category | flops | bytes accessed | tf_op | source)
XLA Modules:
  0.0 20.8 jit_solution(14068023105833155962)
XLA Ops:
  0.0 0.0 copy-start
  0.0 2.3 %shard_map.64 = (f32[80,128]{1,0:T(8,128)S(1)}, f32[8,40,128]{2,1,0:T(8,128)S(1)}, f32[10,40,128]{2,1,0:T(8,128)S(1)}, f32[32,8,128]{2,1,0:T(8,128)S(1)}, f32[16,128]{1,0:T(8,128)S(1)}) custom-call(f32[32,8,128]{2,1,0:T(8,128)} %density.1, f32[1,3]{1,0:T(1,128)} %bitcast.8, f32[3,16]{1,0:T(4,128)} %bitcast.6, f32[1,16]{1,0:T(1,128)} %bitcast.9, ...), custom_call_target="tpu_custom_call" | custom-call | flops 1000000 | bytes 1000000 | tf_op jit(solution)/shard_map/pallas_call | solution.py:824
  2.3 4.0 %collective-permute-start.2 = (f32[80,128]{1,0:T(8,128)S(1)}, f32[80,128]{1,0:T(8,128)S(1)}, u32[]{:S(2)}, u32[]{:S(2)}) collective-permute-start(f32[80,128]{1,0:T(8,128)S(1)} %get-tuple-element.31.refs_0_.refs_7_), channel_id=1, source_target_pairs={{0,3},{1,2},{2,1},{3,0},{4,7},{5,6},{6,5},{7,4},{8,11},{9,10},{10,... | collective-permute-start | bytes 122888 | tf_op jit(solution)/shard_map/ppermute | solution.py:801
  6.3 0.5 %collective-permute-start.1 = (f32[80,128]{1,0:T(8,128)S(1)}, f32[80,128]{1,0:T(8,128)S(1)}, u32[]{:S(2)}, u32[]{:S(2)}) collective-permute-start(f32[80,128]{1,0:T(8,128)S(1)} %get-tuple-element.31.refs_0_.refs_7_), channel_id=1, source_target_pairs={{0,2},{1,3},{2,0},{3,1},{4,6},{5,7},{6,4},{7,5},{8,10},{9,11},{10,... | collective-permute-start | bytes 122888 | tf_op jit(solution)/shard_map/ppermute | solution.py:801
  6.8 0.2 collective-permute-start
  7.0 0.8 %shard_map.65 = (f32[7,3,128,256]{3,2,1,0:T(8,128)S(1)}, f32[2,128,256]{2,1,0:T(8,128)S(1)}, f32[8,128]{1,0:T(8,128)S(1)}, f32[8,256]{1,0:T(8,128)S(1)}) custom-call(f32[16,128]{1,0:T(8,128)S(1)} %get-tuple-element.20.prepared, f32[32,8,128]{2,1,0:T(8,128)S(1)} %get-tuple-element.21.drift_z), custom_call_target="tpu_custom_call" | custom-call | flops 1000000 | bytes 1000000 | tf_op jit(solution)/shard_map/pallas_call | solution.py:824
  7.8 0.7 %shard_map.66 = (f32[4,4,40,128]{3,2,1,0:T(8,128)S(1)}, f32[8,40,128]{2,1,0:T(8,128)S(1)}, f32[8,40,128]{2,1,0:T(8,128)S(1)}, f32[8,40,128]{2,1,0:T(8,128)S(1)}) custom-call(f32[16,128]{1,0:T(8,128)S(1)} %get-tuple-element.20.prepared, f32[8,40,128]{2,1,0:T(8,128)S(1)} %get-tuple-element.25.line_values, f32[10,40,128]{2,1,0:T(8,128)S(1)} %get-tuple-element.26.line_drifts), custom_call_target="tpu_custom_call" | custom-call | flops 1000000 | bytes 1000000 | tf_op jit(solution)/shard_map/pallas_call | solution.py:824
  8.5 0.0 collective-permute-done.2.refs_3_.refs_10_
  8.5 1.8 %collective-permute-done.1.refs_2_.refs_9_ = f32[80,128]{1,0:T(8,128)S(1)} collective-permute-done((f32[80,128]{1,0:T(8,128)S(1)}, f32[80,128]{1,0:T(8,128)S(1)}, u32[]{:S(2)}, u32[]{:S(2)}) %collective-permute-start.1) | collective-permute-done | bytes 40992 | tf_op jit(solution)/shard_map/ppermute | solution.py:801
  10.3 0.5 %collective-permute-done.refs_1_.refs_8_ = f32[80,128]{1,0:T(8,128)S(1)} collective-permute-done((f32[80,128]{1,0:T(8,128)S(1)}, f32[80,128]{1,0:T(8,128)S(1)}, u32[]{:S(2)}, u32[]{:S(2)}) %collective-permute-start) | collective-permute-done | bytes 40992 | tf_op jit(solution)/shard_map/ppermute | solution.py:801
  10.8 0.1 shard_map.68.refs_12_
  10.9 2.7 %collective-permute-start.3 = (f32[40,128]{1,0:T(8,128)S(1)}, f32[40,128]{1,0:T(8,128)S(1)}, u32[]{:S(2)}, u32[]{:S(2)}) collective-permute-start(f32[40,128]{1,0:T(8,128)S(1)} %shard_map.68.refs_12_), channel_id=1, source_target_pairs={{0,4},{1,5},{2,6},{3,7},{4,0},{5,1},{6,2},{7,3},{8,12},{9,13},{10,... | collective-permute-start | bytes 61448 | tf_op jit(solution)/shard_map/ppermute | solution.py:801
  13.5 1.0 %shard_map.67.refs_11_ = f32[2,4,40,128]{3,2,1,0:T(8,128)S(1)} custom-call(f32[16,128]{1,0:T(8,128)S(1)} %get-tuple-element.20.prepared), custom_call_target="tpu_custom_call" | custom-call | flops 1000000 | bytes 1000000 | tf_op jit(solution)/shard_map/pallas_call | solution.py:824
  14.6 1.1 %collective-permute-done.3.refs_13_ = f32[40,128]{1,0:T(8,128)S(1)} collective-permute-done((f32[40,128]{1,0:T(8,128)S(1)}, f32[40,128]{1,0:T(8,128)S(1)}, u32[]{:S(2)}, u32[]{:S(2)}) %collective-permute-start.3) | collective-permute-done | bytes 20512 | tf_op jit(solution)/shard_map/ppermute | solution.py:801
  15.6 0.5 %shard_map.69 = (f32[8,256]{1,0:T(8,128)S(1)}, f32[128,256]{1,0:T(8,128)S(1)}) custom-call(f32[7,3,128,256]{3,2,1,0:T(8,128)S(1)} %get-tuple-element.22.refs_0_, f32[8,128]{1,0:T(8,128)S(1)} %get-tuple-element.23.refs_1_, f32[8,256]{1,0:T(8,128)S(1)} %get-tuple-element.24.refs_4_.refs_2_, f32[8,40,128]{2,1,0:T(8,128)S(1)} %get-tuple-element.27.refs_3_, ...), custom_call_target="tpu_custom_call" | custom-call | flops 1000000 | bytes 1000000 | tf_op jit(solution)/shard_map/pallas_call | solution.py:824
  16.1 0.1 collective-permute-start.6
  16.2 1.6 %collective-permute-start.5 = (f32[8,256]{1,0:T(8,128)S(1)}, f32[8,256]{1,0:T(8,128)S(1)}, u32[]{:S(2)}, u32[]{:S(2)}) collective-permute-start(f32[8,256]{1,0:T(8,128)S(1)} %get-tuple-element.34.refs_0_), channel_id=1, source_target_pairs={{0,16},{8,24},{16,0},{24,8},{1,17},{9,25},{17,1},{25,9},{2,18},{10... | collective-permute-start | bytes 24584 | tf_op jit(solution)/shard_map/ppermute | solution.py:801
  17.7 0.3 %collective-permute-start.4 = (f32[8,256]{1,0:T(8,128)S(1)}, f32[8,256]{1,0:T(8,128)S(1)}, u32[]{:S(2)}, u32[]{:S(2)}) collective-permute-start(f32[8,256]{1,0:T(8,128)S(1)} %get-tuple-element.34.refs_0_), channel_id=1, source_target_pairs={{0,8},{8,0},{16,24},{24,16},{1,9},{9,1},{17,25},{25,17},{2,10},{10... | collective-permute-start | bytes 24584 | tf_op jit(solution)/shard_map/ppermute | solution.py:801
  18.0 1.2 %collective-permute-done.6.refs_3_ = f32[8,256]{1,0:T(8,128)S(1)} collective-permute-done((f32[8,256]{1,0:T(8,128)S(1)}, f32[8,256]{1,0:T(8,128)S(1)}, u32[]{:S(2)}, u32[]{:S(2)}) %collective-permute-start.6) | collective-permute-done | bytes 8224 | tf_op jit(solution)/shard_map/ppermute | solution.py:801
  19.2 0.6 %collective-permute-done.5.refs_2_ = f32[8,256]{1,0:T(8,128)S(1)} collective-permute-done((f32[8,256]{1,0:T(8,128)S(1)}, f32[8,256]{1,0:T(8,128)S(1)}, u32[]{:S(2)}, u32[]{:S(2)}) %collective-permute-start.5) | collective-permute-done | bytes 8224 | tf_op jit(solution)/shard_map/ppermute | solution.py:801
  19.9 0.0 collective-permute-done.4.refs_1_
  19.9 0.0 copy-done
  19.9 0.9 %shard_map.70 = f32[32,8,128]{2,1,0:T(8,128)} custom-call(f32[32,8,128]{2,1,0:T(8,128)S(1)} %copy-done, f32[128,256]{1,0:T(8,128)S(1)} %get-tuple-element.32.doubled, f32[2,128,256]{2,1,0:T(8,128)S(1)} %get-tuple-element.33.ends, f32[8,256]{1,0:T(8,128)S(1)} %get-tuple-element.34.refs_0_, f32[8,256]{1,0:T(8,128)S(1)} %collective-permute-done.4.refs_1_, ...), custom_call_target="tpu_custom_call" | custom-call | flops 1000000 | bytes 1000000 | tf_op jit(solution)/shard_map/pallas_call | solution.py:824
Async XLA Ops:
  0.0 19.9 %copy-start = (f32[32,8,128]{2,1,0:T(8,128)S(1)}, f32[32,8,128]{2,1,0:T(8,128)}, u32[]{:S(2)}) copy-start(f32[32,8,128]{2,1,0:T(8,128)} %density.1) | copy-start | bytes 393220
  2.3 6.2 %collective-permute-start.2 = (f32[80,128]{1,0:T(8,128)S(1)}, f32[80,128]{1,0:T(8,128)S(1)}, u32[]{:S(2)}, u32[]{:S(2)}) collective-permute-start(f32[80,128]{1,0:T(8,128)S(1)} %get-tuple-element.31.refs_0_.refs_7_), channel_id=1, source_target_pairs={{0,3},{1,2},{2,1},{3,0},{4,7},{5,6},{6,5},{7,4},{8,11},{9,10},{10,... | collective-permute-start | bytes 122888 | tf_op jit(solution)/shard_map/ppermute | solution.py:801
  6.3 4.0 %collective-permute-start.1 = (f32[80,128]{1,0:T(8,128)S(1)}, f32[80,128]{1,0:T(8,128)S(1)}, u32[]{:S(2)}, u32[]{:S(2)}) collective-permute-start(f32[80,128]{1,0:T(8,128)S(1)} %get-tuple-element.31.refs_0_.refs_7_), channel_id=1, source_target_pairs={{0,2},{1,3},{2,0},{3,1},{4,6},{5,7},{6,4},{7,5},{8,10},{9,11},{10,... | collective-permute-start | bytes 122888 | tf_op jit(solution)/shard_map/ppermute | solution.py:801
  6.8 4.0 %collective-permute-start = (f32[80,128]{1,0:T(8,128)S(1)}, f32[80,128]{1,0:T(8,128)S(1)}, u32[]{:S(2)}, u32[]{:S(2)}) collective-permute-start(f32[80,128]{1,0:T(8,128)S(1)} %get-tuple-element.31.refs_0_.refs_7_), channel_id=1, source_target_pairs={{0,1},{1,0},{2,3},{3,2},{4,5},{5,4},{6,7},{7,6},{8,9},{9,8},{10,11... | collective-permute-start | bytes 122888 | tf_op jit(solution)/shard_map/ppermute | solution.py:801
  10.9 4.7 %collective-permute-start.3 = (f32[40,128]{1,0:T(8,128)S(1)}, f32[40,128]{1,0:T(8,128)S(1)}, u32[]{:S(2)}, u32[]{:S(2)}) collective-permute-start(f32[40,128]{1,0:T(8,128)S(1)} %shard_map.68.refs_12_), channel_id=1, source_target_pairs={{0,4},{1,5},{2,6},{3,7},{4,0},{5,1},{6,2},{7,3},{8,12},{9,13},{10,... | collective-permute-start | bytes 61448 | tf_op jit(solution)/shard_map/ppermute | solution.py:801
  16.1 3.2 %collective-permute-start.6 = (f32[8,256]{1,0:T(8,128)S(1)}, f32[8,256]{1,0:T(8,128)S(1)}, u32[]{:S(2)}, u32[]{:S(2)}) collective-permute-start(f32[8,256]{1,0:T(8,128)S(1)} %get-tuple-element.34.refs_0_), channel_id=1, source_target_pairs={{0,24},{8,16},{16,8},{24,0},{1,25},{9,17},{17,9},{25,1},{2,26},{10... | collective-permute-start | bytes 24584 | tf_op jit(solution)/shard_map/ppermute | solution.py:801
  16.2 3.7 %collective-permute-start.5 = (f32[8,256]{1,0:T(8,128)S(1)}, f32[8,256]{1,0:T(8,128)S(1)}, u32[]{:S(2)}, u32[]{:S(2)}) collective-permute-start(f32[8,256]{1,0:T(8,128)S(1)} %get-tuple-element.34.refs_0_), channel_id=1, source_target_pairs={{0,16},{8,24},{16,0},{24,8},{1,17},{9,25},{17,1},{25,9},{2,18},{10... | collective-permute-start | bytes 24584 | tf_op jit(solution)/shard_map/ppermute | solution.py:801
  17.7 2.1 %collective-permute-start.4 = (f32[8,256]{1,0:T(8,128)S(1)}, f32[8,256]{1,0:T(8,128)S(1)}, u32[]{:S(2)}, u32[]{:S(2)}) collective-permute-start(f32[8,256]{1,0:T(8,128)S(1)} %get-tuple-element.34.refs_0_), channel_id=1, source_target_pairs={{0,8},{8,0},{16,24},{24,16},{1,9},{9,1},{17,25},{25,17},{2,10},{10... | collective-permute-start | bytes 24584 | tf_op jit(solution)/shard_map/ppermute | solution.py:801

commit v7 on v6

--- a/solution.py
+++ b/solution.py
@@ -10,6 +10,7 @@
 HALF_LIMIT = 600.0
 LANES = 128
 ROWS = 8
+ABOVE, BELOW = 127, 31
 VMEM_LIMIT = 48 * 1024 * 1024
 
 
@@ -91,7 +92,7 @@
 def outer_z_rows(params, maps, z_start, size_z, total_z):
     row = iota((size_z, LANES), 0)
     return z_rows(
-        params, maps, jnp.where(row == 0, z_start + size_z, z_start - 1), total_z
+        params, maps, jnp.where(row == BELOW, z_start - 1, z_start + size_z), total_z
     )
 
 
@@ -106,14 +107,14 @@
 
 
 def xz_rows(params, maps, size_x, z_start, size_z, total_z):
-    row = iota((2 * size_x, LANES), 0)
-    x_coord = coordinate(row % size_x, size_x)
-    z_coord = coordinate(jnp.where(row < size_x, z_start - 1, z_start + size_z), total_z)
+    row = iota((BELOW + 1 + size_x, LANES), 0)
+    x_coord = coordinate(jnp.where(row < size_x, row, row - BELOW - 1), size_x)
+    z_coord = coordinate(jnp.where(row > BELOW, z_start - 1, z_start + size_z), total_z)
     part = slope(params, x_coord, 0) + slope(params, z_coord, 2)
     both = bump(params, x_coord, 0) * bump(params, z_coord, 2)
     both = both * jnp.where(first_term(maps), 1.0, part)
     return jnp.concatenate(
-        [both, jnp.zeros((LANES - 2 * size_x, LANES), jnp.float32)], axis=0
+        [both, jnp.zeros((LANES - BELOW - 1 - size_x, LANES), jnp.float32)], axis=0
     )
 
 
@@ -122,19 +123,16 @@
 
 
 def pack_planes(planes):
-    lane = iota(planes[0].shape, 1)
-    first = last = jnp.zeros(planes[0].shape, jnp.float32)
-    for i, plane in enumerate(planes):
-        turned = roll(plane, i + 1, 1)
-        first = jnp.where(lane == i, turned, first)
-        last = jnp.where(lane == i + 1, turned, last)
-    return first + roll(last, len(planes) - 1, 1)
-
-
-def lines_of(planes, size_x, side):
+    turned = [roll(plane, i + 1, 1) for i, plane in enumerate(planes)]
+    while len(turned) > 1:
+        turned = [sum(turned[i : i + 2]) for i in range(0, len(turned), 2)]
+    return turned[0]
+
+
+def lines_of(planes, size_x, first_lane):
     group = LANES // size_x
     place = iota((1, LANES), 1) // size_x
-    turned = [roll(planes, (q - side) * size_x, 1) for q in range(group)]
+    turned = [roll(planes, q * size_x - first_lane, 1) for q in range(group)]
     rows = []
     for first in range(0, planes.shape[0], group):
         row = turned[0][first : first + 1]
@@ -181,8 +179,29 @@
     )
 
 
+def merge(low, high, low_values, high_values):
+    return merge_coefs(low, high), merge_values(low, high, low_values, high_values)
+
+
+def meet(low, high, below, above):
+    (_, _, a_last, c_last), (_, r_last) = low
+    (a_first, c_first, _, _), (r_first, _) = high
+    inverse = 1.0 / (1.0 - c_last * a_first)
+    upper = r_first + c_first * above
+    left = (r_last + a_last * below + c_last * upper) * inverse
+    return left, upper + a_first * left
+
+
 def chain(coefs, values, below, above):
     count = len(coefs)
+    if count == 4:
+        halves = [merge(coefs[j], coefs[j + 1], values[j], values[j + 1]) for j in (0, 2)]
+        left, right = meet(halves[0], halves[1], below, above)
+        seen = [
+            meet((coefs[j], values[j]), (coefs[j + 1], values[j + 1]), low, high)
+            for j, low, high in ((0, below, right), (2, left, above))
+        ]
+        return [below, seen[0][0], left, seen[1][0]], [seen[0][1], right, seen[1][1], above]
     held, slope = below, None
     befores, firsts = [], []
     for j in range(count):
@@ -377,9 +396,12 @@
     at_low, at_high = sublane == 0, sublane == size_y - 1
     row_source = jnp.where(at_low, up, jnp.where(at_high, down, 0.0))
     total = total + jnp.where(at_low, 0.0, up) + jnp.where(at_high, 0.0, down)
-    up, down = roll((d2 + drift_z) * rho, 1, 2), roll((d2 - drift_z) * rho, -1, 2)
+    up, down = (d2 + drift_z) * rho, (d2 - drift_z) * rho
+    plane_source = jnp.where(
+        lane == ABOVE, up, jnp.where(lane == BELOW, roll(down, BELOW, 2), 0.0)
+    )
+    up, down = roll(up, 1, 2), roll(down, -1, 2)
     at_low, at_high = lane == 0, lane == size_z - 1
-    plane_source = jnp.where(at_low, up, jnp.where(at_high, down, 0.0))
     total = total + jnp.where(at_low, 0.0, up) + jnp.where(at_high, 0.0, down)
 
     source = jnp.concatenate([total, row_source, plane_source], axis=1)
@@ -427,9 +449,9 @@
     pushed_up = solved[:, size_y, :] / (d1 + line_drift[size_y][:size_x])
     pushed_down = solved[:, 2 * size_y - 1, :] / (d1 - line_drift[1][:size_x])
     blank = jnp.zeros((1, LANES), jnp.float32)
-    width = size_x + ROWS
-    message[:width] = r_first + with_extra(pushed_down, blank)
-    message[width:] = r_last + with_extra(pushed_up, blank)
+    message[...] = join_message(
+        r_first + with_extra(pushed_down, blank), r_last + with_extra(pushed_up, blank)
+    )
 
 
 def line_factors(line_drift, j, size_y, d1, y_start, total_y):
@@ -593,8 +615,9 @@
     divisors = []
     for i in range(size_x):
         plane = drift_z[i]
+        factor = jnp.where(lane == ABOVE, d2 + plane, d2 - roll(plane, BELOW, 1))
         divisors.append(
-            1.0 / jnp.where(lane == 0, d2 + roll(plane, 1, 1), d2 - roll(plane, -1, 1))
+            jnp.where((lane == ABOVE) | (lane == BELOW), 1.0 / factor, 0.0)
         )
     pushes[...] = pack_planes(divisors)
     x_bump, x_part = x_factors(params, maps, size_x)
@@ -611,8 +634,8 @@
     scale = 1.0 / (1.0 + 2.0 * d2)
     row = iota(inner.shape, 0)
     low, high = row == 0, row == size_z - 1
-    before = jnp.where(low, outer[size_z - 1 :], turn(inner, 1))
-    after = jnp.where(high, outer[:1], turn(inner, -1))
+    before = jnp.where(low, outer[BELOW : BELOW + 1], turn(inner, 1))
+    after = jnp.where(high, outer[ABOVE : ABOVE + 1], turn(inner, -1))
     below = jnp.where(low & (z_start == 0), 0.0, (d2 + before) * scale)
     above = jnp.where(high & (z_start + size_z == total_z), 0.0, (d2 - after) * scale)
     stride, level = 1, 0
@@ -655,9 +678,18 @@
     ]
 
 
+def join_message(first, last):
+    size_x = first.shape[0] - ROWS
+    extra = jnp.where(iota((ROWS, LANES), 0) == 0, first[size_x:], last[size_x:])
+    return jnp.concatenate([first[:size_x], last[:size_x], extra], axis=0)
+
+
 def split_message(message):
-    width = message.shape[0] // 2
-    return message[:width], message[width:]
+    size_x = (message.shape[0] - ROWS) // 2
+    return (
+        with_extra(message[:size_x], message[2 * size_x : 2 * size_x + 1]),
+        with_extra(message[size_x : 2 * size_x], message[2 * size_x + 1 : 2 * size_x + 2]),
+    )
 
 
 def merge_kernel(stride, radix, local, facing, coefs, *refs):
@@ -674,7 +706,7 @@
         is_low = lax.axis_index("gy") < stride * radix
         message[...] = jnp.where(is_low, total[1], total[0])
     else:
-        message[...] = jnp.concatenate(total, axis=0)
+        message[...] = join_message(*total)
 
 
 def middle_kernel(levels, *refs):
@@ -724,8 +756,8 @@
         stride, level = stride * 2, level + 1
     doubled[...] = values
     message[...] = packed[...]
-    message[0:1] = values[:1] + lines_of(pushed, size_x, 0)
-    message[1:2] = values[-1:] + lines_of(pushed, size_x, 1)
+    message[0:1] = values[:1] + lines_of(pushed, size_x, BELOW + 1)
+    message[1:2] = values[-1:] + lines_of(pushed, size_x, 0)
 
 
 def merge_z(low, high):
@@ -844,7 +876,7 @@
         functools.partial(start_kernel, extent_y, extent_z),
         raw,
         (
-            shape(2 * width, LANES),
+            shape(width + size_x, LANES),
             shape(*wide),
             shape(size_y + 2, width, LANES),
             shape(size_x, size_y, LANES),
@@ -891,7 +923,7 @@
             message = call(
                 functools.partial(merge_kernel, stride, radix, number == 0, facing),
                 [coefs[number]] + received + ([packed] if number == 0 else []),
-                shape(width if facing else 2 * width, LANES),
+                shape(width if facing else width + size_x, LANES),
             )
     message, doubled = call(
         functools.partial(middle_kernel, y_levels),

time: 20.9 us -> 20.7 us (level)
  no operation moved by 1% of the time
where the time goes in v7:
time: 20.7 us; the launch traced here: 20.6 us
  starting transfers between devices  9.23 us (45%)
  Pallas kernels  6.15 us (30%)
  waiting for transfers between devices  5.14 us (25%)
    ppermute x7, starting transfers between devices, exchange(): lax.ppermute(message, axis, [(i, i ^ s * stride) for i in devices])  9.23 us
    pallas_call x7, Pallas kernels, call(): pl.pallas_call(kernel, out_shape=outputs, in_specs=in_specs or [vmem] * l...  6.15 us
    ppermute x7, waiting for transfers between devices, exchange(): lax.ppermute(message, axis, [(i, i ^ s * stride) for i in devices])  5.14 us
  transfers between devices with their start and end apart: 7, of which 5 were waited for; matrix products, arithmetic and copies ran while one was open for 0% of the time, Pallas kernels for 12%

profile of v7, /device:TPU:0, one launch (start us, length us, event | category | flops | bytes accessed | tf_op | source)
XLA Modules:
  0.0 20.6 jit_solution(626743657241044121)
XLA Ops:
  0.0 0.0 copy-start
  0.0 2.2 %shard_map.64 = (f32[72,128]{1,0:T(8,128)S(1)}, f32[8,40,128]{2,1,0:T(8,128)S(1)}, f32[10,40,128]{2,1,0:T(8,128)S(1)}, f32[32,8,128]{2,1,0:T(8,128)S(1)}, f32[16,128]{1,0:T(8,128)S(1)}) custom-call(f32[32,8,128]{2,1,0:T(8,128)} %density.1, f32[1,3]{1,0:T(1,128)} %bitcast.8, f32[3,16]{1,0:T(4,128)} %bitcast.6, f32[1,16]{1,0:T(1,128)} %bitcast.9, ...), custom_call_target="tpu_custom_call" | custom-call | flops 1000000 | bytes 1000000 | tf_op jit(solution)/shard_map/pallas_call | solution.py:856
  2.2 4.0 %collective-permute-start.2 = (f32[72,128]{1,0:T(8,128)S(1)}, f32[72,128]{1,0:T(8,128)S(1)}, u32[]{:S(2)}, u32[]{:S(2)}) collective-permute-start(f32[72,128]{1,0:T(8,128)S(1)} %get-tuple-element.31.refs_0_.refs_7_), channel_id=1, source_target_pairs={{0,3},{1,2},{2,1},{3,0},{4,7},{5,6},{6,5},{7,4},{8,11},{9,10},{10,... | collective-permute-start | bytes 110600 | tf_op jit(solution)/shard_map/ppermute | solution.py:833
  6.2 0.4 %collective-permute-start.1 = (f32[72,128]{1,0:T(8,128)S(1)}, f32[72,128]{1,0:T(8,128)S(1)}, u32[]{:S(2)}, u32[]{:S(2)}) collective-permute-start(f32[72,128]{1,0:T(8,128)S(1)} %get-tuple-element.31.refs_0_.refs_7_), channel_id=1, source_target_pairs={{0,2},{1,3},{2,0},{3,1},{4,6},{5,7},{6,4},{7,5},{8,10},{9,11},{10,... | collective-permute-start | bytes 110600 | tf_op jit(solution)/shard_map/ppermute | solution.py:833
  6.7 0.2 collective-permute-start
  6.9 0.8 %shard_map.65 = (f32[7,3,128,256]{3,2,1,0:T(8,128)S(1)}, f32[2,128,256]{2,1,0:T(8,128)S(1)}, f32[8,128]{1,0:T(8,128)S(1)}, f32[8,256]{1,0:T(8,128)S(1)}) custom-call(f32[16,128]{1,0:T(8,128)S(1)} %get-tuple-element.20.prepared, f32[32,8,128]{2,1,0:T(8,128)S(1)} %get-tuple-element.21.drift_z), custom_call_target="tpu_custom_call" | custom-call | flops 1000000 | bytes 1000000 | tf_op jit(solution)/shard_map/pallas_call | solution.py:856
  7.7 0.7 %shard_map.66 = (f32[4,4,40,128]{3,2,1,0:T(8,128)S(1)}, f32[8,40,128]{2,1,0:T(8,128)S(1)}, f32[8,40,128]{2,1,0:T(8,128)S(1)}, f32[8,40,128]{2,1,0:T(8,128)S(1)}) custom-call(f32[16,128]{1,0:T(8,128)S(1)} %get-tuple-element.20.prepared, f32[8,40,128]{2,1,0:T(8,128)S(1)} %get-tuple-element.25.line_values, f32[10,40,128]{2,1,0:T(8,128)S(1)} %get-tuple-element.26.line_drifts), custom_call_target="tpu_custom_call" | custom-call | flops 1000000 | bytes 1000000 | tf_op jit(solution)/shard_map/pallas_call | solution.py:856
  8.4 0.0 collective-permute-done.2.refs_3_.refs_10_
  8.4 1.8 %collective-permute-done.1.refs_2_.refs_9_ = f32[72,128]{1,0:T(8,128)S(1)} collective-permute-done((f32[72,128]{1,0:T(8,128)S(1)}, f32[72,128]{1,0:T(8,128)S(1)}, u32[]{:S(2)}, u32[]{:S(2)}) %collective-permute-start.1) | collective-permute-done | bytes 36896 | tf_op jit(solution)/shard_map/ppermute | solution.py:833
  10.2 0.4 %collective-permute-done.refs_1_.refs_8_ = f32[72,128]{1,0:T(8,128)S(1)} collective-permute-done((f32[72,128]{1,0:T(8,128)S(1)}, f32[72,128]{1,0:T(8,128)S(1)}, u32[]{:S(2)}, u32[]{:S(2)}) %collective-permute-start) | collective-permute-done | bytes 36896 | tf_op jit(solution)/shard_map/ppermute | solution.py:833
  10.6 0.1 shard_map.68.refs_12_
  10.7 2.7 %collective-permute-start.3 = (f32[40,128]{1,0:T(8,128)S(1)}, f32[40,128]{1,0:T(8,128)S(1)}, u32[]{:S(2)}, u32[]{:S(2)}) collective-permute-start(f32[40,128]{1,0:T(8,128)S(1)} %shard_map.68.refs_12_), channel_id=1, source_target_pairs={{0,4},{1,5},{2,6},{3,7},{4,0},{5,1},{6,2},{7,3},{8,12},{9,13},{10,... | collective-permute-start | bytes 61448 | tf_op jit(solution)/shard_map/ppermute | solution.py:833
  13.4 1.0 %shard_map.67.refs_11_ = f32[2,4,40,128]{3,2,1,0:T(8,128)S(1)} custom-call(f32[16,128]{1,0:T(8,128)S(1)} %get-tuple-element.20.prepared), custom_call_target="tpu_custom_call" | custom-call | flops 1000000 | bytes 1000000 | tf_op jit(solution)/shard_map/pallas_call | solution.py:856
  14.4 1.0 %collective-permute-done.3.refs_13_ = f32[40,128]{1,0:T(8,128)S(1)} collective-permute-done((f32[40,128]{1,0:T(8,128)S(1)}, f32[40,128]{1,0:T(8,128)S(1)}, u32[]{:S(2)}, u32[]{:S(2)}) %collective-permute-start.3) | collective-permute-done | bytes 20512 | tf_op jit(solution)/shard_map/ppermute | solution.py:833
  15.4 0.4 %shard_map.69 = (f32[8,256]{1,0:T(8,128)S(1)}, f32[128,256]{1,0:T(8,128)S(1)}) custom-call(f32[7,3,128,256]{3,2,1,0:T(8,128)S(1)} %get-tuple-element.22.refs_0_, f32[8,128]{1,0:T(8,128)S(1)} %get-tuple-element.23.refs_1_, f32[8,256]{1,0:T(8,128)S(1)} %get-tuple-element.24.refs_4_.refs_2_, f32[8,40,128]{2,1,0:T(8,128)S(1)} %get-tuple-element.27.refs_3_, ...), custom_call_target="tpu_custom_call" | custom-call | flops 1000000 | bytes 1000000 | tf_op jit(solution)/shard_map/pallas_call | solution.py:856
  15.9 0.1 collective-permute-start.6
  16.0 1.6 %collective-permute-start.5 = (f32[8,256]{1,0:T(8,128)S(1)}, f32[8,256]{1,0:T(8,128)S(1)}, u32[]{:S(2)}, u32[]{:S(2)}) collective-permute-start(f32[8,256]{1,0:T(8,128)S(1)} %get-tuple-element.34.refs_0_), channel_id=1, source_target_pairs={{0,16},{8,24},{16,0},{24,8},{1,17},{9,25},{17,1},{25,9},{2,18},{10... | collective-permute-start | bytes 24584 | tf_op jit(solution)/shard_map/ppermute | solution.py:833
  17.6 0.3 %collective-permute-start.4 = (f32[8,256]{1,0:T(8,128)S(1)}, f32[8,256]{1,0:T(8,128)S(1)}, u32[]{:S(2)}, u32[]{:S(2)}) collective-permute-start(f32[8,256]{1,0:T(8,128)S(1)} %get-tuple-element.34.refs_0_), channel_id=1, source_target_pairs={{0,8},{8,0},{16,24},{24,16},{1,9},{9,1},{17,25},{25,17},{2,10},{10... | collective-permute-start | bytes 24584 | tf_op jit(solution)/shard_map/ppermute | solution.py:833
  17.8 1.2 %collective-permute-done.6.refs_3_ = f32[8,256]{1,0:T(8,128)S(1)} collective-permute-done((f32[8,256]{1,0:T(8,128)S(1)}, f32[8,256]{1,0:T(8,128)S(1)}, u32[]{:S(2)}, u32[]{:S(2)}) %collective-permute-start.6) | collective-permute-done | bytes 8224 | tf_op jit(solution)/shard_map/ppermute | solution.py:833
  19.1 0.6 %collective-permute-done.5.refs_2_ = f32[8,256]{1,0:T(8,128)S(1)} collective-permute-done((f32[8,256]{1,0:T(8,128)S(1)}, f32[8,256]{1,0:T(8,128)S(1)}, u32[]{:S(2)}, u32[]{:S(2)}) %collective-permute-start.5) | collective-permute-done | bytes 8224 | tf_op jit(solution)/shard_map/ppermute | solution.py:833
  19.7 0.0 collective-permute-done.4.refs_1_
  19.7 0.0 copy-done
  19.7 0.9 %shard_map.70 = f32[32,8,128]{2,1,0:T(8,128)} custom-call(f32[32,8,128]{2,1,0:T(8,128)S(1)} %copy-done, f32[128,256]{1,0:T(8,128)S(1)} %get-tuple-element.32.doubled, f32[2,128,256]{2,1,0:T(8,128)S(1)} %get-tuple-element.33.ends, f32[8,256]{1,0:T(8,128)S(1)} %get-tuple-element.34.refs_0_, f32[8,256]{1,0:T(8,128)S(1)} %collective-permute-done.4.refs_1_, ...), custom_call_target="tpu_custom_call" | custom-call | flops 1000000 | bytes 1000000 | tf_op jit(solution)/shard_map/pallas_call | solution.py:856
Async XLA Ops:
  0.0 19.7 %copy-start = (f32[32,8,128]{2,1,0:T(8,128)S(1)}, f32[32,8,128]{2,1,0:T(8,128)}, u32[]{:S(2)}) copy-start(f32[32,8,128]{2,1,0:T(8,128)} %density.1) | copy-start | bytes 393220
  2.2 6.2 %collective-permute-start.2 = (f32[72,128]{1,0:T(8,128)S(1)}, f32[72,128]{1,0:T(8,128)S(1)}, u32[]{:S(2)}, u32[]{:S(2)}) collective-permute-start(f32[72,128]{1,0:T(8,128)S(1)} %get-tuple-element.31.refs_0_.refs_7_), channel_id=1, source_target_pairs={{0,3},{1,2},{2,1},{3,0},{4,7},{5,6},{6,5},{7,4},{8,11},{9,10},{10,... | collective-permute-start | bytes 110600 | tf_op jit(solution)/shard_map/ppermute | solution.py:833
  6.2 4.0 %collective-permute-start.1 = (f32[72,128]{1,0:T(8,128)S(1)}, f32[72,128]{1,0:T(8,128)S(1)}, u32[]{:S(2)}, u32[]{:S(2)}) collective-permute-start(f32[72,128]{1,0:T(8,128)S(1)} %get-tuple-element.31.refs_0_.refs_7_), channel_id=1, source_target_pairs={{0,2},{1,3},{2,0},{3,1},{4,6},{5,7},{6,4},{7,5},{8,10},{9,11},{10,... | collective-permute-start | bytes 110600 | tf_op jit(solution)/shard_map/ppermute | solution.py:833
  6.7 4.0 %collective-permute-start = (f32[72,128]{1,0:T(8,128)S(1)}, f32[72,128]{1,0:T(8,128)S(1)}, u32[]{:S(2)}, u32[]{:S(2)}) collective-permute-start(f32[72,128]{1,0:T(8,128)S(1)} %get-tuple-element.31.refs_0_.refs_7_), channel_id=1, source_target_pairs={{0,1},{1,0},{2,3},{3,2},{4,5},{5,4},{6,7},{7,6},{8,9},{9,8},{10,11... | collective-permute-start | bytes 110600 | tf_op jit(solution)/shard_map/ppermute | solution.py:833
  10.7 4.7 %collective-permute-start.3 = (f32[40,128]{1,0:T(8,128)S(1)}, f32[40,128]{1,0:T(8,128)S(1)}, u32[]{:S(2)}, u32[]{:S(2)}) collective-permute-start(f32[40,128]{1,0:T(8,128)S(1)} %shard_map.68.refs_12_), channel_id=1, source_target_pairs={{0,4},{1,5},{2,6},{3,7},{4,0},{5,1},{6,2},{7,3},{8,12},{9,13},{10,... | collective-permute-start | bytes 61448 | tf_op jit(solution)/shard_map/ppermute | solution.py:833
  15.9 3.2 %collective-permute-start.6 = (f32[8,256]{1,0:T(8,128)S(1)}, f32[8,256]{1,0:T(8,128)S(1)}, u32[]{:S(2)}, u32[]{:S(2)}) collective-permute-start(f32[8,256]{1,0:T(8,128)S(1)} %get-tuple-element.34.refs_0_), channel_id=1, source_target_pairs={{0,24},{8,16},{16,8},{24,0},{1,25},{9,17},{17,9},{25,1},{2,26},{10... | collective-permute-start | bytes 24584 | tf_op jit(solution)/shard_map/ppermute | solution.py:833
  16.0 3.7 %collective-permute-start.5 = (f32[8,256]{1,0:T(8,128)S(1)}, f32[8,256]{1,0:T(8,128)S(1)}, u32[]{:S(2)}, u32[]{:S(2)}) collective-permute-start(f32[8,256]{1,0:T(8,128)S(1)} %get-tuple-element.34.refs_0_), channel_id=1, source_target_pairs={{0,16},{8,24},{16,0},{24,8},{1,17},{9,25},{17,1},{25,9},{2,18},{10... | collective-permute-start | bytes 24584 | tf_op jit(solution)/shard_map/ppermute | solution.py:833
  17.6 2.1 %collective-permute-start.4 = (f32[8,256]{1,0:T(8,128)S(1)}, f32[8,256]{1,0:T(8,128)S(1)}, u32[]{:S(2)}, u32[]{:S(2)}) collective-permute-start(f32[8,256]{1,0:T(8,128)S(1)} %get-tuple-element.34.refs_0_), channel_id=1, source_target_pairs={{0,8},{8,0},{16,24},{24,16},{1,9},{9,1},{17,25},{25,17},{2,10},{10... | collective-permute-start | bytes 24584 | tf_op jit(solution)/shard_map/ppermute | solution.py:833

commit v8 on v7

--- a/solution.py
+++ b/solution.py
@@ -604,7 +604,29 @@
                 coefs[number, q] = group[q]
 
 
-def z_coef_kernel(sizes, maps, prepared, drift_z, steps, ends, pushes, packed):
+def double_coefs(below, above, scale, steps=None):
+    size_z = below.shape[0]
+    row = iota(below.shape, 0)
+    stride, level = 1, 0
+    while stride < size_z:
+        low, high = row < stride, row >= size_z - stride
+        low_a = jnp.where(low, 1.0, turn(below, stride))
+        low_c = jnp.where(low, 0.0, turn(above, stride))
+        high_a = jnp.where(high, 0.0, turn(below, -stride))
+        high_c = jnp.where(high, 1.0, turn(above, -stride))
+        inverse = 1.0 / (1.0 - below * low_c - above * high_a)
+        below, above = below * inverse, above * inverse
+        if steps is not None:
+            factor = scale if level == 0 else 1.0
+            steps[level, 0] = inverse * factor
+            steps[level, 1] = jnp.where(low, 0.0, below * factor)
+            steps[level, 2] = jnp.where(high, 0.0, above * factor)
+        below, above = below * low_a, above * high_c
+        stride, level = stride * 2, level + 1
+    return below, above
+
+
+def z_coef_kernel(sizes, maps, prepared, drift_z, steps, ends, pushes, packed, weights):
     extent_y, extent_z, size_x, size_y, size_z = sizes
     total_y, total_z = size_y * extent_y, size_z * extent_z
     y_start = lax.axis_index("gy") * size_y
@@ -638,21 +660,12 @@
     after = jnp.where(high, outer[ABOVE : ABOVE + 1], turn(inner, -1))
     below = jnp.where(low & (z_start == 0), 0.0, (d2 + before) * scale)
     above = jnp.where(high & (z_start + size_z == total_z), 0.0, (d2 - after) * scale)
-    stride, level = 1, 0
-    while stride < size_z:
-        low, high = row < stride, row >= size_z - stride
-        low_a = jnp.where(low, 1.0, turn(below, stride))
-        low_c = jnp.where(low, 0.0, turn(above, stride))
-        high_a = jnp.where(high, 0.0, turn(below, -stride))
-        high_c = jnp.where(high, 1.0, turn(above, -stride))
-        inverse = 1.0 / (1.0 - below * low_c - above * high_a)
-        below, above = below * inverse, above * inverse
-        factor = scale if level == 0 else 1.0
-        steps[level, 0] = inverse * factor
-        steps[level, 1] = jnp.where(low, 0.0, below * factor)
-        steps[level, 2] = jnp.where(high, 0.0, above * factor)
-        below, above = below * low_a, above * high_c
-        stride, level = stride * 2, level + 1
+    turned_below = jnp.where(low, 1.0, turn(above, 1))
+    turned_above = jnp.where(high, 1.0, turn(below, -1))
+    below, above = double_coefs(below, above, scale, steps)
+    turned_below, turned_above = double_coefs(turned_below, turned_above, scale)
+    weights[0] = turned_below * scale
+    weights[1] = turned_above * scale
     ends[0] = below
     ends[1] = above
     packed[...] = jnp.concatenate(
@@ -711,13 +724,13 @@
 
 def middle_kernel(levels, *refs):
     refs = list(refs)
-    steps, pushes, packed, base, from_below, from_above = refs[:6]
+    weights, pushes, packed, base, from_below, from_above = refs[:6]
     refs = refs[6:]
     inputs = []
     for stride, radix in levels:
         inputs.append((refs[0], refs[1 : 1 + radix]))
         refs = refs[1 + radix :]
-    message, doubled, seen = refs
+    message, sources, seen = refs
     size_y, width = base.shape[:2]
     size_x = width - ROWS
     below = above = jnp.zeros((width, LANES), jnp.float32)
@@ -746,6 +759,18 @@
         outer.append(value[size_x : size_x + 1])
     pushed = jnp.concatenate(outer, axis=0) * pushes[...]
     values = to_lines(inner, size_x)
+    sources[...] = values
+    message[...] = packed[...]
+    message[0:1] = total_of(weights[0] * values) + lines_of(pushed, size_x, BELOW + 1)
+    message[1:2] = total_of(weights[1] * values) + lines_of(pushed, size_x, 0)
+
+
+def total_of(values):
+    return jnp.sum(values, axis=0, keepdims=True)
+
+
+def double_kernel(steps, sources, doubled):
+    values = sources[...]
     stride, level = 1, 0
     while stride < values.shape[0]:
         values = (
@@ -755,9 +780,6 @@
         )
         stride, level = stride * 2, level + 1
     doubled[...] = values
-    message[...] = packed[...]
-    message[0:1] = values[:1] + lines_of(pushed, size_x, BELOW + 1)
-    message[1:2] = values[-1:] + lines_of(pushed, size_x, 0)
 
 
 def merge_z(low, high):
@@ -904,7 +926,7 @@
         far = call(functools.partial(far_kernel, sizes, maps, y_levels[:-1]), [prepared], far)
     coefs = [near] + list(far)
     doublings = size_z.bit_length() - 1
-    steps, ends, pushes, packed = call(
+    steps, ends, pushes, packed, weights = call(
         functools.partial(z_coef_kernel, sizes, maps),
         (prepared, drift_z),
         (
@@ -912,6 +934,7 @@
             shape(2, *narrow),
             shape(size_y, LANES),
             shape(ROWS, size_y * size_x),
+            shape(2, *narrow),
         ),
     )
     line_inputs = []
@@ -925,12 +948,13 @@
                 [coefs[number]] + received + ([packed] if number == 0 else []),
                 shape(width if facing else width + size_x, LANES),
             )
-    message, doubled = call(
+    message, sources = call(
         functools.partial(middle_kernel, y_levels),
-        [steps, pushes, packed, base, from_below, from_above] + line_inputs,
+        [weights, pushes, packed, base, from_below, from_above] + line_inputs,
         (shape(ROWS, size_y * size_x), shape(*narrow)),
         scratch=[pltpu.VMEM((4, 2, width, LANES), float32)],
     )
+    doubled = call(double_kernel, [steps, sources], shape(*narrow))
     end_inputs = []
     for number, (stride, radix) in enumerate(z_levels):
         received = exchange(message, "gz", stride, radix)

time: 20.7 us -> 20.5 us (level)
  waiting for transfers between devices: 5.14 us -> 4.51 us
  Pallas kernels: 6.15 us -> 6.55 us
    ppermute x7, waiting for transfers between devices: 5.14 us -> 4.51 us  [exchange(): lax.ppermute(message, axis, [(i, i ^ s * stride) for i in devices])]
    pallas_call x7 -> x8, Pallas kernels: 6.15 us -> 6.55 us  [call(): pl.pallas_call(kernel, out_shape=outputs, in_specs=in_specs or [vmem] * l...]
  transfers between devices with their start and end apart: 7 -> 7, of which waited for: 5 -> 5; matrix products, arithmetic and copies ran while one was open for 0% -> 0% of each run, Pallas kernels for 12% -> 16%
where the time goes in v8:
time: 20.5 us; the launch traced here: 20.4 us
  starting transfers between devices  9.22 us (45%)
  Pallas kernels  6.55 us (32%)
  waiting for transfers between devices  4.51 us (22%)
    ppermute x7, starting transfers between devices, exchange(): lax.ppermute(message, axis, [(i, i ^ s * stride) for i in devices])  9.22 us
    pallas_call x8, Pallas kernels, call(): pl.pallas_call(kernel, out_shape=outputs, in_specs=in_specs or [vmem] * l...  6.55 us
    ppermute x7, waiting for transfers between devices, exchange(): lax.ppermute(message, axis, [(i, i ^ s * stride) for i in devices])  4.51 us
  transfers between devices with their start and end apart: 7, of which 5 were waited for; matrix products, arithmetic and copies ran while one was open for 0% of the time, Pallas kernels for 16%

profile of v8, /device:TPU:0, one launch (start us, length us, event | category | flops | bytes accessed | tf_op | source)
XLA Modules:
  0.0 20.4 jit_solution(11917189932272060607)
XLA Ops:
  0.0 2.1 %shard_map.64 = (f32[72,128]{1,0:T(8,128)S(1)}, f32[8,40,128]{2,1,0:T(8,128)S(1)}, f32[10,40,128]{2,1,0:T(8,128)S(1)}, f32[32,8,128]{2,1,0:T(8,128)S(1)}, f32[16,128]{1,0:T(8,128)S(1)}) custom-call(f32[32,8,128]{2,1,0:T(8,128)} %density.1, f32[1,3]{1,0:T(1,128)} %bitcast.8, f32[3,16]{1,0:T(4,128)} %bitcast.6, f32[1,16]{1,0:T(1,128)} %bitcast.9, ...), custom_call_target="tpu_custom_call" | custom-call | flops 1000000 | bytes 1000000 | tf_op jit(solution)/shard_map/pallas_call | solution.py:878
  2.2 4.0 %collective-permute-start.2 = (f32[72,128]{1,0:T(8,128)S(1)}, f32[72,128]{1,0:T(8,128)S(1)}, u32[]{:S(2)}, u32[]{:S(2)}) collective-permute-start(f32[72,128]{1,0:T(8,128)S(1)} %get-tuple-element.33.refs_0_.refs_7_), channel_id=1, source_target_pairs={{0,3},{1,2},{2,1},{3,0},{4,7},{5,6},{6,5},{7,4},{8,11},{9,10},{10,... | collective-permute-start | bytes 110600 | tf_op jit(solution)/shard_map/ppermute | solution.py:855
  6.2 0.5 %collective-permute-start.1 = (f32[72,128]{1,0:T(8,128)S(1)}, f32[72,128]{1,0:T(8,128)S(1)}, u32[]{:S(2)}, u32[]{:S(2)}) collective-permute-start(f32[72,128]{1,0:T(8,128)S(1)} %get-tuple-element.33.refs_0_.refs_7_), channel_id=1, source_target_pairs={{0,2},{1,3},{2,0},{3,1},{4,6},{5,7},{6,4},{7,5},{8,10},{9,11},{10,... | collective-permute-start | bytes 110600 | tf_op jit(solution)/shard_map/ppermute | solution.py:855
  6.6 0.2 collective-permute-start
  6.8 1.2 %shard_map.65 = (f32[7,3,128,256]{3,2,1,0:T(8,128)S(1)}, f32[2,128,256]{2,1,0:T(8,128)S(1)}, f32[8,128]{1,0:T(8,128)S(1)}, f32[8,256]{1,0:T(8,128)S(1)}, f32[2,128,256]{2,1,0:T(8,128)S(1)}) custom-call(f32[16,128]{1,0:T(8,128)S(1)} %get-tuple-element.21.prepared, f32[32,8,128]{2,1,0:T(8,128)S(1)} %get-tuple-element.22.drift_z), custom_call_target="tpu_custom_call" | custom-call | flops 1000000 | bytes 1000000 | tf_op jit(solution)/shard_map/pallas_call | solution.py:878
  8.0 0.0 copy-start
  8.0 0.7 %shard_map.66 = (f32[4,4,40,128]{3,2,1,0:T(8,128)S(1)}, f32[8,40,128]{2,1,0:T(8,128)S(1)}, f32[8,40,128]{2,1,0:T(8,128)S(1)}, f32[8,40,128]{2,1,0:T(8,128)S(1)}) custom-call(f32[16,128]{1,0:T(8,128)S(1)} %get-tuple-element.21.prepared, f32[8,40,128]{2,1,0:T(8,128)S(1)} %get-tuple-element.27.line_values, f32[10,40,128]{2,1,0:T(8,128)S(1)} %get-tuple-element.28.line_drifts), custom_call_target="tpu_custom_call" | custom-call | flops 1000000 | bytes 1000000 | tf_op jit(solution)/shard_map/pallas_call | solution.py:878
  8.7 0.0 collective-permute-done.2.refs_3_.refs_10_
  8.8 1.4 %collective-permute-done.1.refs_2_.refs_9_ = f32[72,128]{1,0:T(8,128)S(1)} collective-permute-done((f32[72,128]{1,0:T(8,128)S(1)}, f32[72,128]{1,0:T(8,128)S(1)}, u32[]{:S(2)}, u32[]{:S(2)}) %collective-permute-start.1) | collective-permute-done | bytes 36896 | tf_op jit(solution)/shard_map/ppermute | solution.py:855
  10.1 0.5 %collective-permute-done.refs_1_.refs_8_ = f32[72,128]{1,0:T(8,128)S(1)} collective-permute-done((f32[72,128]{1,0:T(8,128)S(1)}, f32[72,128]{1,0:T(8,128)S(1)}, u32[]{:S(2)}, u32[]{:S(2)}) %collective-permute-start) | collective-permute-done | bytes 36896 | tf_op jit(solution)/shard_map/ppermute | solution.py:855
  10.6 0.1 shard_map.68.refs_12_
  10.7 2.6 %collective-permute-start.3 = (f32[40,128]{1,0:T(8,128)S(1)}, f32[40,128]{1,0:T(8,128)S(1)}, u32[]{:S(2)}, u32[]{:S(2)}) collective-permute-start(f32[40,128]{1,0:T(8,128)S(1)} %shard_map.68.refs_12_), channel_id=1, source_target_pairs={{0,4},{1,5},{2,6},{3,7},{4,0},{5,1},{6,2},{7,3},{8,12},{9,13},{10,... | collective-permute-start | bytes 61448 | tf_op jit(solution)/shard_map/ppermute | solution.py:855
  13.3 1.0 %shard_map.67.refs_11_ = f32[2,4,40,128]{3,2,1,0:T(8,128)S(1)} custom-call(f32[16,128]{1,0:T(8,128)S(1)} %get-tuple-element.21.prepared), custom_call_target="tpu_custom_call" | custom-call | flops 1000000 | bytes 1000000 | tf_op jit(solution)/shard_map/pallas_call | solution.py:878
  14.4 1.1 %collective-permute-done.3.refs_13_ = f32[40,128]{1,0:T(8,128)S(1)} collective-permute-done((f32[40,128]{1,0:T(8,128)S(1)}, f32[40,128]{1,0:T(8,128)S(1)}, u32[]{:S(2)}, u32[]{:S(2)}) %collective-permute-start.3) | collective-permute-done | bytes 20512 | tf_op jit(solution)/shard_map/ppermute | solution.py:855
  15.4 0.2 %shard_map.69 = (f32[8,256]{1,0:T(8,128)S(1)}, f32[128,256]{1,0:T(8,128)S(1)}) custom-call(f32[2,128,256]{2,1,0:T(8,128)S(1)} %get-tuple-element.24.refs_0_, f32[8,128]{1,0:T(8,128)S(1)} %get-tuple-element.25.refs_1_, f32[8,256]{1,0:T(8,128)S(1)} %get-tuple-element.26.refs_4_.refs_2_, f32[8,40,128]{2,1,0:T(8,128)S(1)} %get-tuple-element.29.refs_3_, ...), custom_call_target="tpu_custom_call" | custom-call | flops 1000000 | bytes 1000000 | tf_op jit(solution)/shard_map/pallas_call | solution.py:878
  15.7 0.1 collective-permute-start.6
  15.7 1.6 %collective-permute-start.5 = (f32[8,256]{1,0:T(8,128)S(1)}, f32[8,256]{1,0:T(8,128)S(1)}, u32[]{:S(2)}, u32[]{:S(2)}) collective-permute-start(f32[8,256]{1,0:T(8,128)S(1)} %get-tuple-element.36.refs_0_), channel_id=1, source_target_pairs={{0,16},{8,24},{16,0},{24,8},{1,17},{9,25},{17,1},{25,9},{2,18},{10... | collective-permute-start | bytes 24584 | tf_op jit(solution)/shard_map/ppermute | solution.py:855
  17.3 0.3 %collective-permute-start.4 = (f32[8,256]{1,0:T(8,128)S(1)}, f32[8,256]{1,0:T(8,128)S(1)}, u32[]{:S(2)}, u32[]{:S(2)}) collective-permute-start(f32[8,256]{1,0:T(8,128)S(1)} %get-tuple-element.36.refs_0_), channel_id=1, source_target_pairs={{0,8},{8,0},{16,24},{24,16},{1,9},{9,1},{17,25},{25,17},{2,10},{10... | collective-permute-start | bytes 24584 | tf_op jit(solution)/shard_map/ppermute | solution.py:855
  17.6 0.2 %shard_map.70.doubled = f32[128,256]{1,0:T(8,128)S(1)} custom-call(f32[7,3,128,256]{3,2,1,0:T(8,128)S(1)} %get-tuple-element.23.steps, f32[128,256]{1,0:T(8,128)S(1)} %get-tuple-element.34.sources), custom_call_target="tpu_custom_call" | custom-call | flops 1000000 | bytes 1000000 | tf_op jit(solution)/shard_map/pallas_call | solution.py:878
  17.8 1.0 %collective-permute-done.6.refs_3_ = f32[8,256]{1,0:T(8,128)S(1)} collective-permute-done((f32[8,256]{1,0:T(8,128)S(1)}, f32[8,256]{1,0:T(8,128)S(1)}, u32[]{:S(2)}, u32[]{:S(2)}) %collective-permute-start.6) | collective-permute-done | bytes 8224 | tf_op jit(solution)/shard_map/ppermute | solution.py:855
  18.8 0.6 %collective-permute-done.5.refs_2_ = f32[8,256]{1,0:T(8,128)S(1)} collective-permute-done((f32[8,256]{1,0:T(8,128)S(1)}, f32[8,256]{1,0:T(8,128)S(1)}, u32[]{:S(2)}, u32[]{:S(2)}) %collective-permute-start.5) | collective-permute-done | bytes 8224 | tf_op jit(solution)/shard_map/ppermute | solution.py:855
  19.5 0.0 collective-permute-done.4.refs_1_
  19.5 0.0 copy-done
  19.5 0.9 %shard_map.71 = f32[32,8,128]{2,1,0:T(8,128)} custom-call(f32[32,8,128]{2,1,0:T(8,128)S(1)} %copy-done, f32[128,256]{1,0:T(8,128)S(1)} %shard_map.70.doubled, f32[2,128,256]{2,1,0:T(8,128)S(1)} %get-tuple-element.35.ends, f32[8,256]{1,0:T(8,128)S(1)} %get-tuple-element.36.refs_0_, f32[8,256]{1,0:T(8,128)S(1)} %collective-permute-done.4.refs_1_, ...), custom_call_target="tpu_custom_call" | custom-call | flops 1000000 | bytes 1000000 | tf_op jit(solution)/shard_map/pallas_call | solution.py:878
Async XLA Ops:
  2.2 6.6 %collective-permute-start.2 = (f32[72,128]{1,0:T(8,128)S(1)}, f32[72,128]{1,0:T(8,128)S(1)}, u32[]{:S(2)}, u32[]{:S(2)}) collective-permute-start(f32[72,128]{1,0:T(8,128)S(1)} %get-tuple-element.33.refs_0_.refs_7_), channel_id=1, source_target_pairs={{0,3},{1,2},{2,1},{3,0},{4,7},{5,6},{6,5},{7,4},{8,11},{9,10},{10,... | collective-permute-start | bytes 110600 | tf_op jit(solution)/shard_map/ppermute | solution.py:855
  6.2 4.0 %collective-permute-start.1 = (f32[72,128]{1,0:T(8,128)S(1)}, f32[72,128]{1,0:T(8,128)S(1)}, u32[]{:S(2)}, u32[]{:S(2)}) collective-permute-start(f32[72,128]{1,0:T(8,128)S(1)} %get-tuple-element.33.refs_0_.refs_7_), channel_id=1, source_target_pairs={{0,2},{1,3},{2,0},{3,1},{4,6},{5,7},{6,4},{7,5},{8,10},{9,11},{10,... | collective-permute-start | bytes 110600 | tf_op jit(solution)/shard_map/ppermute | solution.py:855
  6.6 4.0 %collective-permute-start = (f32[72,128]{1,0:T(8,128)S(1)}, f32[72,128]{1,0:T(8,128)S(1)}, u32[]{:S(2)}, u32[]{:S(2)}) collective-permute-start(f32[72,128]{1,0:T(8,128)S(1)} %get-tuple-element.33.refs_0_.refs_7_), channel_id=1, source_target_pairs={{0,1},{1,0},{2,3},{3,2},{4,5},{5,4},{6,7},{7,6},{8,9},{9,8},{10,11... | collective-permute-start | bytes 110600 | tf_op jit(solution)/shard_map/ppermute | solution.py:855
  8.0 11.4 %copy-start = (f32[32,8,128]{2,1,0:T(8,128)S(1)}, f32[32,8,128]{2,1,0:T(8,128)}, u32[]{:S(2)}) copy-start(f32[32,8,128]{2,1,0:T(8,128)} %density.1) | copy-start | bytes 393220
  10.7 4.7 %collective-permute-start.3 = (f32[40,128]{1,0:T(8,128)S(1)}, f32[40,128]{1,0:T(8,128)S(1)}, u32[]{:S(2)}, u32[]{:S(2)}) collective-permute-start(f32[40,128]{1,0:T(8,128)S(1)} %shard_map.68.refs_12_), channel_id=1, source_target_pairs={{0,4},{1,5},{2,6},{3,7},{4,0},{5,1},{6,2},{7,3},{8,12},{9,13},{10,... | collective-permute-start | bytes 61448 | tf_op jit(solution)/shard_map/ppermute | solution.py:855
  15.7 3.2 %collective-permute-start.6 = (f32[8,256]{1,0:T(8,128)S(1)}, f32[8,256]{1,0:T(8,128)S(1)}, u32[]{:S(2)}, u32[]{:S(2)}) collective-permute-start(f32[8,256]{1,0:T(8,128)S(1)} %get-tuple-element.36.refs_0_), channel_id=1, source_target_pairs={{0,24},{8,16},{16,8},{24,0},{1,25},{9,17},{17,9},{25,1},{2,26},{10... | collective-permute-start | bytes 24584 | tf_op jit(solution)/shard_map/ppermute | solution.py:855
  15.7 3.7 %collective-permute-start.5 = (f32[8,256]{1,0:T(8,128)S(1)}, f32[8,256]{1,0:T(8,128)S(1)}, u32[]{:S(2)}, u32[]{:S(2)}) collective-permute-start(f32[8,256]{1,0:T(8,128)S(1)} %get-tuple-element.36.refs_0_), channel_id=1, source_target_pairs={{0,16},{8,24},{16,0},{24,8},{1,17},{9,25},{17,1},{25,9},{2,18},{10... | collective-permute-start | bytes 24584 | tf_op jit(solution)/shard_map/ppermute | solution.py:855
  17.3 2.1 %collective-permute-start.4 = (f32[8,256]{1,0:T(8,128)S(1)}, f32[8,256]{1,0:T(8,128)S(1)}, u32[]{:S(2)}, u32[]{:S(2)}) collective-permute-start(f32[8,256]{1,0:T(8,128)S(1)} %get-tuple-element.36.refs_0_), channel_id=1, source_target_pairs={{0,8},{8,0},{16,24},{24,16},{1,9},{9,1},{17,25},{25,17},{2,10},{10... | collective-permute-start | bytes 24584 | tf_op jit(solution)/shard_map/ppermute | solution.py:855

commit v9 on v8

--- a/solution.py
+++ b/solution.py
@@ -19,7 +19,7 @@
 
 
 def coordinate(positions, line_total):
-    return (2.0 * positions.astype(jnp.float32) + 1.0) / line_total - 1.0
+    return (2.0 * positions.astype(jnp.float32) + 1.0) * (1.0 / line_total) - 1.0
 
 
 def roll(values, shift, axis):
@@ -89,11 +89,13 @@
     return z_rows(params, maps, z_start + iota((size_z, LANES), 0), total_z)
 
 
+def outer_positions(z_start, size_z):
+    return jnp.where(iota((ROWS, LANES), 0) == 0, z_start - 1, z_start + size_z)
+
+
 def outer_z_rows(params, maps, z_start, size_z, total_z):
-    row = iota((size_z, LANES), 0)
-    return z_rows(
-        params, maps, jnp.where(row == BELOW, z_start - 1, z_start + size_z), total_z
-    )
+    rows = z_rows(params, maps, outer_positions(z_start, size_z), total_z)
+    return jnp.where(iota((size_z, LANES), 0) == BELOW, rows[:1], rows[1:2])
 
 
 def only(rows, maps, component):
@@ -107,15 +109,19 @@
 
 
 def xz_rows(params, maps, size_x, z_start, size_z, total_z):
-    row = iota((BELOW + 1 + size_x, LANES), 0)
-    x_coord = coordinate(jnp.where(row < size_x, row, row - BELOW - 1), size_x)
-    z_coord = coordinate(jnp.where(row > BELOW, z_start - 1, z_start + size_z), total_z)
-    part = slope(params, x_coord, 0) + slope(params, z_coord, 2)
-    both = bump(params, x_coord, 0) * bump(params, z_coord, 2)
-    both = both * jnp.where(first_term(maps), 1.0, part)
-    return jnp.concatenate(
-        [both, jnp.zeros((LANES - BELOW - 1 - size_x, LANES), jnp.float32)], axis=0
-    )
+    x_coord = coordinate(iota((size_x, LANES), 0), size_x)
+    z_coord = coordinate(outer_positions(z_start, size_z), total_z)
+    x_bump, z_bump = bump(params, x_coord, 0), bump(params, z_coord, 2)
+    x_part, z_part = slope(params, x_coord, 0), slope(params, z_coord, 2)
+    rows = [
+        (x_bump * z_bump[i : i + 1])
+        * jnp.where(first_term(maps), 1.0, x_part + z_part[i : i + 1])
+        for i in (1, 0)
+    ]
+    blank = jnp.zeros((BELOW + 1 - size_x, LANES), jnp.float32)
+    rest = jnp.zeros((LANES - BELOW - 1 - size_x, LANES), jnp.float32)
+    parts = [rows[0], blank, rows[1], rest] if size_x <= BELOW else [rows[0], rows[1], rest]
+    return jnp.concatenate(parts, axis=0)
 
 
 def with_extra(main, row):
@@ -411,11 +417,10 @@
         solved[i] = answers[i][: 2 * size_y]
     planes = pack_planes([answer[2 * size_y :] for answer in answers])
 
-    row = iota((1, LANES), 0)
-    out_rows = []
-    for position in (y_start - 1, y_start + size_y):
-        bumps, part = y_factors(params, maps, row + position, total_y)
-        out_rows.append((x_bump * bumps) * (x_part + part))
+    out_rows = [
+        (x_bump * out_bump[j : j + 1]) * (x_part + out_part[j : j + 1])
+        for j in (size_y - 1, 0)
+    ]
     ends = half_drift(jnp.concatenate(out_rows, axis=0), inner[1])
     position = y_start - 1 + iota((2 * ROWS, LANES), 0)
     extra = half_drift(
@@ -769,7 +774,15 @@
     return jnp.sum(values, axis=0, keepdims=True)
 
 
-def double_kernel(steps, sources, doubled):
+def from_lines(values, size_x):
+    rows = []
+    for first in range(0, values.shape[1], LANES):
+        tile = jnp.transpose(values[:, first : first + LANES])
+        rows += [tile[q : q + size_x] for q in range(0, LANES, size_x)]
+    return rows
+
+
+def double_kernel(steps, sources, density, base):
     values = sources[...]
     stride, level = 1, 0
     while stride < values.shape[0]:
@@ -779,7 +792,8 @@
             + steps[level, 2] * turn(values, -stride)
         )
         stride, level = stride * 2, level + 1
-    doubled[...] = values
+    for j, rows in enumerate(from_lines(values, density.shape[0])):
+        base[j] = density[:, j, :] + rows
 
 
 def merge_z(low, high):
@@ -807,15 +821,14 @@
     message[...] = jnp.concatenate(total + total[:2], axis=0)
 
 
-def end_kernel(levels, density, doubled, ends, *refs):
+def end_kernel(levels, base, ends, *refs):
     refs = list(refs)
     inputs = []
     for stride, radix in levels:
         inputs.append(refs[:radix])
         refs = refs[radix:]
     out, seen = refs
-    size_x, size_y, _ = density.shape
-    below = above = jnp.zeros((1, doubled.shape[1]), jnp.float32)
+    below = above = jnp.zeros((1, ends.shape[2]), jnp.float32)
     for (stride, radix), received in zip(reversed(levels), reversed(inputs)):
         digit = lax.rem(lax.div(lax.axis_index("gz"), stride), radix)
         members = [unpack_ends(m) for m in gather_members(received, digit, radix)]
@@ -829,15 +842,9 @@
             seen[j, 0:1] = lows[j]
             seen[j, 1:2] = highs[j]
         below, above = seen[digit, 0:1], seen[digit, 1:2]
-    values = doubled[...] + ends[0] * below + ends[1] * above
-    group = LANES // size_x
-    for first in range(0, size_y, group):
-        tile = first // group
-        lines = jnp.transpose(values[:, tile * LANES : (tile + 1) * LANES])
-        for q in range(group):
-            out[:, first + q, :] = (
-                density[:, first + q, :] + lines[q * size_x : (q + 1) * size_x]
-            )
+    values = ends[0] * below + ends[1] * above
+    for j, rows in enumerate(from_lines(values, base.shape[1])):
+        out[:, j, :] = base[j] + rows
 
 
 def radices(extent):
@@ -954,7 +961,7 @@
         (shape(ROWS, size_y * size_x), shape(*narrow)),
         scratch=[pltpu.VMEM((4, 2, width, LANES), float32)],
     )
-    doubled = call(double_kernel, [steps, sources], shape(*narrow))
+    base = call(double_kernel, [steps, sources, density], shape(size_y, size_x, size_z))
     end_inputs = []
     for number, (stride, radix) in enumerate(z_levels):
         received = exchange(message, "gz", stride, radix)
@@ -967,7 +974,7 @@
             )
     return call(
         functools.partial(end_kernel, z_levels),
-        [density, doubled, ends] + end_inputs,
+        [base, ends] + end_inputs,
         shape(size_x, size_y, size_z),
         scratch=[pltpu.VMEM((4, ROWS, size_y * size_x), float32)],
     )

time: 20.5 us -> 20.5 us (level)
  no operation moved by 1% of the time
where the time goes in v9:
time: 20.5 us; the launch traced here: 20.4 us
  starting transfers between devices  9.23 us (45%)
  Pallas kernels  6.65 us (32%)
  waiting for transfers between devices  4.42 us (22%)
    ppermute x7, starting transfers between devices, exchange(): lax.ppermute(message, axis, [(i, i ^ s * stride) for i in devices])  9.23 us
    pallas_call x8, Pallas kernels, call(): pl.pallas_call(kernel, out_shape=outputs, in_specs=in_specs or [vmem] * l...  6.65 us
    ppermute x7, waiting for transfers between devices, exchange(): lax.ppermute(message, axis, [(i, i ^ s * stride) for i in devices])  4.42 us
  transfers between devices with their start and end apart: 7, of which 5 were waited for; matrix products, arithmetic and copies ran while one was open for 0% of the time, Pallas kernels for 16%

profile of v9, /device:TPU:0, one launch (start us, length us, event | category | flops | bytes accessed | tf_op | source)
XLA Modules:
  0.0 20.4 jit_solution(14874712514186192496)
XLA Ops:
  0.0 0.0 copy-start
  0.0 2.2 %shard_map.64 = (f32[72,128]{1,0:T(8,128)S(1)}, f32[8,40,128]{2,1,0:T(8,128)S(1)}, f32[10,40,128]{2,1,0:T(8,128)S(1)}, f32[32,8,128]{2,1,0:T(8,128)S(1)}, f32[16,128]{1,0:T(8,128)S(1)}) custom-call(f32[32,8,128]{2,1,0:T(8,128)} %density.1, f32[1,3]{1,0:T(1,128)} %bitcast.8, f32[3,16]{1,0:T(4,128)} %bitcast.6, f32[1,16]{1,0:T(1,128)} %bitcast.9, ...), custom_call_target="tpu_custom_call" | custom-call | flops 1000000 | bytes 1000000 | tf_op jit(solution)/shard_map/pallas_call | solution.py:885
  2.2 4.0 %collective-permute-start.2 = (f32[72,128]{1,0:T(8,128)S(1)}, f32[72,128]{1,0:T(8,128)S(1)}, u32[]{:S(2)}, u32[]{:S(2)}) collective-permute-start(f32[72,128]{1,0:T(8,128)S(1)} %get-tuple-element.33.refs_0_.refs_7_), channel_id=1, source_target_pairs={{0,3},{1,2},{2,1},{3,0},{4,7},{5,6},{6,5},{7,4},{8,11},{9,10},{10,... | collective-permute-start | bytes 110600 | tf_op jit(solution)/shard_map/ppermute | solution.py:862
  6.2 0.4 %collective-permute-start.1 = (f32[72,128]{1,0:T(8,128)S(1)}, f32[72,128]{1,0:T(8,128)S(1)}, u32[]{:S(2)}, u32[]{:S(2)}) collective-permute-start(f32[72,128]{1,0:T(8,128)S(1)} %get-tuple-element.33.refs_0_.refs_7_), channel_id=1, source_target_pairs={{0,2},{1,3},{2,0},{3,1},{4,6},{5,7},{6,4},{7,5},{8,10},{9,11},{10,... | collective-permute-start | bytes 110600 | tf_op jit(solution)/shard_map/ppermute | solution.py:862
  6.7 0.2 collective-permute-start
  6.9 1.2 %shard_map.65 = (f32[7,3,128,256]{3,2,1,0:T(8,128)S(1)}, f32[2,128,256]{2,1,0:T(8,128)S(1)}, f32[8,128]{1,0:T(8,128)S(1)}, f32[8,256]{1,0:T(8,128)S(1)}, f32[2,128,256]{2,1,0:T(8,128)S(1)}) custom-call(f32[16,128]{1,0:T(8,128)S(1)} %get-tuple-element.21.prepared, f32[32,8,128]{2,1,0:T(8,128)S(1)} %get-tuple-element.22.drift_z), custom_call_target="tpu_custom_call" | custom-call | flops 1000000 | bytes 1000000 | tf_op jit(solution)/shard_map/pallas_call | solution.py:885
  8.1 0.7 %shard_map.66 = (f32[4,4,40,128]{3,2,1,0:T(8,128)S(1)}, f32[8,40,128]{2,1,0:T(8,128)S(1)}, f32[8,40,128]{2,1,0:T(8,128)S(1)}, f32[8,40,128]{2,1,0:T(8,128)S(1)}) custom-call(f32[16,128]{1,0:T(8,128)S(1)} %get-tuple-element.21.prepared, f32[8,40,128]{2,1,0:T(8,128)S(1)} %get-tuple-element.27.line_values, f32[10,40,128]{2,1,0:T(8,128)S(1)} %get-tuple-element.28.line_drifts), custom_call_target="tpu_custom_call" | custom-call | flops 1000000 | bytes 1000000 | tf_op jit(solution)/shard_map/pallas_call | solution.py:885
  8.8 0.0 collective-permute-done.2.refs_3_.refs_10_
  8.8 1.4 %collective-permute-done.1.refs_2_.refs_9_ = f32[72,128]{1,0:T(8,128)S(1)} collective-permute-done((f32[72,128]{1,0:T(8,128)S(1)}, f32[72,128]{1,0:T(8,128)S(1)}, u32[]{:S(2)}, u32[]{:S(2)}) %collective-permute-start.1) | collective-permute-done | bytes 36896 | tf_op jit(solution)/shard_map/ppermute | solution.py:862
  10.2 0.4 %collective-permute-done.refs_1_.refs_8_ = f32[72,128]{1,0:T(8,128)S(1)} collective-permute-done((f32[72,128]{1,0:T(8,128)S(1)}, f32[72,128]{1,0:T(8,128)S(1)}, u32[]{:S(2)}, u32[]{:S(2)}) %collective-permute-start) | collective-permute-done | bytes 36896 | tf_op jit(solution)/shard_map/ppermute | solution.py:862
  10.6 0.1 shard_map.68.refs_12_
  10.7 2.7 %collective-permute-start.3 = (f32[40,128]{1,0:T(8,128)S(1)}, f32[40,128]{1,0:T(8,128)S(1)}, u32[]{:S(2)}, u32[]{:S(2)}) collective-permute-start(f32[40,128]{1,0:T(8,128)S(1)} %shard_map.68.refs_12_), channel_id=1, source_target_pairs={{0,4},{1,5},{2,6},{3,7},{4,0},{5,1},{6,2},{7,3},{8,12},{9,13},{10,... | collective-permute-start | bytes 61448 | tf_op jit(solution)/shard_map/ppermute | solution.py:862
  13.4 1.0 %shard_map.67.refs_11_ = f32[2,4,40,128]{3,2,1,0:T(8,128)S(1)} custom-call(f32[16,128]{1,0:T(8,128)S(1)} %get-tuple-element.21.prepared), custom_call_target="tpu_custom_call" | custom-call | flops 1000000 | bytes 1000000 | tf_op jit(solution)/shard_map/pallas_call | solution.py:885
  14.4 1.0 %collective-permute-done.3.refs_13_ = f32[40,128]{1,0:T(8,128)S(1)} collective-permute-done((f32[40,128]{1,0:T(8,128)S(1)}, f32[40,128]{1,0:T(8,128)S(1)}, u32[]{:S(2)}, u32[]{:S(2)}) %collective-permute-start.3) | collective-permute-done | bytes 20512 | tf_op jit(solution)/shard_map/ppermute | solution.py:862
  15.4 0.2 %shard_map.69 = (f32[8,256]{1,0:T(8,128)S(1)}, f32[128,256]{1,0:T(8,128)S(1)}) custom-call(f32[2,128,256]{2,1,0:T(8,128)S(1)} %get-tuple-element.24.refs_0_, f32[8,128]{1,0:T(8,128)S(1)} %get-tuple-element.25.refs_1_, f32[8,256]{1,0:T(8,128)S(1)} %get-tuple-element.26.refs_4_.refs_2_, f32[8,40,128]{2,1,0:T(8,128)S(1)} %get-tuple-element.29.refs_3_, ...), custom_call_target="tpu_custom_call" | custom-call | flops 1000000 | bytes 1000000 | tf_op jit(solution)/shard_map/pallas_call | solution.py:885
  15.7 0.1 collective-permute-start.6
  15.8 1.6 %collective-permute-start.5 = (f32[8,256]{1,0:T(8,128)S(1)}, f32[8,256]{1,0:T(8,128)S(1)}, u32[]{:S(2)}, u32[]{:S(2)}) collective-permute-start(f32[8,256]{1,0:T(8,128)S(1)} %get-tuple-element.36.refs_0_), channel_id=1, source_target_pairs={{0,16},{8,24},{16,0},{24,8},{1,17},{9,25},{17,1},{25,9},{2,18},{10... | collective-permute-start | bytes 24584 | tf_op jit(solution)/shard_map/ppermute | solution.py:862
  17.4 0.3 %collective-permute-start.4 = (f32[8,256]{1,0:T(8,128)S(1)}, f32[8,256]{1,0:T(8,128)S(1)}, u32[]{:S(2)}, u32[]{:S(2)}) collective-permute-start(f32[8,256]{1,0:T(8,128)S(1)} %get-tuple-element.36.refs_0_), channel_id=1, source_target_pairs={{0,8},{8,0},{16,24},{24,16},{1,9},{9,1},{17,25},{25,17},{2,10},{10... | collective-permute-start | bytes 24584 | tf_op jit(solution)/shard_map/ppermute | solution.py:862
  17.6 0.0 copy-done
  17.6 0.3 %shard_map.70.base = f32[8,32,128]{2,1,0:T(8,128)S(1)} custom-call(f32[7,3,128,256]{3,2,1,0:T(8,128)S(1)} %get-tuple-element.23.steps, f32[128,256]{1,0:T(8,128)S(1)} %get-tuple-element.34.sources, f32[32,8,128]{2,1,0:T(8,128)S(1)} %copy-done), custom_call_target="tpu_custom_call" | custom-call | flops 1000000 | bytes 1000000 | tf_op jit(solution)/shard_map/pallas_call | solution.py:885
  17.9 0.9 %collective-permute-done.6.refs_3_ = f32[8,256]{1,0:T(8,128)S(1)} collective-permute-done((f32[8,256]{1,0:T(8,128)S(1)}, f32[8,256]{1,0:T(8,128)S(1)}, u32[]{:S(2)}, u32[]{:S(2)}) %collective-permute-start.6) | collective-permute-done | bytes 8224 | tf_op jit(solution)/shard_map/ppermute | solution.py:862
  18.8 0.6 %collective-permute-done.5.refs_2_ = f32[8,256]{1,0:T(8,128)S(1)} collective-permute-done((f32[8,256]{1,0:T(8,128)S(1)}, f32[8,256]{1,0:T(8,128)S(1)}, u32[]{:S(2)}, u32[]{:S(2)}) %collective-permute-start.5) | collective-permute-done | bytes 8224 | tf_op jit(solution)/shard_map/ppermute | solution.py:862
  19.5 0.0 collective-permute-done.4.refs_1_
  19.5 0.9 %shard_map.71 = f32[32,8,128]{2,1,0:T(8,128)} custom-call(f32[8,32,128]{2,1,0:T(8,128)S(1)} %shard_map.70.base, f32[2,128,256]{2,1,0:T(8,128)S(1)} %get-tuple-element.35.ends, f32[8,256]{1,0:T(8,128)S(1)} %get-tuple-element.36.refs_0_, f32[8,256]{1,0:T(8,128)S(1)} %collective-permute-done.4.refs_1_, f32[8,256]{1,0:T(8,128)S(1)} %collective-permute-done.5.refs_2_, ...), custom_call_target="tpu_custom_call" | custom-call | flops 1000000 | bytes 1000000 | tf_op jit(solution)/shard_map/pallas_call | solution.py:885
Async XLA Ops:
  0.0 17.6 %copy-start = (f32[32,8,128]{2,1,0:T(8,128)S(1)}, f32[32,8,128]{2,1,0:T(8,128)}, u32[]{:S(2)}) copy-start(f32[32,8,128]{2,1,0:T(8,128)} %density.1) | copy-start | bytes 393220
  2.2 6.6 %collective-permute-start.2 = (f32[72,128]{1,0:T(8,128)S(1)}, f32[72,128]{1,0:T(8,128)S(1)}, u32[]{:S(2)}, u32[]{:S(2)}) collective-permute-start(f32[72,128]{1,0:T(8,128)S(1)} %get-tuple-element.33.refs_0_.refs_7_), channel_id=1, source_target_pairs={{0,3},{1,2},{2,1},{3,0},{4,7},{5,6},{6,5},{7,4},{8,11},{9,10},{10,... | collective-permute-start | bytes 110600 | tf_op jit(solution)/shard_map/ppermute | solution.py:862
  6.2 4.0 %collective-permute-start.1 = (f32[72,128]{1,0:T(8,128)S(1)}, f32[72,128]{1,0:T(8,128)S(1)}, u32[]{:S(2)}, u32[]{:S(2)}) collective-permute-start(f32[72,128]{1,0:T(8,128)S(1)} %get-tuple-element.33.refs_0_.refs_7_), channel_id=1, source_target_pairs={{0,2},{1,3},{2,0},{3,1},{4,6},{5,7},{6,4},{7,5},{8,10},{9,11},{10,... | collective-permute-start | bytes 110600 | tf_op jit(solution)/shard_map/ppermute | solution.py:862
  6.7 4.0 %collective-permute-start = (f32[72,128]{1,0:T(8,128)S(1)}, f32[72,128]{1,0:T(8,128)S(1)}, u32[]{:S(2)}, u32[]{:S(2)}) collective-permute-start(f32[72,128]{1,0:T(8,128)S(1)} %get-tuple-element.33.refs_0_.refs_7_), channel_id=1, source_target_pairs={{0,1},{1,0},{2,3},{3,2},{4,5},{5,4},{6,7},{7,6},{8,9},{9,8},{10,11... | collective-permute-start | bytes 110600 | tf_op jit(solution)/shard_map/ppermute | solution.py:862
  10.7 4.7 %collective-permute-start.3 = (f32[40,128]{1,0:T(8,128)S(1)}, f32[40,128]{1,0:T(8,128)S(1)}, u32[]{:S(2)}, u32[]{:S(2)}) collective-permute-start(f32[40,128]{1,0:T(8,128)S(1)} %shard_map.68.refs_12_), channel_id=1, source_target_pairs={{0,4},{1,5},{2,6},{3,7},{4,0},{5,1},{6,2},{7,3},{8,12},{9,13},{10,... | collective-permute-start | bytes 61448 | tf_op jit(solution)/shard_map/ppermute | solution.py:862
  15.7 3.2 %collective-permute-start.6 = (f32[8,256]{1,0:T(8,128)S(1)}, f32[8,256]{1,0:T(8,128)S(1)}, u32[]{:S(2)}, u32[]{:S(2)}) collective-permute-start(f32[8,256]{1,0:T(8,128)S(1)} %get-tuple-element.36.refs_0_), channel_id=1, source_target_pairs={{0,24},{8,16},{16,8},{24,0},{1,25},{9,17},{17,9},{25,1},{2,26},{10... | collective-permute-start | bytes 24584 | tf_op jit(solution)/shard_map/ppermute | solution.py:862
  15.8 3.7 %collective-permute-start.5 = (f32[8,256]{1,0:T(8,128)S(1)}, f32[8,256]{1,0:T(8,128)S(1)}, u32[]{:S(2)}, u32[]{:S(2)}) collective-permute-start(f32[8,256]{1,0:T(8,128)S(1)} %get-tuple-element.36.refs_0_), channel_id=1, source_target_pairs={{0,16},{8,24},{16,0},{24,8},{1,17},{9,25},{17,1},{25,9},{2,18},{10... | collective-permute-start | bytes 24584 | tf_op jit(solution)/shard_map/ppermute | solution.py:862
  17.4 2.1 %collective-permute-start.4 = (f32[8,256]{1,0:T(8,128)S(1)}, f32[8,256]{1,0:T(8,128)S(1)}, u32[]{:S(2)}, u32[]{:S(2)}) collective-permute-start(f32[8,256]{1,0:T(8,128)S(1)} %get-tuple-element.36.refs_0_), channel_id=1, source_target_pairs={{0,8},{8,0},{16,24},{24,16},{1,9},{9,1},{17,25},{25,17},{2,10},{10... | collective-permute-start | bytes 24584 | tf_op jit(solution)/shard_map/ppermute | solution.py:862

commit v10 on v9

--- a/solution.py
+++ b/solution.py
@@ -238,7 +238,7 @@
 
 
 def solve_x(up, down, source, pivot):
-    size = source.shape[0]
+    size = len(source)
     half = size // 2
     low_g, low_c, high_g, high_c = {}, {}, {}, {}
     g = c = None
@@ -438,19 +438,9 @@
         line_values[j] = values[j]
     for j in range(size_y + 2):
         line_drifts[j] = line_drift[j]
-    pivot = 1.0 + 2.0 * d1
-    g = c = None
-    gs, cs = [], []
-    for j in range(size_y):
-        lower, upper = line_factors(line_drift, j, size_y, d1, y_start, total_y)
-        weight = 1.0 / (pivot if j == 0 else pivot - lower * c)
-        g = (values[j] if j == 0 else values[j] + lower * g) * weight
-        c = upper * weight
-        gs.append(g)
-        cs.append(c)
-    r_first = r_last = g
-    for j in reversed(range(size_y - 1)):
-        r_first = gs[j] + cs[j] * r_first
+    inside = line_drift[1:-1]
+    lines = solve_x([d1 + h for h in inside], [d1 - h for h in inside], values, 1.0 + 2.0 * d1)
+    r_first, r_last = lines[0], lines[-1]
     pushed_up = solved[:, size_y, :] / (d1 + line_drift[size_y][:size_x])
     pushed_down = solved[:, 2 * size_y - 1, :] / (d1 - line_drift[1][:size_x])
     blank = jnp.zeros((1, LANES), jnp.float32)

time: 20.5 us -> 20.5 us (level)
  no operation moved by 1% of the time
where the time goes in v10:
time: 20.5 us; the launch traced here: 20.4 us
  starting transfers between devices  9.23 us (45%)
  Pallas kernels  6.67 us (33%)
  waiting for transfers between devices  4.42 us (22%)
    ppermute x7, starting transfers between devices, exchange(): lax.ppermute(message, axis, [(i, i ^ s * stride) for i in devices])  9.23 us
    pallas_call x8, Pallas kernels, call(): pl.pallas_call(kernel, out_shape=outputs, in_specs=in_specs or [vmem] * l...  6.67 us
    ppermute x7, waiting for transfers between devices, exchange(): lax.ppermute(message, axis, [(i, i ^ s * stride) for i in devices])  4.42 us
  transfers between devices with their start and end apart: 7, of which 5 were waited for; matrix products, arithmetic and copies ran while one was open for 0% of the time, Pallas kernels for 16%

profile of v10, /device:TPU:0, one launch (start us, length us, event | category | flops | bytes accessed | tf_op | source)
XLA Modules:
  0.0 20.4 jit_solution(5879857606570030116)
XLA Ops:
  0.0 0.0 copy-start
  0.0 2.2 %shard_map.64 = (f32[72,128]{1,0:T(8,128)S(1)}, f32[8,40,128]{2,1,0:T(8,128)S(1)}, f32[10,40,128]{2,1,0:T(8,128)S(1)}, f32[32,8,128]{2,1,0:T(8,128)S(1)}, f32[16,128]{1,0:T(8,128)S(1)}) custom-call(f32[32,8,128]{2,1,0:T(8,128)} %density.1, f32[1,3]{1,0:T(1,128)} %bitcast.8, f32[3,16]{1,0:T(4,128)} %bitcast.6, f32[1,16]{1,0:T(1,128)} %bitcast.9, ...), custom_call_target="tpu_custom_call" | custom-call | flops 1000000 | bytes 1000000 | tf_op jit(solution)/shard_map/pallas_call | solution.py:875
  2.2 4.0 %collective-permute-start.2 = (f32[72,128]{1,0:T(8,128)S(1)}, f32[72,128]{1,0:T(8,128)S(1)}, u32[]{:S(2)}, u32[]{:S(2)}) collective-permute-start(f32[72,128]{1,0:T(8,128)S(1)} %get-tuple-element.33.refs_0_.refs_7_), channel_id=1, source_target_pairs={{0,3},{1,2},{2,1},{3,0},{4,7},{5,6},{6,5},{7,4},{8,11},{9,10},{10,... | collective-permute-start | bytes 110600 | tf_op jit(solution)/shard_map/ppermute | solution.py:852
  6.2 0.4 %collective-permute-start.1 = (f32[72,128]{1,0:T(8,128)S(1)}, f32[72,128]{1,0:T(8,128)S(1)}, u32[]{:S(2)}, u32[]{:S(2)}) collective-permute-start(f32[72,128]{1,0:T(8,128)S(1)} %get-tuple-element.33.refs_0_.refs_7_), channel_id=1, source_target_pairs={{0,2},{1,3},{2,0},{3,1},{4,6},{5,7},{6,4},{7,5},{8,10},{9,11},{10,... | collective-permute-start | bytes 110600 | tf_op jit(solution)/shard_map/ppermute | solution.py:852
  6.7 0.2 collective-permute-start
  6.9 1.2 %shard_map.65 = (f32[7,3,128,256]{3,2,1,0:T(8,128)S(1)}, f32[2,128,256]{2,1,0:T(8,128)S(1)}, f32[8,128]{1,0:T(8,128)S(1)}, f32[8,256]{1,0:T(8,128)S(1)}, f32[2,128,256]{2,1,0:T(8,128)S(1)}) custom-call(f32[16,128]{1,0:T(8,128)S(1)} %get-tuple-element.21.prepared, f32[32,8,128]{2,1,0:T(8,128)S(1)} %get-tuple-element.22.drift_z), custom_call_target="tpu_custom_call" | custom-call | flops 1000000 | bytes 1000000 | tf_op jit(solution)/shard_map/pallas_call | solution.py:875
  8.1 0.7 %shard_map.66 = (f32[4,4,40,128]{3,2,1,0:T(8,128)S(1)}, f32[8,40,128]{2,1,0:T(8,128)S(1)}, f32[8,40,128]{2,1,0:T(8,128)S(1)}, f32[8,40,128]{2,1,0:T(8,128)S(1)}) custom-call(f32[16,128]{1,0:T(8,128)S(1)} %get-tuple-element.21.prepared, f32[8,40,128]{2,1,0:T(8,128)S(1)} %get-tuple-element.27.line_values, f32[10,40,128]{2,1,0:T(8,128)S(1)} %get-tuple-element.28.line_drifts), custom_call_target="tpu_custom_call" | custom-call | flops 1000000 | bytes 1000000 | tf_op jit(solution)/shard_map/pallas_call | solution.py:875
  8.8 0.0 collective-permute-done.2.refs_3_.refs_10_
  8.8 1.4 %collective-permute-done.1.refs_2_.refs_9_ = f32[72,128]{1,0:T(8,128)S(1)} collective-permute-done((f32[72,128]{1,0:T(8,128)S(1)}, f32[72,128]{1,0:T(8,128)S(1)}, u32[]{:S(2)}, u32[]{:S(2)}) %collective-permute-start.1) | collective-permute-done | bytes 36896 | tf_op jit(solution)/shard_map/ppermute | solution.py:852
  10.2 0.4 %collective-permute-done.refs_1_.refs_8_ = f32[72,128]{1,0:T(8,128)S(1)} collective-permute-done((f32[72,128]{1,0:T(8,128)S(1)}, f32[72,128]{1,0:T(8,128)S(1)}, u32[]{:S(2)}, u32[]{:S(2)}) %collective-permute-start) | collective-permute-done | bytes 36896 | tf_op jit(solution)/shard_map/ppermute | solution.py:852
  10.6 0.1 shard_map.68.refs_12_
  10.7 2.7 %collective-permute-start.3 = (f32[40,128]{1,0:T(8,128)S(1)}, f32[40,128]{1,0:T(8,128)S(1)}, u32[]{:S(2)}, u32[]{:S(2)}) collective-permute-start(f32[40,128]{1,0:T(8,128)S(1)} %shard_map.68.refs_12_), channel_id=1, source_target_pairs={{0,4},{1,5},{2,6},{3,7},{4,0},{5,1},{6,2},{7,3},{8,12},{9,13},{10,... | collective-permute-start | bytes 61448 | tf_op jit(solution)/shard_map/ppermute | solution.py:852
  13.4 1.0 %shard_map.67.refs_11_ = f32[2,4,40,128]{3,2,1,0:T(8,128)S(1)} custom-call(f32[16,128]{1,0:T(8,128)S(1)} %get-tuple-element.21.prepared), custom_call_target="tpu_custom_call" | custom-call | flops 1000000 | bytes 1000000 | tf_op jit(solution)/shard_map/pallas_call | solution.py:875
  14.4 1.0 %collective-permute-done.3.refs_13_ = f32[40,128]{1,0:T(8,128)S(1)} collective-permute-done((f32[40,128]{1,0:T(8,128)S(1)}, f32[40,128]{1,0:T(8,128)S(1)}, u32[]{:S(2)}, u32[]{:S(2)}) %collective-permute-start.3) | collective-permute-done | bytes 20512 | tf_op jit(solution)/shard_map/ppermute | solution.py:852
  15.5 0.2 %shard_map.69 = (f32[8,256]{1,0:T(8,128)S(1)}, f32[128,256]{1,0:T(8,128)S(1)}) custom-call(f32[2,128,256]{2,1,0:T(8,128)S(1)} %get-tuple-element.24.refs_0_, f32[8,128]{1,0:T(8,128)S(1)} %get-tuple-element.25.refs_1_, f32[8,256]{1,0:T(8,128)S(1)} %get-tuple-element.26.refs_4_.refs_2_, f32[8,40,128]{2,1,0:T(8,128)S(1)} %get-tuple-element.29.refs_3_, ...), custom_call_target="tpu_custom_call" | custom-call | flops 1000000 | bytes 1000000 | tf_op jit(solution)/shard_map/pallas_call | solution.py:875
  15.7 0.1 collective-permute-start.6
  15.8 1.6 %collective-permute-start.5 = (f32[8,256]{1,0:T(8,128)S(1)}, f32[8,256]{1,0:T(8,128)S(1)}, u32[]{:S(2)}, u32[]{:S(2)}) collective-permute-start(f32[8,256]{1,0:T(8,128)S(1)} %get-tuple-element.36.refs_0_), channel_id=1, source_target_pairs={{0,16},{8,24},{16,0},{24,8},{1,17},{9,25},{17,1},{25,9},{2,18},{10... | collective-permute-start | bytes 24584 | tf_op jit(solution)/shard_map/ppermute | solution.py:852
  17.4 0.3 %collective-permute-start.4 = (f32[8,256]{1,0:T(8,128)S(1)}, f32[8,256]{1,0:T(8,128)S(1)}, u32[]{:S(2)}, u32[]{:S(2)}) collective-permute-start(f32[8,256]{1,0:T(8,128)S(1)} %get-tuple-element.36.refs_0_), channel_id=1, source_target_pairs={{0,8},{8,0},{16,24},{24,16},{1,9},{9,1},{17,25},{25,17},{2,10},{10... | collective-permute-start | bytes 24584 | tf_op jit(solution)/shard_map/ppermute | solution.py:852
  17.6 0.0 copy-done
  17.6 0.3 %shard_map.70.base = f32[8,32,128]{2,1,0:T(8,128)S(1)} custom-call(f32[7,3,128,256]{3,2,1,0:T(8,128)S(1)} %get-tuple-element.23.steps, f32[128,256]{1,0:T(8,128)S(1)} %get-tuple-element.34.sources, f32[32,8,128]{2,1,0:T(8,128)S(1)} %copy-done), custom_call_target="tpu_custom_call" | custom-call | flops 1000000 | bytes 1000000 | tf_op jit(solution)/shard_map/pallas_call | solution.py:875
  18.0 0.9 %collective-permute-done.6.refs_3_ = f32[8,256]{1,0:T(8,128)S(1)} collective-permute-done((f32[8,256]{1,0:T(8,128)S(1)}, f32[8,256]{1,0:T(8,128)S(1)}, u32[]{:S(2)}, u32[]{:S(2)}) %collective-permute-start.6) | collective-permute-done | bytes 8224 | tf_op jit(solution)/shard_map/ppermute | solution.py:852
  18.9 0.6 %collective-permute-done.5.refs_2_ = f32[8,256]{1,0:T(8,128)S(1)} collective-permute-done((f32[8,256]{1,0:T(8,128)S(1)}, f32[8,256]{1,0:T(8,128)S(1)}, u32[]{:S(2)}, u32[]{:S(2)}) %collective-permute-start.5) | collective-permute-done | bytes 8224 | tf_op jit(solution)/shard_map/ppermute | solution.py:852
  19.5 0.0 collective-permute-done.4.refs_1_
  19.5 0.9 %shard_map.71 = f32[32,8,128]{2,1,0:T(8,128)} custom-call(f32[8,32,128]{2,1,0:T(8,128)S(1)} %shard_map.70.base, f32[2,128,256]{2,1,0:T(8,128)S(1)} %get-tuple-element.35.ends, f32[8,256]{1,0:T(8,128)S(1)} %get-tuple-element.36.refs_0_, f32[8,256]{1,0:T(8,128)S(1)} %collective-permute-done.4.refs_1_, f32[8,256]{1,0:T(8,128)S(1)} %collective-permute-done.5.refs_2_, ...), custom_call_target="tpu_custom_call" | custom-call | flops 1000000 | bytes 1000000 | tf_op jit(solution)/shard_map/pallas_call | solution.py:875
Async XLA Ops:
  0.0 17.6 %copy-start = (f32[32,8,128]{2,1,0:T(8,128)S(1)}, f32[32,8,128]{2,1,0:T(8,128)}, u32[]{:S(2)}) copy-start(f32[32,8,128]{2,1,0:T(8,128)} %density.1) | copy-start | bytes 393220
  2.2 6.6 %collective-permute-start.2 = (f32[72,128]{1,0:T(8,128)S(1)}, f32[72,128]{1,0:T(8,128)S(1)}, u32[]{:S(2)}, u32[]{:S(2)}) collective-permute-start(f32[72,128]{1,0:T(8,128)S(1)} %get-tuple-element.33.refs_0_.refs_7_), channel_id=1, source_target_pairs={{0,3},{1,2},{2,1},{3,0},{4,7},{5,6},{6,5},{7,4},{8,11},{9,10},{10,... | collective-permute-start | bytes 110600 | tf_op jit(solution)/shard_map/ppermute | solution.py:852
  6.2 4.0 %collective-permute-start.1 = (f32[72,128]{1,0:T(8,128)S(1)}, f32[72,128]{1,0:T(8,128)S(1)}, u32[]{:S(2)}, u32[]{:S(2)}) collective-permute-start(f32[72,128]{1,0:T(8,128)S(1)} %get-tuple-element.33.refs_0_.refs_7_), channel_id=1, source_target_pairs={{0,2},{1,3},{2,0},{3,1},{4,6},{5,7},{6,4},{7,5},{8,10},{9,11},{10,... | collective-permute-start | bytes 110600 | tf_op jit(solution)/shard_map/ppermute | solution.py:852
  6.7 4.0 %collective-permute-start = (f32[72,128]{1,0:T(8,128)S(1)}, f32[72,128]{1,0:T(8,128)S(1)}, u32[]{:S(2)}, u32[]{:S(2)}) collective-permute-start(f32[72,128]{1,0:T(8,128)S(1)} %get-tuple-element.33.refs_0_.refs_7_), channel_id=1, source_target_pairs={{0,1},{1,0},{2,3},{3,2},{4,5},{5,4},{6,7},{7,6},{8,9},{9,8},{10,11... | collective-permute-start | bytes 110600 | tf_op jit(solution)/shard_map/ppermute | solution.py:852
  10.7 4.7 %collective-permute-start.3 = (f32[40,128]{1,0:T(8,128)S(1)}, f32[40,128]{1,0:T(8,128)S(1)}, u32[]{:S(2)}, u32[]{:S(2)}) collective-permute-start(f32[40,128]{1,0:T(8,128)S(1)} %shard_map.68.refs_12_), channel_id=1, source_target_pairs={{0,4},{1,5},{2,6},{3,7},{4,0},{5,1},{6,2},{7,3},{8,12},{9,13},{10,... | collective-permute-start | bytes 61448 | tf_op jit(solution)/shard_map/ppermute | solution.py:852
  15.7 3.2 %collective-permute-start.6 = (f32[8,256]{1,0:T(8,128)S(1)}, f32[8,256]{1,0:T(8,128)S(1)}, u32[]{:S(2)}, u32[]{:S(2)}) collective-permute-start(f32[8,256]{1,0:T(8,128)S(1)} %get-tuple-element.36.refs_0_), channel_id=1, source_target_pairs={{0,24},{8,16},{16,8},{24,0},{1,25},{9,17},{17,9},{25,1},{2,26},{10... | collective-permute-start | bytes 24584 | tf_op jit(solution)/shard_map/ppermute | solution.py:852
  15.8 3.7 %collective-permute-start.5 = (f32[8,256]{1,0:T(8,128)S(1)}, f32[8,256]{1,0:T(8,128)S(1)}, u32[]{:S(2)}, u32[]{:S(2)}) collective-permute-start(f32[8,256]{1,0:T(8,128)S(1)} %get-tuple-element.36.refs_0_), channel_id=1, source_target_pairs={{0,16},{8,24},{16,0},{24,8},{1,17},{9,25},{17,1},{25,9},{2,18},{10... | collective-permute-start | bytes 24584 | tf_op jit(solution)/shard_map/ppermute | solution.py:852
  17.4 2.1 %collective-permute-start.4 = (f32[8,256]{1,0:T(8,128)S(1)}, f32[8,256]{1,0:T(8,128)S(1)}, u32[]{:S(2)}, u32[]{:S(2)}) collective-permute-start(f32[8,256]{1,0:T(8,128)S(1)} %get-tuple-element.36.refs_0_), channel_id=1, source_target_pairs={{0,8},{8,0},{16,24},{24,16},{1,9},{9,1},{17,25},{25,17},{2,10},{10... | collective-permute-start | bytes 24584 | tf_op jit(solution)/shard_map/ppermute | solution.py:852

commit v11 on v9

--- a/solution.py
+++ b/solution.py
@@ -716,10 +716,11 @@
     first = 0 if local else lax.div(lax.axis_index("gy"), stride) - digit
     values = [split_message(m) for m in gather_members(received, digit, radix)]
     group = [tuple(coefs[first + j, q] for q in range(4)) for j in range(radix)]
-    merged, total = group[0], values[0]
-    for j in range(1, radix):
-        total = merge_values(merged, group[j], total, values[j])
-        merged = merge_coefs(merged, group[j])
+    while len(group) > 1:
+        pairs = range(0, len(group), 2)
+        values = [merge_values(group[j], group[j + 1], values[j], values[j + 1]) for j in pairs]
+        group = [merge_coefs(group[j], group[j + 1]) for j in pairs]
+    total = values[0]
     if facing:
         is_low = lax.axis_index("gy") < stride * radix
         message[...] = jnp.where(is_low, total[1], total[0])
@@ -952,7 +953,7 @@
             facing = number + 2 == len(y_levels) and y_levels[-1][1] == 2
             message = call(
                 functools.partial(merge_kernel, stride, radix, number == 0, facing),
-                [coefs[number]] + received + ([packed] if number == 0 else []),
+                [coefs[number]] + received + ([packed] + list(far) if number == 0 else []),
                 shape(width if facing else width + size_x, LANES),
             )
     message, sources = call(

time: 20.5 us -> 20.5 us (level)
  no operation moved by 1% of the time
where the time goes in v11:
time: 20.5 us; the launch traced here: 20.4 us
  starting transfers between devices  9.23 us (45%)
  Pallas kernels  6.66 us (32%)
  waiting for transfers between devices  4.41 us (22%)
    ppermute x7, starting transfers between devices, exchange(): lax.ppermute(message, axis, [(i, i ^ s * stride) for i in devices])  9.23 us
    pallas_call x8, Pallas kernels, call(): pl.pallas_call(kernel, out_shape=outputs, in_specs=in_specs or [vmem] * l...  6.66 us
    ppermute x7, waiting for transfers between devices, exchange(): lax.ppermute(message, axis, [(i, i ^ s * stride) for i in devices])  4.41 us
  transfers between devices with their start and end apart: 7, of which 5 were waited for; matrix products, arithmetic and copies ran while one was open for 0% of the time, Pallas kernels for 16%

profile of v11, /device:TPU:0, one launch (start us, length us, event | category | flops | bytes accessed | tf_op | source)
XLA Modules:
  0.0 20.4 jit_solution(8057811489223261095)
XLA Ops:
  0.0 0.0 copy-start
  0.0 2.2 %shard_map.64 = (f32[72,128]{1,0:T(8,128)S(1)}, f32[8,40,128]{2,1,0:T(8,128)S(1)}, f32[10,40,128]{2,1,0:T(8,128)S(1)}, f32[32,8,128]{2,1,0:T(8,128)S(1)}, f32[16,128]{1,0:T(8,128)S(1)}) custom-call(f32[32,8,128]{2,1,0:T(8,128)} %density.1, f32[1,3]{1,0:T(1,128)} %bitcast.8, f32[3,16]{1,0:T(4,128)} %bitcast.6, f32[1,16]{1,0:T(1,128)} %bitcast.9, ...), custom_call_target="tpu_custom_call" | custom-call | flops 1000000 | bytes 1000000 | tf_op jit(solution)/shard_map/pallas_call | solution.py:886
  2.2 4.0 %collective-permute-start.2 = (f32[72,128]{1,0:T(8,128)S(1)}, f32[72,128]{1,0:T(8,128)S(1)}, u32[]{:S(2)}, u32[]{:S(2)}) collective-permute-start(f32[72,128]{1,0:T(8,128)S(1)} %get-tuple-element.33.refs_0_.refs_7_), channel_id=1, source_target_pairs={{0,3},{1,2},{2,1},{3,0},{4,7},{5,6},{6,5},{7,4},{8,11},{9,10},{10,... | collective-permute-start | bytes 110600 | tf_op jit(solution)/shard_map/ppermute | solution.py:863
  6.2 0.4 %collective-permute-start.1 = (f32[72,128]{1,0:T(8,128)S(1)}, f32[72,128]{1,0:T(8,128)S(1)}, u32[]{:S(2)}, u32[]{:S(2)}) collective-permute-start(f32[72,128]{1,0:T(8,128)S(1)} %get-tuple-element.33.refs_0_.refs_7_), channel_id=1, source_target_pairs={{0,2},{1,3},{2,0},{3,1},{4,6},{5,7},{6,4},{7,5},{8,10},{9,11},{10,... | collective-permute-start | bytes 110600 | tf_op jit(solution)/shard_map/ppermute | solution.py:863
  6.7 0.2 collective-permute-start
  6.9 1.0 %shard_map.67.refs_5_.refs_11_ = f32[2,4,40,128]{3,2,1,0:T(8,128)S(1)} custom-call(f32[16,128]{1,0:T(8,128)S(1)} %get-tuple-element.21.prepared), custom_call_target="tpu_custom_call" | custom-call | flops 1000000 | bytes 1000000 | tf_op jit(solution)/shard_map/pallas_call | solution.py:886
  7.9 1.2 %shard_map.65 = (f32[7,3,128,256]{3,2,1,0:T(8,128)S(1)}, f32[2,128,256]{2,1,0:T(8,128)S(1)}, f32[8,128]{1,0:T(8,128)S(1)}, f32[8,256]{1,0:T(8,128)S(1)}, f32[2,128,256]{2,1,0:T(8,128)S(1)}) custom-call(f32[16,128]{1,0:T(8,128)S(1)} %get-tuple-element.21.prepared, f32[32,8,128]{2,1,0:T(8,128)S(1)} %get-tuple-element.22.drift_z), custom_call_target="tpu_custom_call" | custom-call | flops 1000000 | bytes 1000000 | tf_op jit(solution)/shard_map/pallas_call | solution.py:886
  9.1 0.7 %shard_map.66 = (f32[4,4,40,128]{3,2,1,0:T(8,128)S(1)}, f32[8,40,128]{2,1,0:T(8,128)S(1)}, f32[8,40,128]{2,1,0:T(8,128)S(1)}, f32[8,40,128]{2,1,0:T(8,128)S(1)}) custom-call(f32[16,128]{1,0:T(8,128)S(1)} %get-tuple-element.21.prepared, f32[8,40,128]{2,1,0:T(8,128)S(1)} %get-tuple-element.27.line_values, f32[10,40,128]{2,1,0:T(8,128)S(1)} %get-tuple-element.28.line_drifts), custom_call_target="tpu_custom_call" | custom-call | flops 1000000 | bytes 1000000 | tf_op jit(solution)/shard_map/pallas_call | solution.py:886
  9.8 0.0 collective-permute-done.2.refs_3_.refs_10_
  9.8 0.3 %collective-permute-done.1.refs_2_.refs_9_ = f32[72,128]{1,0:T(8,128)S(1)} collective-permute-done((f32[72,128]{1,0:T(8,128)S(1)}, f32[72,128]{1,0:T(8,128)S(1)}, u32[]{:S(2)}, u32[]{:S(2)}) %collective-permute-start.1) | collective-permute-done | bytes 36896 | tf_op jit(solution)/shard_map/ppermute | solution.py:863
  10.2 0.4 %collective-permute-done.refs_1_.refs_8_ = f32[72,128]{1,0:T(8,128)S(1)} collective-permute-done((f32[72,128]{1,0:T(8,128)S(1)}, f32[72,128]{1,0:T(8,128)S(1)}, u32[]{:S(2)}, u32[]{:S(2)}) %collective-permute-start) | collective-permute-done | bytes 36896 | tf_op jit(solution)/shard_map/ppermute | solution.py:863
  10.6 0.1 shard_map.68.refs_12_
  10.7 2.7 %collective-permute-start.3 = (f32[40,128]{1,0:T(8,128)S(1)}, f32[40,128]{1,0:T(8,128)S(1)}, u32[]{:S(2)}, u32[]{:S(2)}) collective-permute-start(f32[40,128]{1,0:T(8,128)S(1)} %shard_map.68.refs_12_), channel_id=1, source_target_pairs={{0,4},{1,5},{2,6},{3,7},{4,0},{5,1},{6,2},{7,3},{8,12},{9,13},{10,... | collective-permute-start | bytes 61448 | tf_op jit(solution)/shard_map/ppermute | solution.py:863
  13.3 2.1 %collective-permute-done.3.refs_13_ = f32[40,128]{1,0:T(8,128)S(1)} collective-permute-done((f32[40,128]{1,0:T(8,128)S(1)}, f32[40,128]{1,0:T(8,128)S(1)}, u32[]{:S(2)}, u32[]{:S(2)}) %collective-permute-start.3) | collective-permute-done | bytes 20512 | tf_op jit(solution)/shard_map/ppermute | solution.py:863
  15.4 0.3 %shard_map.69 = (f32[8,256]{1,0:T(8,128)S(1)}, f32[128,256]{1,0:T(8,128)S(1)}) custom-call(f32[2,128,256]{2,1,0:T(8,128)S(1)} %get-tuple-element.24.refs_0_, f32[8,128]{1,0:T(8,128)S(1)} %get-tuple-element.25.refs_1_, f32[8,256]{1,0:T(8,128)S(1)} %get-tuple-element.26.refs_4_.refs_2_, f32[8,40,128]{2,1,0:T(8,128)S(1)} %get-tuple-element.29.refs_3_, ...), custom_call_target="tpu_custom_call" | custom-call | flops 1000000 | bytes 1000000 | tf_op jit(solution)/shard_map/pallas_call | solution.py:886
  15.7 0.1 collective-permute-start.6
  15.8 1.6 %collective-permute-start.5 = (f32[8,256]{1,0:T(8,128)S(1)}, f32[8,256]{1,0:T(8,128)S(1)}, u32[]{:S(2)}, u32[]{:S(2)}) collective-permute-start(f32[8,256]{1,0:T(8,128)S(1)} %get-tuple-element.36.refs_0_), channel_id=1, source_target_pairs={{0,16},{8,24},{16,0},{24,8},{1,17},{9,25},{17,1},{25,9},{2,18},{10... | collective-permute-start | bytes 24584 | tf_op jit(solution)/shard_map/ppermute | solution.py:863
  17.4 0.3 %collective-permute-start.4 = (f32[8,256]{1,0:T(8,128)S(1)}, f32[8,256]{1,0:T(8,128)S(1)}, u32[]{:S(2)}, u32[]{:S(2)}) collective-permute-start(f32[8,256]{1,0:T(8,128)S(1)} %get-tuple-element.36.refs_0_), channel_id=1, source_target_pairs={{0,8},{8,0},{16,24},{24,16},{1,9},{9,1},{17,25},{25,17},{2,10},{10... | collective-permute-start | bytes 24584 | tf_op jit(solution)/shard_map/ppermute | solution.py:863
  17.6 0.0 copy-done
  17.6 0.3 %shard_map.70.base = f32[8,32,128]{2,1,0:T(8,128)S(1)} custom-call(f32[7,3,128,256]{3,2,1,0:T(8,128)S(1)} %get-tuple-element.23.steps, f32[128,256]{1,0:T(8,128)S(1)} %get-tuple-element.34.sources, f32[32,8,128]{2,1,0:T(8,128)S(1)} %copy-done), custom_call_target="tpu_custom_call" | custom-call | flops 1000000 | bytes 1000000 | tf_op jit(solution)/shard_map/pallas_call | solution.py:886
  17.9 0.9 %collective-permute-done.6.refs_3_ = f32[8,256]{1,0:T(8,128)S(1)} collective-permute-done((f32[8,256]{1,0:T(8,128)S(1)}, f32[8,256]{1,0:T(8,128)S(1)}, u32[]{:S(2)}, u32[]{:S(2)}) %collective-permute-start.6) | collective-permute-done | bytes 8224 | tf_op jit(solution)/shard_map/ppermute | solution.py:863
  18.8 0.6 %collective-permute-done.5.refs_2_ = f32[8,256]{1,0:T(8,128)S(1)} collective-permute-done((f32[8,256]{1,0:T(8,128)S(1)}, f32[8,256]{1,0:T(8,128)S(1)}, u32[]{:S(2)}, u32[]{:S(2)}) %collective-permute-start.5) | collective-permute-done | bytes 8224 | tf_op jit(solution)/shard_map/ppermute | solution.py:863
  19.5 0.0 collective-permute-done.4.refs_1_
  19.5 0.9 %shard_map.71 = f32[32,8,128]{2,1,0:T(8,128)} custom-call(f32[8,32,128]{2,1,0:T(8,128)S(1)} %shard_map.70.base, f32[2,128,256]{2,1,0:T(8,128)S(1)} %get-tuple-element.35.ends, f32[8,256]{1,0:T(8,128)S(1)} %get-tuple-element.36.refs_0_, f32[8,256]{1,0:T(8,128)S(1)} %collective-permute-done.4.refs_1_, f32[8,256]{1,0:T(8,128)S(1)} %collective-permute-done.5.refs_2_, ...), custom_call_target="tpu_custom_call" | custom-call | flops 1000000 | bytes 1000000 | tf_op jit(solution)/shard_map/pallas_call | solution.py:886
Async XLA Ops:
  0.0 17.6 %copy-start = (f32[32,8,128]{2,1,0:T(8,128)S(1)}, f32[32,8,128]{2,1,0:T(8,128)}, u32[]{:S(2)}) copy-start(f32[32,8,128]{2,1,0:T(8,128)} %density.1) | copy-start | bytes 393220
  2.2 7.6 %collective-permute-start.2 = (f32[72,128]{1,0:T(8,128)S(1)}, f32[72,128]{1,0:T(8,128)S(1)}, u32[]{:S(2)}, u32[]{:S(2)}) collective-permute-start(f32[72,128]{1,0:T(8,128)S(1)} %get-tuple-element.33.refs_0_.refs_7_), channel_id=1, source_target_pairs={{0,3},{1,2},{2,1},{3,0},{4,7},{5,6},{6,5},{7,4},{8,11},{9,10},{10,... | collective-permute-start | bytes 110600 | tf_op jit(solution)/shard_map/ppermute | solution.py:863
  6.2 4.0 %collective-permute-start.1 = (f32[72,128]{1,0:T(8,128)S(1)}, f32[72,128]{1,0:T(8,128)S(1)}, u32[]{:S(2)}, u32[]{:S(2)}) collective-permute-start(f32[72,128]{1,0:T(8,128)S(1)} %get-tuple-element.33.refs_0_.refs_7_), channel_id=1, source_target_pairs={{0,2},{1,3},{2,0},{3,1},{4,6},{5,7},{6,4},{7,5},{8,10},{9,11},{10,... | collective-permute-start | bytes 110600 | tf_op jit(solution)/shard_map/ppermute | solution.py:863
  6.7 4.0 %collective-permute-start = (f32[72,128]{1,0:T(8,128)S(1)}, f32[72,128]{1,0:T(8,128)S(1)}, u32[]{:S(2)}, u32[]{:S(2)}) collective-permute-start(f32[72,128]{1,0:T(8,128)S(1)} %get-tuple-element.33.refs_0_.refs_7_), channel_id=1, source_target_pairs={{0,1},{1,0},{2,3},{3,2},{4,5},{5,4},{6,7},{7,6},{8,9},{9,8},{10,11... | collective-permute-start | bytes 110600 | tf_op jit(solution)/shard_map/ppermute | solution.py:863
  10.7 4.7 %collective-permute-start.3 = (f32[40,128]{1,0:T(8,128)S(1)}, f32[40,128]{1,0:T(8,128)S(1)}, u32[]{:S(2)}, u32[]{:S(2)}) collective-permute-start(f32[40,128]{1,0:T(8,128)S(1)} %shard_map.68.refs_12_), channel_id=1, source_target_pairs={{0,4},{1,5},{2,6},{3,7},{4,0},{5,1},{6,2},{7,3},{8,12},{9,13},{10,... | collective-permute-start | bytes 61448 | tf_op jit(solution)/shard_map/ppermute | solution.py:863
  15.7 3.2 %collective-permute-start.6 = (f32[8,256]{1,0:T(8,128)S(1)}, f32[8,256]{1,0:T(8,128)S(1)}, u32[]{:S(2)}, u32[]{:S(2)}) collective-permute-start(f32[8,256]{1,0:T(8,128)S(1)} %get-tuple-element.36.refs_0_), channel_id=1, source_target_pairs={{0,24},{8,16},{16,8},{24,0},{1,25},{9,17},{17,9},{25,1},{2,26},{10... | collective-permute-start | bytes 24584 | tf_op jit(solution)/shard_map/ppermute | solution.py:863
  15.8 3.7 %collective-permute-start.5 = (f32[8,256]{1,0:T(8,128)S(1)}, f32[8,256]{1,0:T(8,128)S(1)}, u32[]{:S(2)}, u32[]{:S(2)}) collective-permute-start(f32[8,256]{1,0:T(8,128)S(1)} %get-tuple-element.36.refs_0_), channel_id=1, source_target_pairs={{0,16},{8,24},{16,0},{24,8},{1,17},{9,25},{17,1},{25,9},{2,18},{10... | collective-permute-start | bytes 24584 | tf_op jit(solution)/shard_map/ppermute | solution.py:863
  17.4 2.1 %collective-permute-start.4 = (f32[8,256]{1,0:T(8,128)S(1)}, f32[8,256]{1,0:T(8,128)S(1)}, u32[]{:S(2)}, u32[]{:S(2)}) collective-permute-start(f32[8,256]{1,0:T(8,128)S(1)} %get-tuple-element.36.refs_0_), channel_id=1, source_target_pairs={{0,8},{8,0},{16,24},{24,16},{1,9},{9,1},{17,25},{25,17},{2,10},{10... | collective-permute-start | bytes 24584 | tf_op jit(solution)/shard_map/ppermute | solution.py:863

commit v12 on v11

--- a/solution.py
+++ b/solution.py
@@ -686,8 +686,11 @@
     )
 
 
-def gather_members(refs, own, count):
-    held = [ref[...] for ref in refs]
+ORDER = {("gy", 2): (1,), ("gz", 2): (1,), ("gy", 4): (1, 3, 2), ("gz", 4): (1, 2, 3)}
+
+
+def gather_members(refs, own, count, axis):
+    held = {s: ref[...] for s, ref in zip((0,) + ORDER[axis, count], refs)}
     return [
         functools.reduce(
             lambda acc, s: jnp.where((own ^ s) == j, held[s], acc), range(1, count), held[0]
@@ -714,7 +717,7 @@
     received, message = refs[:radix], refs[-1]
     digit = lax.rem(lax.div(lax.axis_index("gy"), stride), radix)
     first = 0 if local else lax.div(lax.axis_index("gy"), stride) - digit
-    values = [split_message(m) for m in gather_members(received, digit, radix)]
+    values = [split_message(m) for m in gather_members(received, digit, radix, "gy")]
     group = [tuple(coefs[first + j, q] for q in range(4)) for j in range(radix)]
     while len(group) > 1:
         pairs = range(0, len(group), 2)
@@ -744,7 +747,7 @@
         (stride, radix), (coefs, received) = levels[number], inputs[number]
         digit = lax.rem(lax.div(lax.axis_index("gy"), stride), radix)
         first = 0 if number == 0 else lax.div(lax.axis_index("gy"), stride) - digit
-        members = gather_members(received, digit, radix)
+        members = gather_members(received, digit, radix, "gy")
         group = [tuple(coefs[first + j, q] for q in range(4)) for j in range(radix)]
         if members[0].shape[0] == width:
             c_last, a_first = group[0][3], group[1][0]
@@ -817,7 +820,7 @@
 def merge_z_kernel(stride, radix, *refs):
     received, message = refs[:radix], refs[radix]
     digit = lax.rem(lax.div(lax.axis_index("gz"), stride), radix)
-    members = [unpack_ends(m) for m in gather_members(received, digit, radix)]
+    members = [unpack_ends(m) for m in gather_members(received, digit, radix, "gz")]
     total = functools.reduce(merge_z, members)
     message[...] = jnp.concatenate(total + total[:2], axis=0)
 
@@ -832,7 +835,7 @@
     below = above = jnp.zeros((1, ends.shape[2]), jnp.float32)
     for (stride, radix), received in zip(reversed(levels), reversed(inputs)):
         digit = lax.rem(lax.div(lax.axis_index("gz"), stride), radix)
-        members = [unpack_ends(m) for m in gather_members(received, digit, radix)]
+        members = [unpack_ends(m) for m in gather_members(received, digit, radix, "gz")]
         lows, highs = chain(
             [(m[2], m[4], m[3], m[5]) for m in members],
             [(m[0], m[1]) for m in members],
@@ -861,7 +864,7 @@
     devices = range(lax.axis_size(axis))
     return [message] + [
         lax.ppermute(message, axis, [(i, i ^ (s * stride)) for i in devices])
-        for s in range(1, radix)
+        for s in ORDER[axis, radix]
     ]
 
 

time: 20.5 us -> 20.5 us (level)
  no operation moved by 1% of the time
where the time goes in v12:
time: 20.5 us; the launch traced here: 20.4 us
  starting transfers between devices  9.21 us (45%)
  Pallas kernels  6.66 us (32%)
  waiting for transfers between devices  4.44 us (22%)
    ppermute x7, starting transfers between devices, exchange(): lax.ppermute(message, axis, [(i, i ^ s * stride) for i in devices])  9.21 us
    pallas_call x8, Pallas kernels, call(): pl.pallas_call(kernel, out_shape=outputs, in_specs=in_specs or [vmem] * l...  6.66 us
    ppermute x7, waiting for transfers between devices, exchange(): lax.ppermute(message, axis, [(i, i ^ s * stride) for i in devices])  4.44 us
  transfers between devices with their start and end apart: 7, of which 5 were waited for; matrix products, arithmetic and copies ran while one was open for 0% of the time, Pallas kernels for 16%

profile of v12, /device:TPU:0, one launch (start us, length us, event | category | flops | bytes accessed | tf_op | source)
XLA Modules:
  0.0 20.4 jit_solution(2280448714941673629)
XLA Ops:
  0.0 0.0 copy-start
  0.0 2.2 %shard_map.64 = (f32[72,128]{1,0:T(8,128)S(1)}, f32[8,40,128]{2,1,0:T(8,128)S(1)}, f32[10,40,128]{2,1,0:T(8,128)S(1)}, f32[32,8,128]{2,1,0:T(8,128)S(1)}, f32[16,128]{1,0:T(8,128)S(1)}) custom-call(f32[32,8,128]{2,1,0:T(8,128)} %density.1, f32[1,3]{1,0:T(1,128)} %bitcast.8, f32[3,16]{1,0:T(4,128)} %bitcast.6, f32[1,16]{1,0:T(1,128)} %bitcast.9, ...), custom_call_target="tpu_custom_call" | custom-call | flops 1000000 | bytes 1000000 | tf_op jit(solution)/shard_map/pallas_call | solution.py:889
  2.2 3.1 %collective-permute-start.2 = (f32[72,128]{1,0:T(8,128)S(1)}, f32[72,128]{1,0:T(8,128)S(1)}, u32[]{:S(2)}, u32[]{:S(2)}) collective-permute-start(f32[72,128]{1,0:T(8,128)S(1)} %get-tuple-element.33.refs_0_.refs_7_), channel_id=1, source_target_pairs={{0,2},{1,3},{2,0},{3,1},{4,6},{5,7},{6,4},{7,5},{8,10},{9,11},{10,... | collective-permute-start | bytes 110600 | tf_op jit(solution)/shard_map/ppermute | solution.py:866
  5.3 1.4 %collective-permute-start.1 = (f32[72,128]{1,0:T(8,128)S(1)}, f32[72,128]{1,0:T(8,128)S(1)}, u32[]{:S(2)}, u32[]{:S(2)}) collective-permute-start(f32[72,128]{1,0:T(8,128)S(1)} %get-tuple-element.33.refs_0_.refs_7_), channel_id=1, source_target_pairs={{0,3},{1,2},{2,1},{3,0},{4,7},{5,6},{6,5},{7,4},{8,11},{9,10},{10,... | collective-permute-start | bytes 110600 | tf_op jit(solution)/shard_map/ppermute | solution.py:866
  6.7 0.2 collective-permute-start
  6.8 1.0 %shard_map.67.refs_5_.refs_11_ = f32[2,4,40,128]{3,2,1,0:T(8,128)S(1)} custom-call(f32[16,128]{1,0:T(8,128)S(1)} %get-tuple-element.21.prepared), custom_call_target="tpu_custom_call" | custom-call | flops 1000000 | bytes 1000000 | tf_op jit(solution)/shard_map/pallas_call | solution.py:889
  7.9 1.2 %shard_map.65 = (f32[7,3,128,256]{3,2,1,0:T(8,128)S(1)}, f32[2,128,256]{2,1,0:T(8,128)S(1)}, f32[8,128]{1,0:T(8,128)S(1)}, f32[8,256]{1,0:T(8,128)S(1)}, f32[2,128,256]{2,1,0:T(8,128)S(1)}) custom-call(f32[16,128]{1,0:T(8,128)S(1)} %get-tuple-element.21.prepared, f32[32,8,128]{2,1,0:T(8,128)S(1)} %get-tuple-element.22.drift_z), custom_call_target="tpu_custom_call" | custom-call | flops 1000000 | bytes 1000000 | tf_op jit(solution)/shard_map/pallas_call | solution.py:889
  9.1 0.7 %shard_map.66 = (f32[4,4,40,128]{3,2,1,0:T(8,128)S(1)}, f32[8,40,128]{2,1,0:T(8,128)S(1)}, f32[8,40,128]{2,1,0:T(8,128)S(1)}, f32[8,40,128]{2,1,0:T(8,128)S(1)}) custom-call(f32[16,128]{1,0:T(8,128)S(1)} %get-tuple-element.21.prepared, f32[8,40,128]{2,1,0:T(8,128)S(1)} %get-tuple-element.27.line_values, f32[10,40,128]{2,1,0:T(8,128)S(1)} %get-tuple-element.28.line_drifts), custom_call_target="tpu_custom_call" | custom-call | flops 1000000 | bytes 1000000 | tf_op jit(solution)/shard_map/pallas_call | solution.py:889
  9.8 0.0 collective-permute-done.2.refs_3_.refs_10_
  9.8 0.3 %collective-permute-done.1.refs_2_.refs_9_ = f32[72,128]{1,0:T(8,128)S(1)} collective-permute-done((f32[72,128]{1,0:T(8,128)S(1)}, f32[72,128]{1,0:T(8,128)S(1)}, u32[]{:S(2)}, u32[]{:S(2)}) %collective-permute-start.1) | collective-permute-done | bytes 36896 | tf_op jit(solution)/shard_map/ppermute | solution.py:866
  10.1 0.5 %collective-permute-done.refs_1_.refs_8_ = f32[72,128]{1,0:T(8,128)S(1)} collective-permute-done((f32[72,128]{1,0:T(8,128)S(1)}, f32[72,128]{1,0:T(8,128)S(1)}, u32[]{:S(2)}, u32[]{:S(2)}) %collective-permute-start) | collective-permute-done | bytes 36896 | tf_op jit(solution)/shard_map/ppermute | solution.py:866
  10.6 0.1 shard_map.68.refs_12_
  10.7 2.7 %collective-permute-start.3 = (f32[40,128]{1,0:T(8,128)S(1)}, f32[40,128]{1,0:T(8,128)S(1)}, u32[]{:S(2)}, u32[]{:S(2)}) collective-permute-start(f32[40,128]{1,0:T(8,128)S(1)} %shard_map.68.refs_12_), channel_id=1, source_target_pairs={{0,4},{1,5},{2,6},{3,7},{4,0},{5,1},{6,2},{7,3},{8,12},{9,13},{10,... | collective-permute-start | bytes 61448 | tf_op jit(solution)/shard_map/ppermute | solution.py:866
  13.3 2.1 %collective-permute-done.3.refs_13_ = f32[40,128]{1,0:T(8,128)S(1)} collective-permute-done((f32[40,128]{1,0:T(8,128)S(1)}, f32[40,128]{1,0:T(8,128)S(1)}, u32[]{:S(2)}, u32[]{:S(2)}) %collective-permute-start.3) | collective-permute-done | bytes 20512 | tf_op jit(solution)/shard_map/ppermute | solution.py:866
  15.4 0.3 %shard_map.69 = (f32[8,256]{1,0:T(8,128)S(1)}, f32[128,256]{1,0:T(8,128)S(1)}) custom-call(f32[2,128,256]{2,1,0:T(8,128)S(1)} %get-tuple-element.24.refs_0_, f32[8,128]{1,0:T(8,128)S(1)} %get-tuple-element.25.refs_1_, f32[8,256]{1,0:T(8,128)S(1)} %get-tuple-element.26.refs_4_.refs_2_, f32[8,40,128]{2,1,0:T(8,128)S(1)} %get-tuple-element.29.refs_3_, ...), custom_call_target="tpu_custom_call" | custom-call | flops 1000000 | bytes 1000000 | tf_op jit(solution)/shard_map/pallas_call | solution.py:889
  15.7 0.1 collective-permute-start.6
  15.8 1.6 %collective-permute-start.5 = (f32[8,256]{1,0:T(8,128)S(1)}, f32[8,256]{1,0:T(8,128)S(1)}, u32[]{:S(2)}, u32[]{:S(2)}) collective-permute-start(f32[8,256]{1,0:T(8,128)S(1)} %get-tuple-element.36.refs_0_), channel_id=1, source_target_pairs={{0,16},{8,24},{16,0},{24,8},{1,17},{9,25},{17,1},{25,9},{2,18},{10... | collective-permute-start | bytes 24584 | tf_op jit(solution)/shard_map/ppermute | solution.py:866
  17.4 0.3 %collective-permute-start.4 = (f32[8,256]{1,0:T(8,128)S(1)}, f32[8,256]{1,0:T(8,128)S(1)}, u32[]{:S(2)}, u32[]{:S(2)}) collective-permute-start(f32[8,256]{1,0:T(8,128)S(1)} %get-tuple-element.36.refs_0_), channel_id=1, source_target_pairs={{0,8},{8,0},{16,24},{24,16},{1,9},{9,1},{17,25},{25,17},{2,10},{10... | collective-permute-start | bytes 24584 | tf_op jit(solution)/shard_map/ppermute | solution.py:866
  17.6 0.0 copy-done
  17.6 0.3 %shard_map.70.base = f32[8,32,128]{2,1,0:T(8,128)S(1)} custom-call(f32[7,3,128,256]{3,2,1,0:T(8,128)S(1)} %get-tuple-element.23.steps, f32[128,256]{1,0:T(8,128)S(1)} %get-tuple-element.34.sources, f32[32,8,128]{2,1,0:T(8,128)S(1)} %copy-done), custom_call_target="tpu_custom_call" | custom-call | flops 1000000 | bytes 1000000 | tf_op jit(solution)/shard_map/pallas_call | solution.py:889
  17.9 0.9 %collective-permute-done.6.refs_3_ = f32[8,256]{1,0:T(8,128)S(1)} collective-permute-done((f32[8,256]{1,0:T(8,128)S(1)}, f32[8,256]{1,0:T(8,128)S(1)}, u32[]{:S(2)}, u32[]{:S(2)}) %collective-permute-start.6) | collective-permute-done | bytes 8224 | tf_op jit(solution)/shard_map/ppermute | solution.py:866
  18.8 0.6 %collective-permute-done.5.refs_2_ = f32[8,256]{1,0:T(8,128)S(1)} collective-permute-done((f32[8,256]{1,0:T(8,128)S(1)}, f32[8,256]{1,0:T(8,128)S(1)}, u32[]{:S(2)}, u32[]{:S(2)}) %collective-permute-start.5) | collective-permute-done | bytes 8224 | tf_op jit(solution)/shard_map/ppermute | solution.py:866
  19.5 0.0 collective-permute-done.4.refs_1_
  19.5 0.9 %shard_map.71 = f32[32,8,128]{2,1,0:T(8,128)} custom-call(f32[8,32,128]{2,1,0:T(8,128)S(1)} %shard_map.70.base, f32[2,128,256]{2,1,0:T(8,128)S(1)} %get-tuple-element.35.ends, f32[8,256]{1,0:T(8,128)S(1)} %get-tuple-element.36.refs_0_, f32[8,256]{1,0:T(8,128)S(1)} %collective-permute-done.4.refs_1_, f32[8,256]{1,0:T(8,128)S(1)} %collective-permute-done.5.refs_2_, ...), custom_call_target="tpu_custom_call" | custom-call | flops 1000000 | bytes 1000000 | tf_op jit(solution)/shard_map/pallas_call | solution.py:889
Async XLA Ops:
  0.0 17.6 %copy-start = (f32[32,8,128]{2,1,0:T(8,128)S(1)}, f32[32,8,128]{2,1,0:T(8,128)}, u32[]{:S(2)}) copy-start(f32[32,8,128]{2,1,0:T(8,128)} %density.1) | copy-start | bytes 393220
  2.2 7.6 %collective-permute-start.2 = (f32[72,128]{1,0:T(8,128)S(1)}, f32[72,128]{1,0:T(8,128)S(1)}, u32[]{:S(2)}, u32[]{:S(2)}) collective-permute-start(f32[72,128]{1,0:T(8,128)S(1)} %get-tuple-element.33.refs_0_.refs_7_), channel_id=1, source_target_pairs={{0,2},{1,3},{2,0},{3,1},{4,6},{5,7},{6,4},{7,5},{8,10},{9,11},{10,... | collective-permute-start | bytes 110600 | tf_op jit(solution)/shard_map/ppermute | solution.py:866
  5.3 4.9 %collective-permute-start.1 = (f32[72,128]{1,0:T(8,128)S(1)}, f32[72,128]{1,0:T(8,128)S(1)}, u32[]{:S(2)}, u32[]{:S(2)}) collective-permute-start(f32[72,128]{1,0:T(8,128)S(1)} %get-tuple-element.33.refs_0_.refs_7_), channel_id=1, source_target_pairs={{0,3},{1,2},{2,1},{3,0},{4,7},{5,6},{6,5},{7,4},{8,11},{9,10},{10,... | collective-permute-start | bytes 110600 | tf_op jit(solution)/shard_map/ppermute | solution.py:866
  6.7 4.0 %collective-permute-start = (f32[72,128]{1,0:T(8,128)S(1)}, f32[72,128]{1,0:T(8,128)S(1)}, u32[]{:S(2)}, u32[]{:S(2)}) collective-permute-start(f32[72,128]{1,0:T(8,128)S(1)} %get-tuple-element.33.refs_0_.refs_7_), channel_id=1, source_target_pairs={{0,1},{1,0},{2,3},{3,2},{4,5},{5,4},{6,7},{7,6},{8,9},{9,8},{10,11... | collective-permute-start | bytes 110600 | tf_op jit(solution)/shard_map/ppermute | solution.py:866
  10.7 4.7 %collective-permute-start.3 = (f32[40,128]{1,0:T(8,128)S(1)}, f32[40,128]{1,0:T(8,128)S(1)}, u32[]{:S(2)}, u32[]{:S(2)}) collective-permute-start(f32[40,128]{1,0:T(8,128)S(1)} %shard_map.68.refs_12_), channel_id=1, source_target_pairs={{0,4},{1,5},{2,6},{3,7},{4,0},{5,1},{6,2},{7,3},{8,12},{9,13},{10,... | collective-permute-start | bytes 61448 | tf_op jit(solution)/shard_map/ppermute | solution.py:866
  15.7 3.2 %collective-permute-start.6 = (f32[8,256]{1,0:T(8,128)S(1)}, f32[8,256]{1,0:T(8,128)S(1)}, u32[]{:S(2)}, u32[]{:S(2)}) collective-permute-start(f32[8,256]{1,0:T(8,128)S(1)} %get-tuple-element.36.refs_0_), channel_id=1, source_target_pairs={{0,24},{8,16},{16,8},{24,0},{1,25},{9,17},{17,9},{25,1},{2,26},{10... | collective-permute-start | bytes 24584 | tf_op jit(solution)/shard_map/ppermute | solution.py:866
  15.8 3.7 %collective-permute-start.5 = (f32[8,256]{1,0:T(8,128)S(1)}, f32[8,256]{1,0:T(8,128)S(1)}, u32[]{:S(2)}, u32[]{:S(2)}) collective-permute-start(f32[8,256]{1,0:T(8,128)S(1)} %get-tuple-element.36.refs_0_), channel_id=1, source_target_pairs={{0,16},{8,24},{16,0},{24,8},{1,17},{9,25},{17,1},{25,9},{2,18},{10... | collective-permute-start | bytes 24584 | tf_op jit(solution)/shard_map/ppermute | solution.py:866
  17.4 2.1 %collective-permute-start.4 = (f32[8,256]{1,0:T(8,128)S(1)}, f32[8,256]{1,0:T(8,128)S(1)}, u32[]{:S(2)}, u32[]{:S(2)}) collective-permute-start(f32[8,256]{1,0:T(8,128)S(1)} %get-tuple-element.36.refs_0_), channel_id=1, source_target_pairs={{0,8},{8,0},{16,24},{24,16},{1,9},{9,1},{17,25},{25,17},{2,10},{10... | collective-permute-start | bytes 24584 | tf_op jit(solution)/shard_map/ppermute | solution.py:866
